TPU v7x, 768 devices: a whole 4x8x12 slice. The times are simulated.
768 devices in a mesh: row: 12 (over z), col: 64 (over y, x, core).
Axes of the slice: x: 4, y: 8, z: 12, core: 2. Of those that a mesh axis runs over, the one named last changes fastest.
Arguments:
- obs_innovation: float32 [12, 64, 64, 32], P('row', 'col'), may hold values from -6 to 6
- obs_precision: float32 [12, 64, 64, 32], P('row', 'col'), may hold values from 0.5 to 4
- obs_offsets: float32 [12, 64, 64, 2, 32], P('row', 'col'), may hold values from 0 to 1
- obs_cell: int32 [12, 64, 64, 32], P('row', 'col'), may hold values from 0 to 130814, as said below
- obs_counts: int32 [12, 64, 64], P('row', 'col'), may hold values from 4 to 32, as said below
- land_sea: int32 [192, 16384], P('row', 'col'), may hold values 0 or 1
- diffusivity: float32 [192, 16384], P('row', 'col'), may hold values from 0.05 to 0.245
- background_std: bfloat16 [32, 192, 16384], P(None, 'row', 'col'), may hold values from 0.5 to 2
Outputs:
- increment: float32 [32, 192, 16384], P(None, 'row', 'col')
Inputs may be any that keep to these rules, and one draw needn't show every extreme that they name: Live slots are the first obs_counts[r, s, d] of the 32 slots; in every tile row some destination tile column receives 32 records from every source tile column. `obs_cell`: encodes c * 16 * 256 + i * 256 + j with channel c < 32, i < 15, j < 255, so all four interpolation cells lie in the destination tile.
All inputs are finite; a program needn't handle non-finite values. No bound on the sum of `land_sea` on one device may be relied on, other than what follows from the above.
Results may differ from a plain program's by a relative error of at most 0.0012.
Values sent between devices are 32-bit elements; how exact they have to be, the bound alone decides.
No kernel may reach another device: no remote copies, remote signals or barrier semaphores. Data moves between devices by JAX's collectives and lax.ppermute only.
A program may use at most 32 MiB of HBM per device.

v0:
```python
import jax
import jax.numpy as jnp
from jax import lax
from jax.sharding import PartitionSpec as P

SWEEPS = 6


def padded_2(shard, sides, width):
    for axis, dim in sides:
        count, length = (lax.axis_size(axis), shard.shape[dim])
        up = [(i, (i + 1) % count) for i in range(count)]
        down = [(j, i) for i, j in up]
        last = lax.slice_in_dim(shard, length - width, length, axis=dim)
        initial = lax.slice_in_dim(shard, 0, width, axis=dim)
        before = lax.ppermute(last, axis, up)
        after = lax.ppermute(initial, axis, down)
        shard = jnp.concatenate([before, shard, after], axis=dim)
    return shard


def corner_terms(weighted, east_frac, north_frac):
    return jnp.stack(
        [
            (1.0 - east_frac) * (1.0 - north_frac) * weighted,
            east_frac * (1.0 - north_frac) * weighted,
            (1.0 - east_frac) * north_frac * weighted,
            east_frac * north_frac * weighted,
        ],
        axis=1,
    )


def sweep(field, diffusion):
    centre = diffusion[1:-1, 1:-1]
    east_face = jnp.sqrt(centre * diffusion[1:-1, 2:])
    west_face = jnp.sqrt(centre * diffusion[1:-1, :-2])
    north_face = jnp.sqrt(centre * diffusion[2:, 1:-1])
    south_face = jnp.sqrt(centre * diffusion[:-2, 1:-1])
    inner = field[:, 1:-1, 1:-1]
    updated = inner + (
        east_face * (field[:, 1:-1, 2:] - inner)
        + west_face * (field[:, 1:-1, :-2] - inner)
        + (north_face * (field[:, 2:, 1:-1] - inner) + south_face * (field[:, :-2, 1:-1] - inner))
    )
    return (updated, centre)


def per_device(
    obs_innovation,
    obs_precision,
    obs_offsets,
    obs_cell,
    obs_counts,
    land_sea,
    diffusivity,
    background_std,
):
    sources = obs_innovation.shape[2]
    slot_count = obs_innovation.shape[3]
    innovation = obs_innovation.reshape(sources, slot_count)
    precision = obs_precision.reshape(sources, slot_count)
    offsets_here = obs_offsets.reshape(sources, 2, slot_count)
    cell_ids = obs_cell.reshape(sources, slot_count)
    counts = obs_counts.reshape(sources, 1)
    live_slot = lax.broadcasted_iota(jnp.int32, (sources, slot_count), 1) < counts
    weighted = jnp.where(live_slot, innovation * precision, jnp.float32(0.0))
    corners = corner_terms(weighted, offsets_here[:, 0], offsets_here[:, 1])
    arrived, arrived_cells = (
        lax.all_to_all(corners, "col", split_axis=0, concat_axis=0, tiled=True),
        lax.all_to_all(cell_ids, "col", split_axis=0, concat_axis=0, tiled=True),
    )
    channels, rows_here, cols_here = background_std.shape
    steps_off = jnp.array([0, 1, cols_here, cols_here + 1], dtype=jnp.int32)
    targets = arrived_cells[:, None, :] + steps_off[None, :, None]
    adjoint = (
        jnp.zeros((channels * rows_here * cols_here,), jnp.float32)
        .at[targets.reshape(-1)]
        .add(arrived.reshape(-1))
    )
    adjoint = adjoint.reshape(channels, rows_here, cols_here)
    sea_mask = land_sea.astype(jnp.float32)
    spread = background_std.astype(jnp.float32)
    state = spread * sea_mask * adjoint
    rim_depth = 1
    diffusion = diffusivity * sea_mask
    diff_pad = padded_2(diffusion, (("row", 0), ("col", 1)), rim_depth)
    global_row = (
        lax.axis_index("row") * rows_here
        - rim_depth
        + lax.broadcasted_iota(jnp.int32, (rows_here + 2 * rim_depth, 1), 0)
    )
    inside = jnp.logical_and(global_row >= 0, global_row < rows_here * lax.axis_size("row"))
    diff_pad = jnp.where(inside, diff_pad, jnp.float32(0.0))
    for round_index in range(SWEEPS // rim_depth):
        padded = padded_2(state, (("row", 1), ("col", 2)), rim_depth)
        coef_now = diff_pad
        padded, coef_now = sweep(padded, coef_now)
        state = padded
    return spread * sea_mask * state


def solution(mesh):
    placed = (
        P("row", "col", None, None),
        P("row", "col", None, None),
        P("row", "col", None, None, None),
        P("row", "col", None, None),
        P("row", "col", None),
        P("row", "col"),
        P("row", "col"),
        P(None, "row", "col"),
    )
    return jax.shard_map(
        per_device, mesh=mesh, in_specs=placed, out_specs=P(None, "row", "col"), check_vma=False
    )
```

profile of v0, /device:TPU:64, one launch (start us, length us, event | category | flops | bytes accessed | tf_op | source)
XLA Modules:
  0.0 250.4 jit_solution(15949558745488506874)
XLA Ops:
  0.8 4.3 %collective-permute-start = (f32[1,256]{1,0:T(1,128)S(1)}, f32[1,256]{1,0:T(1,128)S(1)}, u32[]{:S(2)}, u32[]{:S(2)}) collective-permute-start(f32[1,256]{1,0:T(1,128)S(1)} %get-tuple-element.40), channel_id=1, source_target_pairs={{0,64},{64,128},{128,192},{192,256},{256,320},{320,384},{384,448},... | collective-permute-start | bytes 3080 | tf_op jit(solution)/shard_map/ppermute | solution.py:16
  5.0 8.2 %collective-permute-start.1 = (f32[1,256]{1,0:T(1,128)S(1)}, f32[1,256]{1,0:T(1,128)S(1)}, u32[]{:S(2)}, u32[]{:S(2)}) collective-permute-start(f32[1,256]{1,0:T(1,128)S(1)} %get-tuple-element.41), channel_id=1, source_target_pairs={{64,0},{128,64},{192,128},{256,192},{320,256},{384,320},{448,384},... | collective-permute-start | bytes 3080 | tf_op jit(solution)/shard_map/ppermute | solution.py:17
  14.0 4.7 %all-to-all-start = ((s32[64,1,32]{2,1,0:T(1,128)}), s32[64,1,32]{2,1,0:T(1,128)S(1)}, u32[]{:S(2)}, u32[]{:S(2)}) async-start(s32[64,1,32]{2,1,0:T(1,128)} %bitcast), calls=%async_computation | async-start | bytes 65536 | tf_op jit(solution)/shard_map/all_to_all | solution.py:71
  23.0 7.0 %collective-permute-start.3 = (f32[18,1]{1,0:T(8,128)S(1)}, f32[18,1]{1,0:T(8,128)S(1)}, u32[]{:S(2)}, u32[]{:S(2)}) collective-permute-start(f32[18,1]{1,0:T(8,128)S(1)} %get-tuple-element.39), channel_id=1, source_target_pairs={{1,0},{2,1},{3,2},{4,3},{5,4},{6,5},{7,6},{8,7},{9,8},{10,9},{11,1... | collective-permute-start | bytes 224 | tf_op jit(solution)/shard_map/ppermute | solution.py:17
  30.0 7.9 %all-to-all-start.1 = ((f32[64,1,128]{2,1,0:T(1,128)}), f32[64,1,128]{2,1,0:T(1,128)S(1)}, u32[]{:S(2)}, u32[]{:S(2)}) async-start(f32[64,1,128]{2,1,0:T(1,128)} %reshape.165), calls=%async_computation.1 | async-start | bytes 65536 | tf_op jit(solution)/shard_map/all_to_all | solution.py:70
  38.8 8.7 %all-to-all-done.1 = f32[64,1,128]{2,1,0:T(1,128)S(1)} async-done(((f32[64,1,128]{2,1,0:T(1,128)}), f32[64,1,128]{2,1,0:T(1,128)S(1)}, u32[]{:S(2)}, u32[]{:S(2)}) %all-to-all-start.1) | async-done | bytes 32800 | tf_op jit(solution)/shard_map/all_to_all | solution.py:70
  48.9 43.3 %scatter_custom_fusion = f32[131072]{0:T(1024)S(1)} fusion(s32[8192]{0:T(1024)S(1)} %bitcast.11, f32[8192]{0:T(1024)S(1)} %reshape.159, f32[]{:T(128)} %constant.10.clone.1), kind=kCustom, calls=%fused_computation.130 | custom fusion | flops 8192 | bytes 524292 | tf_op jit(solution)/shard_map/scatter-add | solution.py:79
  93.4 11.6 %collective-permute-start.5 = (f32[32,1,256]{2,1,0:T(1,128)S(1)}, f32[32,1,256]{2,1,0:T(1,128)S(1)}, u32[]{:S(2)}, u32[]{:S(2)}) collective-permute-start(f32[32,1,256]{2,1,0:T(1,128)S(1)} %get-tuple-element.29), channel_id=1, source_target_pairs={{64,0},{128,64},{192,128},{256,192},{320,256},{384,320},{448,384},... | collective-permute-start | bytes 98312 | tf_op jit(solution)/shard_map/ppermute | solution.py:17
  105.0 1.9 collective-permute-start.4
  107.0 3.8 %collective-permute-done.4 = f32[32,1,256]{2,1,0:T(1,128)S(1)} collective-permute-done((f32[32,1,256]{2,1,0:T(1,128)S(1)}, f32[32,1,256]{2,1,0:T(1,128)S(1)}, u32[]{:S(2)}, u32[]{:S(2)}) %collective-permute-start.4) | collective-permute-done | bytes 32800 | tf_op jit(solution)/shard_map/ppermute | solution.py:16
  111.1 1.9 collective-permute-start.6
  113.0 2.4 collective-permute-start.7
  115.5 2.8 %collective-permute-done.6 = f32[32,18,1]{2,1,0:T(8,128)S(1)} collective-permute-done((f32[32,18,1]{2,1,0:T(8,128)S(1)}, f32[32,18,1]{2,1,0:T(8,128)S(1)}, u32[]{:S(2)}, u32[]{:S(2)}) %collective-permute-start.6) | collective-permute-done | bytes 2336 | tf_op jit(solution)/shard_map/ppermute | solution.py:17
  118.3 7.1 %collective-permute-done.7 = f32[32,18,1]{2,1,0:T(8,128)S(1)} collective-permute-done((f32[32,18,1]{2,1,0:T(8,128)S(1)}, f32[32,18,1]{2,1,0:T(8,128)S(1)}, u32[]{:S(2)}, u32[]{:S(2)}) %collective-permute-start.7) | collective-permute-done | bytes 2336 | tf_op jit(solution)/shard_map/ppermute | solution.py:16
  126.1 5.1 %collective-permute-start.9 = (f32[32,1,256]{2,1,0:T(1,128)S(1)}, f32[32,1,256]{2,1,0:T(1,128)S(1)}, u32[]{:S(2)}, u32[]{:S(2)}) collective-permute-start(f32[32,1,256]{2,1,0:T(1,128)S(1)} %get-tuple-element.27), channel_id=1, source_target_pairs={{64,0},{128,64},{192,128},{256,192},{320,256},{384,320},{448,384},... | collective-permute-start | bytes 98312 | tf_op jit(solution)/shard_map/ppermute | solution.py:17
  131.3 1.9 collective-permute-start.8
  133.2 3.9 %collective-permute-done.8 = f32[32,1,256]{2,1,0:T(1,128)S(1)} collective-permute-done((f32[32,1,256]{2,1,0:T(1,128)S(1)}, f32[32,1,256]{2,1,0:T(1,128)S(1)}, u32[]{:S(2)}, u32[]{:S(2)}) %collective-permute-start.8) | collective-permute-done | bytes 32800 | tf_op jit(solution)/shard_map/ppermute | solution.py:16
  137.4 1.9 collective-permute-start.10
  139.3 2.4 collective-permute-start.11
  141.7 2.9 %collective-permute-done.10 = f32[32,18,1]{2,1,0:T(8,128)S(1)} collective-permute-done((f32[32,18,1]{2,1,0:T(8,128)S(1)}, f32[32,18,1]{2,1,0:T(8,128)S(1)}, u32[]{:S(2)}, u32[]{:S(2)}) %collective-permute-start.10) | collective-permute-done | bytes 2336 | tf_op jit(solution)/shard_map/ppermute | solution.py:17
  144.6 7.1 %collective-permute-done.11 = f32[32,18,1]{2,1,0:T(8,128)S(1)} collective-permute-done((f32[32,18,1]{2,1,0:T(8,128)S(1)}, f32[32,18,1]{2,1,0:T(8,128)S(1)}, u32[]{:S(2)}, u32[]{:S(2)}) %collective-permute-start.11) | collective-permute-done | bytes 2336 | tf_op jit(solution)/shard_map/ppermute | solution.py:16
  152.4 3.1 %collective-permute-start.13 = (f32[32,1,256]{2,1,0:T(1,128)S(1)}, f32[32,1,256]{2,1,0:T(1,128)S(1)}, u32[]{:S(2)}, u32[]{:S(2)}) collective-permute-start(f32[32,1,256]{2,1,0:T(1,128)S(1)} %get-tuple-element.25), channel_id=1, source_target_pairs={{64,0},{128,64},{192,128},{256,192},{320,256},{384,320},{448,384},... | collective-permute-start | bytes 98312 | tf_op jit(solution)/shard_map/ppermute | solution.py:17
  155.6 2.7 %collective-permute-start.12 = (f32[32,1,256]{2,1,0:T(1,128)S(1)}, f32[32,1,256]{2,1,0:T(1,128)S(1)}, u32[]{:S(2)}, u32[]{:S(2)}) collective-permute-start(f32[32,1,256]{2,1,0:T(1,128)S(1)} %get-tuple-element.26), channel_id=1, source_target_pairs={{0,64},{64,128},{128,192},{192,256},{256,320},{320,384},{384,448},... | collective-permute-start | bytes 98312 | tf_op jit(solution)/shard_map/ppermute | solution.py:16
  158.3 3.1 %collective-permute-done.12 = f32[32,1,256]{2,1,0:T(1,128)S(1)} collective-permute-done((f32[32,1,256]{2,1,0:T(1,128)S(1)}, f32[32,1,256]{2,1,0:T(1,128)S(1)}, u32[]{:S(2)}, u32[]{:S(2)}) %collective-permute-start.12) | collective-permute-done | bytes 32800 | tf_op jit(solution)/shard_map/ppermute | solution.py:16
  161.7 1.9 collective-permute-start.14
  163.6 2.4 collective-permute-start.15
  166.0 2.9 %collective-permute-done.14 = f32[32,18,1]{2,1,0:T(8,128)S(1)} collective-permute-done((f32[32,18,1]{2,1,0:T(8,128)S(1)}, f32[32,18,1]{2,1,0:T(8,128)S(1)}, u32[]{:S(2)}, u32[]{:S(2)}) %collective-permute-start.14) | collective-permute-done | bytes 2336 | tf_op jit(solution)/shard_map/ppermute | solution.py:17
  168.9 7.1 %collective-permute-done.15 = f32[32,18,1]{2,1,0:T(8,128)S(1)} collective-permute-done((f32[32,18,1]{2,1,0:T(8,128)S(1)}, f32[32,18,1]{2,1,0:T(8,128)S(1)}, u32[]{:S(2)}, u32[]{:S(2)}) %collective-permute-start.15) | collective-permute-done | bytes 2336 | tf_op jit(solution)/shard_map/ppermute | solution.py:16
  176.7 3.1 %collective-permute-start.17 = (f32[32,1,256]{2,1,0:T(1,128)S(1)}, f32[32,1,256]{2,1,0:T(1,128)S(1)}, u32[]{:S(2)}, u32[]{:S(2)}) collective-permute-start(f32[32,1,256]{2,1,0:T(1,128)S(1)} %get-tuple-element.23), channel_id=1, source_target_pairs={{64,0},{128,64},{192,128},{256,192},{320,256},{384,320},{448,384},... | collective-permute-start | bytes 98312 | tf_op jit(solution)/shard_map/ppermute | solution.py:17
  179.9 2.7 %collective-permute-start.16 = (f32[32,1,256]{2,1,0:T(1,128)S(1)}, f32[32,1,256]{2,1,0:T(1,128)S(1)}, u32[]{:S(2)}, u32[]{:S(2)}) collective-permute-start(f32[32,1,256]{2,1,0:T(1,128)S(1)} %get-tuple-element.24), channel_id=1, source_target_pairs={{0,64},{64,128},{128,192},{192,256},{256,320},{320,384},{384,448},... | collective-permute-start | bytes 98312 | tf_op jit(solution)/shard_map/ppermute | solution.py:16
  182.6 3.1 %collective-permute-done.16 = f32[32,1,256]{2,1,0:T(1,128)S(1)} collective-permute-done((f32[32,1,256]{2,1,0:T(1,128)S(1)}, f32[32,1,256]{2,1,0:T(1,128)S(1)}, u32[]{:S(2)}, u32[]{:S(2)}) %collective-permute-start.16) | collective-permute-done | bytes 32800 | tf_op jit(solution)/shard_map/ppermute | solution.py:16
  185.9 1.9 collective-permute-start.18
  187.9 2.4 collective-permute-start.19
  190.3 2.9 %collective-permute-done.18 = f32[32,18,1]{2,1,0:T(8,128)S(1)} collective-permute-done((f32[32,18,1]{2,1,0:T(8,128)S(1)}, f32[32,18,1]{2,1,0:T(8,128)S(1)}, u32[]{:S(2)}, u32[]{:S(2)}) %collective-permute-start.18) | collective-permute-done | bytes 2336 | tf_op jit(solution)/shard_map/ppermute | solution.py:17
  193.1 7.1 %collective-permute-done.19 = f32[32,18,1]{2,1,0:T(8,128)S(1)} collective-permute-done((f32[32,18,1]{2,1,0:T(8,128)S(1)}, f32[32,18,1]{2,1,0:T(8,128)S(1)}, u32[]{:S(2)}, u32[]{:S(2)}) %collective-permute-start.19) | collective-permute-done | bytes 2336 | tf_op jit(solution)/shard_map/ppermute | solution.py:16
  201.0 3.1 %collective-permute-start.21 = (f32[32,1,256]{2,1,0:T(1,128)S(1)}, f32[32,1,256]{2,1,0:T(1,128)S(1)}, u32[]{:S(2)}, u32[]{:S(2)}) collective-permute-start(f32[32,1,256]{2,1,0:T(1,128)S(1)} %get-tuple-element.21), channel_id=1, source_target_pairs={{64,0},{128,64},{192,128},{256,192},{320,256},{384,320},{448,384},... | collective-permute-start | bytes 98312 | tf_op jit(solution)/shard_map/ppermute | solution.py:17
  204.1 2.7 %collective-permute-start.20 = (f32[32,1,256]{2,1,0:T(1,128)S(1)}, f32[32,1,256]{2,1,0:T(1,128)S(1)}, u32[]{:S(2)}, u32[]{:S(2)}) collective-permute-start(f32[32,1,256]{2,1,0:T(1,128)S(1)} %get-tuple-element.22), channel_id=1, source_target_pairs={{0,64},{64,128},{128,192},{192,256},{256,320},{320,384},{384,448},... | collective-permute-start | bytes 98312 | tf_op jit(solution)/shard_map/ppermute | solution.py:16
  206.9 3.1 %collective-permute-done.20 = f32[32,1,256]{2,1,0:T(1,128)S(1)} collective-permute-done((f32[32,1,256]{2,1,0:T(1,128)S(1)}, f32[32,1,256]{2,1,0:T(1,128)S(1)}, u32[]{:S(2)}, u32[]{:S(2)}) %collective-permute-start.20) | collective-permute-done | bytes 32800 | tf_op jit(solution)/shard_map/ppermute | solution.py:16
  212.2 2.4 collective-permute-start.23
  214.6 2.9 %collective-permute-done.22 = f32[32,18,1]{2,1,0:T(8,128)S(1)} collective-permute-done((f32[32,18,1]{2,1,0:T(8,128)S(1)}, f32[32,18,1]{2,1,0:T(8,128)S(1)}, u32[]{:S(2)}, u32[]{:S(2)}) %collective-permute-start.22) | collective-permute-done | bytes 2336 | tf_op jit(solution)/shard_map/ppermute | solution.py:17
  217.4 7.1 %collective-permute-done.23 = f32[32,18,1]{2,1,0:T(8,128)S(1)} collective-permute-done((f32[32,18,1]{2,1,0:T(8,128)S(1)}, f32[32,18,1]{2,1,0:T(8,128)S(1)}, u32[]{:S(2)}, u32[]{:S(2)}) %collective-permute-start.23) | collective-permute-done | bytes 2336 | tf_op jit(solution)/shard_map/ppermute | solution.py:16
  225.3 3.1 %collective-permute-start.25 = (f32[32,1,256]{2,1,0:T(1,128)S(1)}, f32[32,1,256]{2,1,0:T(1,128)S(1)}, u32[]{:S(2)}, u32[]{:S(2)}) collective-permute-start(f32[32,1,256]{2,1,0:T(1,128)S(1)} %get-tuple-element.19), channel_id=1, source_target_pairs={{64,0},{128,64},{192,128},{256,192},{320,256},{384,320},{448,384},... | collective-permute-start | bytes 98312 | tf_op jit(solution)/shard_map/ppermute | solution.py:17
  228.4 2.7 %collective-permute-start.24 = (f32[32,1,256]{2,1,0:T(1,128)S(1)}, f32[32,1,256]{2,1,0:T(1,128)S(1)}, u32[]{:S(2)}, u32[]{:S(2)}) collective-permute-start(f32[32,1,256]{2,1,0:T(1,128)S(1)} %get-tuple-element.20), channel_id=1, source_target_pairs={{0,64},{64,128},{128,192},{192,256},{256,320},{320,384},{384,448},... | collective-permute-start | bytes 98312 | tf_op jit(solution)/shard_map/ppermute | solution.py:16
  231.2 3.1 %collective-permute-done.24 = f32[32,1,256]{2,1,0:T(1,128)S(1)} collective-permute-done((f32[32,1,256]{2,1,0:T(1,128)S(1)}, f32[32,1,256]{2,1,0:T(1,128)S(1)}, u32[]{:S(2)}, u32[]{:S(2)}) %collective-permute-start.24) | collective-permute-done | bytes 32800 | tf_op jit(solution)/shard_map/ppermute | solution.py:16
  234.5 1.9 collective-permute-start.26
  236.5 2.4 collective-permute-start.27
  238.9 2.9 %collective-permute-done.26 = f32[32,18,1]{2,1,0:T(8,128)S(1)} collective-permute-done((f32[32,18,1]{2,1,0:T(8,128)S(1)}, f32[32,18,1]{2,1,0:T(8,128)S(1)}, u32[]{:S(2)}, u32[]{:S(2)}) %collective-permute-start.26) | collective-permute-done | bytes 2336 | tf_op jit(solution)/shard_map/ppermute | solution.py:17
  241.7 7.1 %collective-permute-done.27 = f32[32,18,1]{2,1,0:T(8,128)S(1)} collective-permute-done((f32[32,18,1]{2,1,0:T(8,128)S(1)}, f32[32,18,1]{2,1,0:T(8,128)S(1)}, u32[]{:S(2)}, u32[]{:S(2)}) %collective-permute-start.27) | collective-permute-done | bytes 2336 | tf_op jit(solution)/shard_map/ppermute | solution.py:16
  (76 shorter events, 17.9 us)
Async XLA Ops:
  0.0 13.3 %copy-start.3 = (s32[1,1,64,32]{2,3,1,0:T(8,128)S(1)}, s32[1,1,64,32]{2,3,1,0:T(8,128)}, u32[]{:S(2)}) copy-start(s32[1,1,64,32]{2,3,1,0:T(8,128)} %param.12) | copy-start | bytes 24580
  0.8 20.2 %collective-permute-start = (f32[1,256]{1,0:T(1,128)S(1)}, f32[1,256]{1,0:T(1,128)S(1)}, u32[]{:S(2)}, u32[]{:S(2)}) collective-permute-start(f32[1,256]{1,0:T(1,128)S(1)} %get-tuple-element.40), channel_id=1, source_target_pairs={{0,64},{64,128},{128,192},{192,256},{256,320},{320,384},{384,448},... | collective-permute-start | bytes 3080 | tf_op jit(solution)/shard_map/ppermute | solution.py:16
  5.0 16.0 %collective-permute-start.1 = (f32[1,256]{1,0:T(1,128)S(1)}, f32[1,256]{1,0:T(1,128)S(1)}, u32[]{:S(2)}, u32[]{:S(2)}) collective-permute-start(f32[1,256]{1,0:T(1,128)S(1)} %get-tuple-element.41), channel_id=1, source_target_pairs={{64,0},{128,64},{192,128},{256,192},{320,256},{384,320},{448,384},... | collective-permute-start | bytes 3080 | tf_op jit(solution)/shard_map/ppermute | solution.py:17
  14.0 4.8 %copy-start.1 = (f32[1,1,64,2,32]{2,4,3,1,0:T(8,128)S(1)}, f32[1,1,64,2,32]{2,4,3,1,0:T(8,128)}, u32[]{:S(2)}) copy-start(f32[1,1,64,2,32]{2,4,3,1,0:T(8,128)} %param.11) | copy-start | bytes 49156
  14.0 4.8 %copy-start.4 = (f32[1,1,64,32]{2,3,1,0:T(8,128)S(1)}, f32[1,1,64,32]{2,3,1,0:T(8,128)}, u32[]{:S(2)}) copy-start(f32[1,1,64,32]{2,3,1,0:T(8,128)} %param.9) | copy-start | bytes 24580
  14.0 4.8 %copy-start.5 = (f32[1,1,64,32]{2,3,1,0:T(8,128)S(1)}, f32[1,1,64,32]{2,3,1,0:T(8,128)}, u32[]{:S(2)}) copy-start(f32[1,1,64,32]{2,3,1,0:T(8,128)} %param.10) | copy-start | bytes 24580
  14.0 16.0 %all-to-all-start = ((s32[64,1,32]{2,1,0:T(1,128)}), s32[64,1,32]{2,1,0:T(1,128)S(1)}, u32[]{:S(2)}, u32[]{:S(2)}) async-start(s32[64,1,32]{2,1,0:T(1,128)} %bitcast), calls=%async_computation | async-start | bytes 65536 | tf_op jit(solution)/shard_map/all_to_all | solution.py:71
  18.7 0.7 copy-start.6
  19.4 0.7 copy-start.2
  21.1 85.8 %collective-permute-start.2 = (f32[18,1]{1,0:T(8,128)S(1)}, f32[18,1]{1,0:T(8,128)S(1)}, u32[]{:S(2)}, u32[]{:S(2)}) collective-permute-start(f32[18,1]{1,0:T(8,128)S(1)} %get-tuple-element.38), channel_id=1, source_target_pairs={{0,1},{1,2},{2,3},{3,4},{4,5},{5,6},{6,7},{7,8},{8,9},{9,10},{10,1... | collective-permute-start | bytes 224 | tf_op jit(solution)/shard_map/ppermute | solution.py:16
  23.0 83.9 %collective-permute-start.3 = (f32[18,1]{1,0:T(8,128)S(1)}, f32[18,1]{1,0:T(8,128)S(1)}, u32[]{:S(2)}, u32[]{:S(2)}) collective-permute-start(f32[18,1]{1,0:T(8,128)S(1)} %get-tuple-element.39), channel_id=1, source_target_pairs={{1,0},{2,1},{3,2},{4,3},{5,4},{6,5},{7,6},{8,7},{9,8},{10,9},{11,1... | collective-permute-start | bytes 224 | tf_op jit(solution)/shard_map/ppermute | solution.py:17
  30.0 17.5 %all-to-all-start.1 = ((f32[64,1,128]{2,1,0:T(1,128)}), f32[64,1,128]{2,1,0:T(1,128)S(1)}, u32[]{:S(2)}, u32[]{:S(2)}) async-start(f32[64,1,128]{2,1,0:T(1,128)} %reshape.165), calls=%async_computation.1 | async-start | bytes 65536 | tf_op jit(solution)/shard_map/all_to_all | solution.py:70
  37.9 0.7 copy-start.7
  92.3 1.0 copy-start
  93.4 13.6 %collective-permute-start.5 = (f32[32,1,256]{2,1,0:T(1,128)S(1)}, f32[32,1,256]{2,1,0:T(1,128)S(1)}, u32[]{:S(2)}, u32[]{:S(2)}) collective-permute-start(f32[32,1,256]{2,1,0:T(1,128)S(1)} %get-tuple-element.29), channel_id=1, source_target_pairs={{64,0},{128,64},{192,128},{256,192},{320,256},{384,320},{448,384},... | collective-permute-start | bytes 98312 | tf_op jit(solution)/shard_map/ppermute | solution.py:17
  105.0 5.8 %collective-permute-start.4 = (f32[32,1,256]{2,1,0:T(1,128)S(1)}, f32[32,1,256]{2,1,0:T(1,128)S(1)}, u32[]{:S(2)}, u32[]{:S(2)}) collective-permute-start(f32[32,1,256]{2,1,0:T(1,128)S(1)} %get-tuple-element.30), channel_id=1, source_target_pairs={{0,64},{64,128},{128,192},{192,256},{256,320},{320,384},{384,448},... | collective-permute-start | bytes 98312 | tf_op jit(solution)/shard_map/ppermute | solution.py:16
  111.1 7.2 %collective-permute-start.6 = (f32[32,18,1]{2,1,0:T(8,128)S(1)}, f32[32,18,1]{2,1,0:T(8,128)S(1)}, u32[]{:S(2)}, u32[]{:S(2)}) collective-permute-start(f32[32,18,1]{2,1,0:T(8,128)S(1)} %get-tuple-element.17), channel_id=1, source_target_pairs={{1,0},{2,1},{3,2},{4,3},{5,4},{6,5},{7,6},{8,7},{9,8},{10,9},{11,1... | collective-permute-start | bytes 6920 | tf_op jit(solution)/shard_map/ppermute | solution.py:17
  113.0 12.4 %collective-permute-start.7 = (f32[32,18,1]{2,1,0:T(8,128)S(1)}, f32[32,18,1]{2,1,0:T(8,128)S(1)}, u32[]{:S(2)}, u32[]{:S(2)}) collective-permute-start(f32[32,18,1]{2,1,0:T(8,128)S(1)} %get-tuple-element.18), channel_id=1, source_target_pairs={{0,1},{1,2},{2,3},{3,4},{4,5},{5,6},{6,7},{7,8},{8,9},{9,10},{10,1... | collective-permute-start | bytes 6920 | tf_op jit(solution)/shard_map/ppermute | solution.py:16
  126.1 7.1 %collective-permute-start.9 = (f32[32,1,256]{2,1,0:T(1,128)S(1)}, f32[32,1,256]{2,1,0:T(1,128)S(1)}, u32[]{:S(2)}, u32[]{:S(2)}) collective-permute-start(f32[32,1,256]{2,1,0:T(1,128)S(1)} %get-tuple-element.27), channel_id=1, source_target_pairs={{64,0},{128,64},{192,128},{256,192},{320,256},{384,320},{448,384},... | collective-permute-start | bytes 98312 | tf_op jit(solution)/shard_map/ppermute | solution.py:17
  131.3 5.8 %collective-permute-start.8 = (f32[32,1,256]{2,1,0:T(1,128)S(1)}, f32[32,1,256]{2,1,0:T(1,128)S(1)}, u32[]{:S(2)}, u32[]{:S(2)}) collective-permute-start(f32[32,1,256]{2,1,0:T(1,128)S(1)} %get-tuple-element.28), channel_id=1, source_target_pairs={{0,64},{64,128},{128,192},{192,256},{256,320},{320,384},{384,448},... | collective-permute-start | bytes 98312 | tf_op jit(solution)/shard_map/ppermute | solution.py:16
  137.4 7.2 %collective-permute-start.10 = (f32[32,18,1]{2,1,0:T(8,128)S(1)}, f32[32,18,1]{2,1,0:T(8,128)S(1)}, u32[]{:S(2)}, u32[]{:S(2)}) collective-permute-start(f32[32,18,1]{2,1,0:T(8,128)S(1)} %get-tuple-element.15), channel_id=1, source_target_pairs={{1,0},{2,1},{3,2},{4,3},{5,4},{6,5},{7,6},{8,7},{9,8},{10,9},{11,1... | collective-permute-start | bytes 6920 | tf_op jit(solution)/shard_map/ppermute | solution.py:17
  139.3 12.4 %collective-permute-start.11 = (f32[32,18,1]{2,1,0:T(8,128)S(1)}, f32[32,18,1]{2,1,0:T(8,128)S(1)}, u32[]{:S(2)}, u32[]{:S(2)}) collective-permute-start(f32[32,18,1]{2,1,0:T(8,128)S(1)} %get-tuple-element.16), channel_id=1, source_target_pairs={{0,1},{1,2},{2,3},{3,4},{4,5},{5,6},{6,7},{7,8},{8,9},{9,10},{10,1... | collective-permute-start | bytes 6920 | tf_op jit(solution)/shard_map/ppermute | solution.py:16
  152.4 5.9 %collective-permute-start.13 = (f32[32,1,256]{2,1,0:T(1,128)S(1)}, f32[32,1,256]{2,1,0:T(1,128)S(1)}, u32[]{:S(2)}, u32[]{:S(2)}) collective-permute-start(f32[32,1,256]{2,1,0:T(1,128)S(1)} %get-tuple-element.25), channel_id=1, source_target_pairs={{64,0},{128,64},{192,128},{256,192},{320,256},{384,320},{448,384},... | collective-permute-start | bytes 98312 | tf_op jit(solution)/shard_map/ppermute | solution.py:17
  155.6 5.8 %collective-permute-start.12 = (f32[32,1,256]{2,1,0:T(1,128)S(1)}, f32[32,1,256]{2,1,0:T(1,128)S(1)}, u32[]{:S(2)}, u32[]{:S(2)}) collective-permute-start(f32[32,1,256]{2,1,0:T(1,128)S(1)} %get-tuple-element.26), channel_id=1, source_target_pairs={{0,64},{64,128},{128,192},{192,256},{256,320},{320,384},{384,448},... | collective-permute-start | bytes 98312 | tf_op jit(solution)/shard_map/ppermute | solution.py:16
  161.7 7.2 %collective-permute-start.14 = (f32[32,18,1]{2,1,0:T(8,128)S(1)}, f32[32,18,1]{2,1,0:T(8,128)S(1)}, u32[]{:S(2)}, u32[]{:S(2)}) collective-permute-start(f32[32,18,1]{2,1,0:T(8,128)S(1)} %get-tuple-element.13), channel_id=1, source_target_pairs={{1,0},{2,1},{3,2},{4,3},{5,4},{6,5},{7,6},{8,7},{9,8},{10,9},{11,1... | collective-permute-start | bytes 6920 | tf_op jit(solution)/shard_map/ppermute | solution.py:17
  163.6 12.4 %collective-permute-start.15 = (f32[32,18,1]{2,1,0:T(8,128)S(1)}, f32[32,18,1]{2,1,0:T(8,128)S(1)}, u32[]{:S(2)}, u32[]{:S(2)}) collective-permute-start(f32[32,18,1]{2,1,0:T(8,128)S(1)} %get-tuple-element.14), channel_id=1, source_target_pairs={{0,1},{1,2},{2,3},{3,4},{4,5},{5,6},{6,7},{7,8},{8,9},{9,10},{10,1... | collective-permute-start | bytes 6920 | tf_op jit(solution)/shard_map/ppermute | solution.py:16
  176.7 5.9 %collective-permute-start.17 = (f32[32,1,256]{2,1,0:T(1,128)S(1)}, f32[32,1,256]{2,1,0:T(1,128)S(1)}, u32[]{:S(2)}, u32[]{:S(2)}) collective-permute-start(f32[32,1,256]{2,1,0:T(1,128)S(1)} %get-tuple-element.23), channel_id=1, source_target_pairs={{64,0},{128,64},{192,128},{256,192},{320,256},{384,320},{448,384},... | collective-permute-start | bytes 98312 | tf_op jit(solution)/shard_map/ppermute | solution.py:17
  179.9 5.8 %collective-permute-start.16 = (f32[32,1,256]{2,1,0:T(1,128)S(1)}, f32[32,1,256]{2,1,0:T(1,128)S(1)}, u32[]{:S(2)}, u32[]{:S(2)}) collective-permute-start(f32[32,1,256]{2,1,0:T(1,128)S(1)} %get-tuple-element.24), channel_id=1, source_target_pairs={{0,64},{64,128},{128,192},{192,256},{256,320},{320,384},{384,448},... | collective-permute-start | bytes 98312 | tf_op jit(solution)/shard_map/ppermute | solution.py:16
  185.9 7.2 %collective-permute-start.18 = (f32[32,18,1]{2,1,0:T(8,128)S(1)}, f32[32,18,1]{2,1,0:T(8,128)S(1)}, u32[]{:S(2)}, u32[]{:S(2)}) collective-permute-start(f32[32,18,1]{2,1,0:T(8,128)S(1)} %get-tuple-element.11), channel_id=1, source_target_pairs={{1,0},{2,1},{3,2},{4,3},{5,4},{6,5},{7,6},{8,7},{9,8},{10,9},{11,1... | collective-permute-start | bytes 6920 | tf_op jit(solution)/shard_map/ppermute | solution.py:17
  187.9 12.4 %collective-permute-start.19 = (f32[32,18,1]{2,1,0:T(8,128)S(1)}, f32[32,18,1]{2,1,0:T(8,128)S(1)}, u32[]{:S(2)}, u32[]{:S(2)}) collective-permute-start(f32[32,18,1]{2,1,0:T(8,128)S(1)} %get-tuple-element.12), channel_id=1, source_target_pairs={{0,1},{1,2},{2,3},{3,4},{4,5},{5,6},{6,7},{7,8},{8,9},{9,10},{10,1... | collective-permute-start | bytes 6920 | tf_op jit(solution)/shard_map/ppermute | solution.py:16
  201.0 5.9 %collective-permute-start.21 = (f32[32,1,256]{2,1,0:T(1,128)S(1)}, f32[32,1,256]{2,1,0:T(1,128)S(1)}, u32[]{:S(2)}, u32[]{:S(2)}) collective-permute-start(f32[32,1,256]{2,1,0:T(1,128)S(1)} %get-tuple-element.21), channel_id=1, source_target_pairs={{64,0},{128,64},{192,128},{256,192},{320,256},{384,320},{448,384},... | collective-permute-start | bytes 98312 | tf_op jit(solution)/shard_map/ppermute | solution.py:17
  204.1 5.8 %collective-permute-start.20 = (f32[32,1,256]{2,1,0:T(1,128)S(1)}, f32[32,1,256]{2,1,0:T(1,128)S(1)}, u32[]{:S(2)}, u32[]{:S(2)}) collective-permute-start(f32[32,1,256]{2,1,0:T(1,128)S(1)} %get-tuple-element.22), channel_id=1, source_target_pairs={{0,64},{64,128},{128,192},{192,256},{256,320},{320,384},{384,448},... | collective-permute-start | bytes 98312 | tf_op jit(solution)/shard_map/ppermute | solution.py:16
  210.2 7.2 %collective-permute-start.22 = (f32[32,18,1]{2,1,0:T(8,128)S(1)}, f32[32,18,1]{2,1,0:T(8,128)S(1)}, u32[]{:S(2)}, u32[]{:S(2)}) collective-permute-start(f32[32,18,1]{2,1,0:T(8,128)S(1)} %get-tuple-element.9), channel_id=1, source_target_pairs={{1,0},{2,1},{3,2},{4,3},{5,4},{6,5},{7,6},{8,7},{9,8},{10,9},{11,1... | collective-permute-start | bytes 6920 | tf_op jit(solution)/shard_map/ppermute | solution.py:17
  212.2 12.4 %collective-permute-start.23 = (f32[32,18,1]{2,1,0:T(8,128)S(1)}, f32[32,18,1]{2,1,0:T(8,128)S(1)}, u32[]{:S(2)}, u32[]{:S(2)}) collective-permute-start(f32[32,18,1]{2,1,0:T(8,128)S(1)} %get-tuple-element.10), channel_id=1, source_target_pairs={{0,1},{1,2},{2,3},{3,4},{4,5},{5,6},{6,7},{7,8},{8,9},{9,10},{10,1... | collective-permute-start | bytes 6920 | tf_op jit(solution)/shard_map/ppermute | solution.py:16
  225.3 5.9 %collective-permute-start.25 = (f32[32,1,256]{2,1,0:T(1,128)S(1)}, f32[32,1,256]{2,1,0:T(1,128)S(1)}, u32[]{:S(2)}, u32[]{:S(2)}) collective-permute-start(f32[32,1,256]{2,1,0:T(1,128)S(1)} %get-tuple-element.19), channel_id=1, source_target_pairs={{64,0},{128,64},{192,128},{256,192},{320,256},{384,320},{448,384},... | collective-permute-start | bytes 98312 | tf_op jit(solution)/shard_map/ppermute | solution.py:17
  228.4 5.8 %collective-permute-start.24 = (f32[32,1,256]{2,1,0:T(1,128)S(1)}, f32[32,1,256]{2,1,0:T(1,128)S(1)}, u32[]{:S(2)}, u32[]{:S(2)}) collective-permute-start(f32[32,1,256]{2,1,0:T(1,128)S(1)} %get-tuple-element.20), channel_id=1, source_target_pairs={{0,64},{64,128},{128,192},{192,256},{256,320},{320,384},{384,448},... | collective-permute-start | bytes 98312 | tf_op jit(solution)/shard_map/ppermute | solution.py:16
  234.5 7.2 %collective-permute-start.26 = (f32[32,18,1]{2,1,0:T(8,128)S(1)}, f32[32,18,1]{2,1,0:T(8,128)S(1)}, u32[]{:S(2)}, u32[]{:S(2)}) collective-permute-start(f32[32,18,1]{2,1,0:T(8,128)S(1)} %get-tuple-element.7), channel_id=1, source_target_pairs={{1,0},{2,1},{3,2},{4,3},{5,4},{6,5},{7,6},{8,7},{9,8},{10,9},{11,1... | collective-permute-start | bytes 6920 | tf_op jit(solution)/shard_map/ppermute | solution.py:17
  236.5 12.4 %collective-permute-start.27 = (f32[32,18,1]{2,1,0:T(8,128)S(1)}, f32[32,18,1]{2,1,0:T(8,128)S(1)}, u32[]{:S(2)}, u32[]{:S(2)}) collective-permute-start(f32[32,18,1]{2,1,0:T(8,128)S(1)} %get-tuple-element.8), channel_id=1, source_target_pairs={{0,1},{1,2},{2,3},{3,4},{4,5},{5,6},{6,7},{7,8},{8,9},{9,10},{10,1... | collective-permute-start | bytes 6920 | tf_op jit(solution)/shard_map/ppermute | solution.py:16
where the time goes:
time: 252 us; the launch traced here: 250 us
  starting transfers between devices  104 us (41%)
  waiting for transfers between devices  88.5 us (35%)
  other arithmetic  50.7 us (20%)
  local copies, waits for them, and re-layouts  6.71 us (3%)
    ppermute x14, waiting for transfers between devices, padded_2(): before = lax.ppermute(last, axis, up)  62.8 us
    ppermute x14, starting transfers between devices, padded_2(): after = lax.ppermute(initial, axis, down)  55.9 us
    scatter-add x1, other arithmetic, per_device(): adjoint = jnp.zeros((channels * rows_here * cols_here,), jnp.float32).at[...  43.3 us
    ppermute x14, starting transfers between devices, padded_2(): before = lax.ppermute(last, axis, up)  35.3 us
    ppermute x14, waiting for transfers between devices, padded_2(): after = lax.ppermute(initial, axis, down)  17.1 us
    all_to_all x1, waiting for transfers between devices, per_device(): lax.all_to_all(corners, 'col', split_axis=0, concat_axis=0, tiled=True)  8.66 us
    all_to_all x1, starting transfers between devices, per_device(): lax.all_to_all(corners, 'col', split_axis=0, concat_axis=0, tiled=True)  7.88 us
  transfers between devices with their start and end apart: 30, of which 19 were waited for; matrix products, arithmetic and copies ran while one was open for 19% of the time, Pallas kernels for 0%

commit v1 on v0

v1 whole, which is shorter than its diff:
```python
import jax
import jax.numpy as jnp
from jax import lax
from jax.experimental import pallas as pl
from jax.experimental.pallas import tpu as pltpu
from jax.sharding import PartitionSpec as P

SWEEPS = 6
LANES = 128
RIM = 8
VMEM_BYTES = 24 * 1024 * 1024

WHOLE = pl.BlockSpec(memory_space=pltpu.VMEM)
NT = (((1,), (1,)), ((), ()))


def kernel_call(body, name, outs, inputs, scratch=(), flops=0, moved=0):
    return pl.pallas_call(
        body,
        name=name,
        out_shape=outs,
        in_specs=[WHOLE] * len(inputs),
        out_specs=jax.tree.map(lambda _: WHOLE, outs),
        scratch_shapes=list(scratch),
        compiler_params=pltpu.CompilerParams(vmem_limit_bytes=VMEM_BYTES),
        cost_estimate=pl.CostEstimate(flops=flops, bytes_accessed=moved, transcendentals=0),
    )(*inputs)


def f32(*shape):
    return jax.ShapeDtypeStruct(shape, jnp.float32)


def pack_body(innovation, precision, offsets, cells, counts, out, tile, rows):
    slots, dests = innovation.shape
    live = lax.broadcasted_iota(jnp.int32, (slots, dests), 0) < counts[...]
    tile[0:slots, 0:dests] = jnp.where(live, innovation[...] * precision[...], 0.0)
    tile[slots : 2 * slots, 0:dests] = offsets[0]
    tile[2 * slots : 3 * slots, 0:dests] = offsets[1]
    tile[3 * slots : 4 * slots, 0:dests] = cells[...].astype(jnp.float32)
    rows[...] = tile[...].T
    for d in range(dests):
        for k in range(3):
            out[d, :, k * LANES : (k + 1) * LANES] = rows[pl.ds((d + k - 1) % dests, 1), :]


def fixed_body(std, sea, diffusivity, spread, coef, first, last, stage):
    channels, rows, cols = std.shape
    mask = sea[...].astype(jnp.float32)
    product = std[...].astype(jnp.float32) * mask[None]
    for part in range(cols // LANES):
        stage[part] = product[:, :, part * LANES : (part + 1) * LANES].reshape(channels * rows, LANES)
    coef[...] = diffusivity[...] * mask
    lane = lax.broadcasted_iota(jnp.int32, (channels, LANES), 1)
    ends = [jnp.zeros((channels, LANES), jnp.float32)] * 2
    for i in range(rows):
        here = [stage[part, pl.ds(i, channels, stride=rows), :] for part in range(cols // LANES)]
        for part, values in enumerate(here):
            spread[i, :, part * LANES : (part + 1) * LANES] = values
        inside = (lane >= RIM * i) & (lane < RIM * (i + 1))
        ends[0] = jnp.where(inside, pltpu.roll(here[0], (RIM * i) % LANES, 1), ends[0])
        ends[1] = jnp.where(inside, pltpu.roll(here[-1], (RIM * i + RIM) % LANES, 1), ends[1])
    lane_row = lax.broadcasted_iota(jnp.int32, (1, LANES), 1)
    for which, rim in enumerate((first, last)):
        edge = coef[:, 0:LANES] if which == 0 else coef[:, cols - LANES : cols]
        packed = jnp.zeros((1, LANES), jnp.float32)
        for i in range(rows):
            inside = (lane_row >= RIM * i) & (lane_row < RIM * (i + 1))
            turned = pltpu.roll(edge[i : i + 1], (RIM * i + RIM * which) % LANES, 1)
            packed = jnp.where(inside, turned, packed)
        rim[0:channels] = ends[which]
        rim[channels : channels + 8] = jnp.broadcast_to(packed, (8, LANES))


def record_fields(block, slots):
    quarter = block.shape[0] // 4
    lane = lax.broadcasted_iota(jnp.int32, (quarter, LANES), 1)
    fields = []
    for f in range(4):
        joined = None
        for b in range(4):
            part = block[b * quarter : (b + 1) * quarter]
            turn = (slots * (b - f)) % LANES
            if turn:
                part = pltpu.roll(part, turn, 1)
            joined = part if b == 0 else jnp.where(lane >= slots * b, part, joined)
        fields.append(joined)
    return fields


def split(values):
    high = values.astype(jnp.bfloat16)
    low = (values - high.astype(jnp.float32)).astype(jnp.bfloat16)
    return high, low


def two_hot(size, position, at, after):
    row = lax.broadcasted_iota(jnp.int32, (size, position.shape[1]), 0) - position
    return jnp.where(row == 0, at, jnp.where(row == 1, after, 0.0))


def dot_split(a, b):
    dot = lambda x, y: lax.dot_general(x[...], y[...], NT, preferred_element_type=jnp.float32)
    return dot(a[0], b[0]) + (dot(a[0], b[1]) + dot(a[1], b[0]))


def build_body(
    arrived, spread, coef, rim_left, rim_right,
    state, coef_out, to_up, to_down,
    field_ref, a_high, a_low, b_high, b_low, c_high, c_low, d_high, d_low,
):
    rows, channels, cols = spread.shape
    slots = LANES // 4
    blocks = field_ref.shape[2]

    for k in range(3):
        for f, values in enumerate(record_fields(arrived[:, 0, k * LANES : (k + 1) * LANES], slots)):
            field_ref[k, f] = values

    def unpack(k, n):
        weight, east, north, cell = [field_ref[k, f, pl.ds(n, 1), :] for f in range(4)]
        cell = cell.astype(jnp.int32)
        return weight, east, north, cell >> 12, (cell >> 8) & 15, cell & 255

    def own(n, carry):
        weight, east, north, channel, i, j = unpack(1, n)
        here = pl.ds(pl.multiple_of(n * LANES, LANES), LANES)
        hot = lax.broadcasted_iota(jnp.int32, (channels, LANES), 0) == channel
        by_row = two_hot(rows, i, weight * (1.0 - north), weight * north)
        high = by_row.astype(jnp.bfloat16).astype(jnp.float32)
        low = by_row - high
        for row in range(rows):
            at = slice(row * channels, (row + 1) * channels)
            a_high[at, here] = jnp.where(hot, high[row : row + 1], 0.0).astype(jnp.bfloat16)
            a_low[at, here] = jnp.where(hot, low[row : row + 1], 0.0).astype(jnp.bfloat16)
        b_high[:, here], b_low[:, here] = split(two_hot(cols, j, 1.0 - east, east))
        return carry

    lax.fori_loop(0, blocks, own, 0)

    def rim(n, carry):
        here = pl.ds(pl.multiple_of(n * LANES, LANES), LANES)
        for side, (k, base) in enumerate(((0, cols - RIM), (2, 0))):
            weight, east, north, channel, i, j = unpack(k, n)
            hot = lax.broadcasted_iota(jnp.int32, (channels, LANES), 0) == channel
            c_high[side, :, here], c_low[side, :, here] = split(jnp.where(hot, weight, 0.0))
            by_row = two_hot(rows, i, 1.0 - north, north)
            by_col = two_hot(RIM, j - base, 1.0 - east, east)
            both = (by_row[:, None, :] * by_col[None, :, :]).reshape(rows * RIM, LANES)
            d_high[side, :, here], d_low[side, :, here] = split(both)
        return carry

    lax.fori_loop(0, blocks, rim, 0)

    adjoint = dot_split((a_high, a_low), (b_high, b_low))
    sides = []
    for side, halo in enumerate((rim_left, rim_right)):
        product = dot_split((c_high.at[side], c_low.at[side]), (d_high.at[side], d_low.at[side]))
        sides.append(product * halo[0:channels])

    lane = lax.broadcasted_iota(jnp.int32, (channels, LANES), 1)
    lane_row = lax.broadcasted_iota(jnp.int32, (1, LANES), 1)

    def outer(left, right, i, lanes):
        left = pltpu.roll(left, (LANES - RIM - RIM * i) % LANES, 1)
        right = pltpu.roll(right, (LANES - RIM * i) % LANES, 1)
        return jnp.where(lanes < RIM, right, jnp.where(lanes >= LANES - RIM, left, 0.0))

    coef_out[:, 0:cols] = coef[...]
    tails = []
    for i in range(rows):
        state[i, :, 0:cols] = adjoint[i * channels : (i + 1) * channels] * spread[i]
        tail = outer(sides[0], sides[1], i, lane)
        state[i, :, cols : cols + LANES] = tail
        tails.append(tail)
        coef_out[i : i + 1, cols : cols + LANES] = outer(
            rim_left[channels : channels + 1], rim_right[channels : channels + 1], i, lane_row
        )

    for out, start in ((to_down, 0), (to_up, rows - SWEEPS)):
        packed = jnp.zeros((channels, LANES), jnp.float32)
        for q in range(SWEEPS):
            i = start + q
            out[q * channels : (q + 1) * channels, :] = state[i, :, 0:cols]
            inside = (lane >= 2 * RIM * q) & (lane < 2 * RIM * (q + 1))
            packed = jnp.where(inside, pltpu.roll(tails[i], (2 * RIM * q + RIM) % LANES, 1), packed)
        base = SWEEPS * channels
        half = channels // 2
        out[base : base + half, 0:LANES] = packed[0:half]
        out[base : base + half, LANES : 2 * LANES] = packed[half:channels]
        base = base + half
        out[base : base + 8, :] = jnp.zeros((8, cols), jnp.float32)
        out[base : base + SWEEPS, :] = coef_out[start : start + SWEEPS, 0:cols]
        out[base + 8 : base + 16, :] = jnp.zeros((8, cols), jnp.float32)
        out[base + 8 : base + 8 + SWEEPS, 0:LANES] = coef_out[start : start + SWEEPS, cols : cols + LANES]


def sweep_body(state, coef, spread, from_down, from_up, out, work, east, north, stage):
    rows, channels, width = state.shape
    cols = width - LANES
    depth = rows + 2 * SWEEPS
    groups = channels // 8
    half = channels // 2
    lane = lax.broadcasted_iota(jnp.int32, (channels, LANES), 1)

    stage[...] = jnp.zeros_like(stage)
    stage[SWEEPS : SWEEPS + rows, :] = coef[...]
    for block, start in ((from_down, 0), (from_up, SWEEPS + rows)):
        base = SWEEPS * channels
        packed = jnp.concatenate([block[base : base + half, 0:LANES], block[base : base + half, LANES : 2 * LANES]], axis=0)
        for q in range(SWEEPS):
            work[start + q, :, 0:cols] = block[q * channels : (q + 1) * channels, :]
            tail = pltpu.roll(packed, (LANES - 2 * RIM * q - RIM) % LANES, 1)
            work[start + q, :, cols:width] = jnp.where((lane < RIM) | (lane >= LANES - RIM), tail, 0.0)
        base = base + half
        stage[start : start + SWEEPS, 0:cols] = block[base : base + SWEEPS, :]
        stage[start : start + SWEEPS, cols:width] = block[base + 8 : base + 8 + SWEEPS, 0:LANES]
    for i in range(rows):
        work[SWEEPS + i] = state[i]

    centre = stage[...]
    east_face = jnp.sqrt(centre * pltpu.roll(centre, width - 1, 1))
    north_face = jnp.sqrt(centre * pltpu.roll(centre, centre.shape[0] - 1, 0))
    for y in range(depth):
        east[y] = jnp.broadcast_to(east_face[y : y + 1], (8, width))
        north[y] = jnp.broadcast_to(north_face[y : y + 1], (8, width))

    def load(y):
        return [work[y, 8 * g : 8 * (g + 1), :] for g in range(groups)]

    for t in range(1, SWEEPS + 1):
        below, current = load(t - 1), load(t)
        flux = [north[t - 1] * (c - b) for b, c in zip(below, current)]

        def step(y, carry):
            now, flux_in = carry
            above = load(y + 1)
            e, n = east[y], north[y]
            flux_out = []
            for g in range(groups):
                s = now[g]
                along = e * (pltpu.roll(s, width - 1, 1) - s)
                across = n * (above[g] - s)
                flux_out.append(across)
                work[y, 8 * g : 8 * (g + 1), :] = s + ((along - pltpu.roll(along, 1, 1)) + (across - flux_in[g]))
            return above, flux_out

        lax.fori_loop(t, depth - t, step, (current, flux))

    for i in range(rows):
        result = work[SWEEPS + i, :, 0:cols] * spread[i]
        for part in range(cols // LANES):
            first = (i // 8) * 8 * (cols // LANES) + part * 8 + i % 8
            out[pl.ds(first, channels, stride=rows * cols // LANES), :] = result[:, part * LANES : (part + 1) * LANES]


def per_device(
    obs_innovation,
    obs_precision,
    obs_offsets,
    obs_cell,
    obs_counts,
    land_sea,
    diffusivity,
    background_std,
):
    dests, slots = obs_innovation.shape[2:]
    channels, rows, cols = background_std.shape
    width = cols + LANES
    count_rows, count_cols = lax.axis_size("row"), lax.axis_size("col")
    records = dests * slots

    by_slot = lambda x: x.reshape(dests, slots).T
    offsets = obs_offsets.reshape(dests, 2, slots).transpose(1, 2, 0)
    packed = kernel_call(
        pack_body,
        "pack_records",
        f32(dests, 1, 3 * LANES),
        (by_slot(obs_innovation), by_slot(obs_precision), offsets, by_slot(obs_cell), obs_counts.reshape(1, dests)),
        [pltpu.VMEM((LANES, LANES), jnp.float32)] * 2,
        moved=200_000,
    )
    arrived = lax.all_to_all(packed, "col", split_axis=0, concat_axis=0, tiled=True)

    spread, coef, first, last = kernel_call(
        fixed_body,
        "fixed_fields",
        (f32(rows, channels, cols), f32(rows, cols), f32(channels + 8, LANES), f32(channels + 8, LANES)),
        (background_std, land_sea, diffusivity),
        [pltpu.VMEM((cols // LANES, channels * rows, LANES), jnp.float32)],
        moved=2_000_000,
    )
    to_east = [(i, (i + 1) % count_cols) for i in range(count_cols)]
    to_west = [(j, i) for i, j in to_east]
    rim_left = lax.ppermute(last, "col", to_east)
    rim_right = lax.ppermute(first, "col", to_west)

    slab = SWEEPS * channels + channels // 2 + 16
    blocks = records // LANES
    bf16 = lambda *shape: pltpu.VMEM(shape, jnp.bfloat16)
    state, coef_wide, to_up, to_down = kernel_call(
        build_body,
        "build_state",
        (f32(rows, channels, width), f32(rows, width), f32(slab, cols), f32(slab, cols)),
        (arrived, spread, coef, rim_left, rim_right),
        [pltpu.VMEM((3, 4, blocks, LANES), jnp.float32)]
        + [bf16(rows * channels, records)] * 2
        + [bf16(cols, records)] * 2
        + [bf16(2, channels, records)] * 2
        + [bf16(2, rows * RIM, records)] * 2,
        moved=10_000_000,
    )
    up = [(i, i + 1) for i in range(count_rows - 1)]
    down = [(j, i) for i, j in up]
    from_down = lax.ppermute(to_up, "row", up)
    from_up = lax.ppermute(to_down, "row", down)

    depth = rows + 2 * SWEEPS
    out = kernel_call(
        sweep_body,
        "sweeps",
        f32(channels * rows * cols // LANES, LANES),
        (state, coef_wide, spread, from_down, from_up),
        [
            pltpu.VMEM((depth, channels, width), jnp.float32),
            pltpu.VMEM((depth, 8, width), jnp.float32),
            pltpu.VMEM((depth, 8, width), jnp.float32),
            pltpu.VMEM(((depth + 7) // 8 * 8, width), jnp.float32),
        ],
        moved=10_000_000,
    )
    out = out.reshape(channels, rows // 8, cols // LANES, 8, LANES)
    return out.transpose(0, 1, 3, 2, 4).reshape(channels, rows, cols)


def solution(mesh):
    placed = (
        P("row", "col", None, None),
        P("row", "col", None, None),
        P("row", "col", None, None, None),
        P("row", "col", None, None),
        P("row", "col", None),
        P("row", "col"),
        P("row", "col"),
        P(None, "row", "col"),
    )
    return jax.shard_map(
        per_device, mesh=mesh, in_specs=placed, out_specs=P(None, "row", "col"), check_vma=False
    )
```

time: 252 us -> 69.4 us (0.28)
  the two profiles are of different devices: /device:TPU:64 before, /device:TPU:223 now
where the time goes in v1:
time: 69.4 us; the launch traced here: 68.8 us
  Pallas kernels  28.2 us (41%)
  starting transfers between devices  24.4 us (35%)
  waiting for transfers between devices  12.5 us (18%)
  local copies, waits for them, and re-layouts  3.62 us (5%)
    pallas_call x4, Pallas kernels, kernel_call(): pl.pallas_call(body, name=name, out_shape=outs, in_specs=[WHOLE] * len(in...  28.2 us
    all_to_all x1, starting transfers between devices, per_device(): lax.all_to_all(packed, 'col', split_axis=0, concat_axis=0, tiled=True)  10.8 us
    ppermute x1, waiting for transfers between devices, per_device(): rim_right = lax.ppermute(first, 'col', to_west)  6.48 us
    ppermute x1, starting transfers between devices, per_device(): from_down = lax.ppermute(to_up, 'row', up)  5.21 us
    ppermute x1, waiting for transfers between devices, per_device(): from_up = lax.ppermute(to_down, 'row', down)  5.03 us
    ppermute x1, starting transfers between devices, per_device(): rim_left = lax.ppermute(last, 'col', to_east)  4.56 us
    unnamed x16, local copies, waits for them, and re-layouts  3.62 us
    ppermute x1, starting transfers between devices, per_device(): from_up = lax.ppermute(to_down, 'row', down)  1.92 us
  transfers between devices with their start and end apart: 5, of which 3 were waited for; matrix products, arithmetic and copies ran while one was open for 0% of the time, Pallas kernels for 0%

profile of v1, /device:TPU:223, one launch (start us, length us, event | category | flops | bytes accessed | tf_op | source)
XLA Modules:
  0.0 68.8 jit_solution(2131629441632014017)
XLA Ops:
  0.0 0.0 copy-start
  0.0 0.0 copy-start.1
  0.0 0.8 %copy-done.1 = f32[1,1,64,2,32]{2,4,3,1,0:T(8,128)S(1)} copy-done((f32[1,1,64,2,32]{2,4,3,1,0:T(8,128)S(1)}, f32[1,1,64,2,32]{2,4,3,1,0:T(8,128)}, u32[]{:S(2)}) %copy-start.1) | copy-done | bytes 16408
  0.8 0.0 copy-start.4
  0.8 0.7 %copy-done.4 = f32[1,1,64,32]{2,3,1,0:T(8,128)S(1)} copy-done((f32[1,1,64,32]{2,3,1,0:T(8,128)S(1)}, f32[1,1,64,32]{2,3,1,0:T(8,128)}, u32[]{:S(2)}) %copy-start.4) | copy-done | bytes 8216
  1.5 0.0 copy-start.5
  1.5 0.7 %copy-done.5 = f32[1,1,64,32]{2,3,1,0:T(8,128)S(1)} copy-done((f32[1,1,64,32]{2,3,1,0:T(8,128)S(1)}, f32[1,1,64,32]{2,3,1,0:T(8,128)}, u32[]{:S(2)}) %copy-start.5) | copy-done | bytes 8216
  2.2 0.0 copy-start.6
  2.2 0.7 %copy-done.6 = s32[1,1,64,32]{2,3,1,0:T(8,128)S(1)} copy-done((s32[1,1,64,32]{2,3,1,0:T(8,128)S(1)}, s32[1,1,64,32]{2,3,1,0:T(8,128)}, u32[]{:S(2)}) %copy-start.6) | copy-done | bytes 8216
  3.0 0.0 copy-start.7
  3.0 0.7 copy-done.7
  3.6 0.8 %pack_records.1 = f32[64,1,384]{2,1,0:T(1,128)} custom-call(f32[32,64]{1,0:T(8,128)S(1)} %bitcast.19, f32[32,64]{1,0:T(8,128)S(1)} %bitcast.20, f32[2,32,64]{2,1,0:T(8,128)S(1)} %bitcast.18, s32[32,64]{1,0:T(8,128)S(1)} %bitcast.21, s32[1,64]{1,0:T(1,128)S(1)} %bitcast.22), custom_call_target="tpu_custom_call" | custom-call | bytes 200000 | tf_op jit(solution)/shard_map/pack_records/pallas_call | solution.py:18
  4.4 0.0 copy-start.2
  4.4 0.0 copy-start.3
  4.4 10.8 %all-to-all-start = ((f32[64,1,384]{2,1,0:T(1,128)}), f32[64,1,384]{2,1,0:T(1,128)S(1)}, u32[]{:S(2)}, u32[]{:S(2)}) async-start(f32[64,1,384]{2,1,0:T(1,128)} %pack_records.1), calls=%async_computation | async-start | bytes 196608 | tf_op jit(solution)/shard_map/all_to_all | solution.py:283
  15.2 0.0 copy-done
  15.2 0.0 copy-done.2
  15.2 0.0 copy-done.3
  15.2 0.3 fixed_fields.1
  15.5 4.6 %collective-permute-start = (f32[40,128]{1,0:T(8,128)S(1)}, f32[40,128]{1,0:T(8,128)S(1)}, u32[]{:S(2)}, u32[]{:S(2)}) collective-permute-start(f32[40,128]{1,0:T(8,128)S(1)} %get-tuple-element.15), channel_id=1, source_target_pairs={{0,1},{1,2},{2,3},{3,4},{4,5},{5,6},{6,7},{7,8},{8,9},{9,10},{10,1... | collective-permute-start | bytes 61448 | tf_op jit(solution)/shard_map/ppermute | solution.py:295
  20.1 1.9 %collective-permute-start.1 = (f32[40,128]{1,0:T(8,128)S(1)}, f32[40,128]{1,0:T(8,128)S(1)}, u32[]{:S(2)}, u32[]{:S(2)}) collective-permute-start(f32[40,128]{1,0:T(8,128)S(1)} %get-tuple-element.16), channel_id=1, source_target_pairs={{1,0},{2,1},{3,2},{4,3},{5,4},{6,5},{7,6},{8,7},{9,8},{10,9},{11,1... | collective-permute-start | bytes 61448 | tf_op jit(solution)/shard_map/ppermute | solution.py:296
  22.0 0.0 collective-permute-done.rim_left
  22.0 6.5 %collective-permute-done.1.rim_right = f32[40,128]{1,0:T(8,128)S(1)} collective-permute-done((f32[40,128]{1,0:T(8,128)S(1)}, f32[40,128]{1,0:T(8,128)S(1)}, u32[]{:S(2)}, u32[]{:S(2)}) %collective-permute-start.1) | collective-permute-done | bytes 20512 | tf_op jit(solution)/shard_map/ppermute | solution.py:296
  28.5 0.0 all-to-all-done.arrived
  28.5 6.1 %build_state.1 = (f32[16,32,384]{2,1,0:T(8,128)S(1)}, f32[16,384]{1,0:T(8,128)S(1)}, f32[224,256]{1,0:T(8,128)S(1)}, f32[224,256]{1,0:T(8,128)S(1)}) custom-call(f32[64,1,384]{2,1,0:T(1,128)S(1)} %all-to-all-done.arrived, f32[16,32,256]{2,1,0:T(8,128)S(1)} %get-tuple-element.13.spread, f32[16,256]{1,0:T(8,128)S(1)} %get-tuple-element.14.coef, ...), custom_call_target="tpu_custom_call" | custom-call | bytes 10000000 | tf_op jit(solution)/shard_map/build_state/pallas_call | solution.py:18
  34.6 5.2 %collective-permute-start.2 = (f32[224,256]{1,0:T(8,128)S(1)}, f32[224,256]{1,0:T(8,128)S(1)}, u32[]{:S(2)}, u32[]{:S(2)}) collective-permute-start(f32[224,256]{1,0:T(8,128)S(1)} %get-tuple-element.19), channel_id=1, source_target_pairs={{0,64},{64,128},{128,192},{192,256},{256,320},{320,384},{384,448},... | collective-permute-start | bytes 688136 | tf_op jit(solution)/shard_map/ppermute | solution.py:315
  39.9 1.9 %collective-permute-start.3 = (f32[224,256]{1,0:T(8,128)S(1)}, f32[224,256]{1,0:T(8,128)S(1)}, u32[]{:S(2)}, u32[]{:S(2)}) collective-permute-start(f32[224,256]{1,0:T(8,128)S(1)} %get-tuple-element.20), channel_id=1, source_target_pairs={{64,0},{128,64},{192,128},{256,192},{320,256},{384,320},{448,384},... | collective-permute-start | bytes 688136 | tf_op jit(solution)/shard_map/ppermute | solution.py:316
  41.8 1.0 %collective-permute-done.2.from_down = f32[224,256]{1,0:T(8,128)S(1)} collective-permute-done((f32[224,256]{1,0:T(8,128)S(1)}, f32[224,256]{1,0:T(8,128)S(1)}, u32[]{:S(2)}, u32[]{:S(2)}) %collective-permute-start.2) | collective-permute-done | bytes 229408 | tf_op jit(solution)/shard_map/ppermute | solution.py:315
  42.8 5.0 %collective-permute-done.3.from_up = f32[224,256]{1,0:T(8,128)S(1)} collective-permute-done((f32[224,256]{1,0:T(8,128)S(1)}, f32[224,256]{1,0:T(8,128)S(1)}, u32[]{:S(2)}, u32[]{:S(2)}) %collective-permute-start.3) | collective-permute-done | bytes 229408 | tf_op jit(solution)/shard_map/ppermute | solution.py:316
  47.8 21.0 %sweeps.1 = f32[1024,128]{1,0:T(8,128)} custom-call(f32[16,32,384]{2,1,0:T(8,128)S(1)} %get-tuple-element.17.state, f32[16,384]{1,0:T(8,128)S(1)} %get-tuple-element.18.coef, f32[16,32,256]{2,1,0:T(8,128)S(1)} %get-tuple-element.13.spread, f32[224,256]{1,0:T(8,128)S(1)} %collective-permute-done.2.from_down, f32[224,256]{1,0:T(8,128)S(1)} %collective-permute-done.3.from_up), custom_call_target="tpu_custom_call" | custom-call | bytes 10000000 | tf_op jit(solution)/shard_map/sweeps/pallas_call | solution.py:18
Async XLA Ops:
  0.0 15.2 %copy-start = (bf16[32,16,256]{2,1,0:T(8,128)(2,1)S(1)}, bf16[32,16,256]{2,1,0:T(8,128)(2,1)}, u32[]{:S(2)}) copy-start(bf16[32,16,256]{2,1,0:T(8,128)(2,1)} %std.1) | copy-start | bytes 786436
  0.0 0.8 %copy-start.1 = (f32[1,1,64,2,32]{2,4,3,1,0:T(8,128)S(1)}, f32[1,1,64,2,32]{2,4,3,1,0:T(8,128)}, u32[]{:S(2)}) copy-start(f32[1,1,64,2,32]{2,4,3,1,0:T(8,128)} %param.10) | copy-start | bytes 49156
  0.8 0.7 %copy-start.4 = (f32[1,1,64,32]{2,3,1,0:T(8,128)S(1)}, f32[1,1,64,32]{2,3,1,0:T(8,128)}, u32[]{:S(2)}) copy-start(f32[1,1,64,32]{2,3,1,0:T(8,128)} %param.8) | copy-start | bytes 24580
  1.5 0.7 %copy-start.5 = (f32[1,1,64,32]{2,3,1,0:T(8,128)S(1)}, f32[1,1,64,32]{2,3,1,0:T(8,128)}, u32[]{:S(2)}) copy-start(f32[1,1,64,32]{2,3,1,0:T(8,128)} %param.9) | copy-start | bytes 24580
  2.2 0.7 %copy-start.6 = (s32[1,1,64,32]{2,3,1,0:T(8,128)S(1)}, s32[1,1,64,32]{2,3,1,0:T(8,128)}, u32[]{:S(2)}) copy-start(s32[1,1,64,32]{2,3,1,0:T(8,128)} %param.11) | copy-start | bytes 24580
  3.0 0.7 copy-start.7
  4.4 10.8 %copy-start.2 = (s32[16,256]{1,0:T(8,128)S(1)}, s32[16,256]{1,0:T(8,128)}, u32[]{:S(2)}) copy-start(s32[16,256]{1,0:T(8,128)} %sea.1) | copy-start | bytes 49156
  4.4 10.8 %copy-start.3 = (f32[16,256]{1,0:T(8,128)S(1)}, f32[16,256]{1,0:T(8,128)}, u32[]{:S(2)}) copy-start(f32[16,256]{1,0:T(8,128)} %diffusivity.1) | copy-start | bytes 49156
  4.4 24.1 %all-to-all-start = ((f32[64,1,384]{2,1,0:T(1,128)}), f32[64,1,384]{2,1,0:T(1,128)S(1)}, u32[]{:S(2)}, u32[]{:S(2)}) async-start(f32[64,1,384]{2,1,0:T(1,128)} %pack_records.1), calls=%async_computation | async-start | bytes 196608 | tf_op jit(solution)/shard_map/all_to_all | solution.py:283
  15.5 6.5 %collective-permute-start = (f32[40,128]{1,0:T(8,128)S(1)}, f32[40,128]{1,0:T(8,128)S(1)}, u32[]{:S(2)}, u32[]{:S(2)}) collective-permute-start(f32[40,128]{1,0:T(8,128)S(1)} %get-tuple-element.15), channel_id=1, source_target_pairs={{0,1},{1,2},{2,3},{3,4},{4,5},{5,6},{6,7},{7,8},{8,9},{9,10},{10,1... | collective-permute-start | bytes 61448 | tf_op jit(solution)/shard_map/ppermute | solution.py:295
  20.1 8.4 %collective-permute-start.1 = (f32[40,128]{1,0:T(8,128)S(1)}, f32[40,128]{1,0:T(8,128)S(1)}, u32[]{:S(2)}, u32[]{:S(2)}) collective-permute-start(f32[40,128]{1,0:T(8,128)S(1)} %get-tuple-element.16), channel_id=1, source_target_pairs={{1,0},{2,1},{3,2},{4,3},{5,4},{6,5},{7,6},{8,7},{9,8},{10,9},{11,1... | collective-permute-start | bytes 61448 | tf_op jit(solution)/shard_map/ppermute | solution.py:296
  34.6 8.2 %collective-permute-start.2 = (f32[224,256]{1,0:T(8,128)S(1)}, f32[224,256]{1,0:T(8,128)S(1)}, u32[]{:S(2)}, u32[]{:S(2)}) collective-permute-start(f32[224,256]{1,0:T(8,128)S(1)} %get-tuple-element.19), channel_id=1, source_target_pairs={{0,64},{64,128},{128,192},{192,256},{256,320},{320,384},{384,448},... | collective-permute-start | bytes 688136 | tf_op jit(solution)/shard_map/ppermute | solution.py:315
  39.9 8.0 %collective-permute-start.3 = (f32[224,256]{1,0:T(8,128)S(1)}, f32[224,256]{1,0:T(8,128)S(1)}, u32[]{:S(2)}, u32[]{:S(2)}) collective-permute-start(f32[224,256]{1,0:T(8,128)S(1)} %get-tuple-element.20), channel_id=1, source_target_pairs={{64,0},{128,64},{192,128},{256,192},{320,256},{384,320},{448,384},... | collective-permute-start | bytes 688136 | tf_op jit(solution)/shard_map/ppermute | solution.py:316

commit v2 on v1

v2 whole, which is shorter than its diff:
```python
import jax
import jax.numpy as jnp
from jax import lax
from jax.experimental import pallas as pl
from jax.experimental.pallas import tpu as pltpu
from jax.sharding import PartitionSpec as P

SWEEPS = 6
LANES = 128
CHUNKS = 4
RIM = 8
VMEM_BYTES = 24 * 1024 * 1024
ALL_VMEM_BYTES = 58 * 1024 * 1024

WHOLE = pl.BlockSpec(memory_space=pltpu.VMEM)
NT = (((1,), (1,)), ((), ()))


def kernel_call(body, name, outs, inputs, scratch=(), moved=0, place=pltpu.VMEM, grant=VMEM_BYTES):
    return pl.pallas_call(
        body,
        name=name,
        out_shape=outs,
        in_specs=[pl.BlockSpec(memory_space=place)] * len(inputs),
        out_specs=jax.tree.map(lambda _: WHOLE, outs),
        scratch_shapes=list(scratch),
        compiler_params=pltpu.CompilerParams(vmem_limit_bytes=grant),
        cost_estimate=pl.CostEstimate(flops=0, bytes_accessed=moved, transcendentals=0),
    )(*inputs)


def f32(*shape):
    return jax.ShapeDtypeStruct(shape, jnp.float32)


def pack_body(innovation_in, precision_in, offsets_in, cells_in, counts_in, out, innovation, precision, offsets, cells, counts, tile, rows, arrived):
    pairs = (
        (counts_in, counts),
        (innovation_in, innovation),
        (precision_in, precision),
        (offsets_in, offsets),
        (cells_in, cells),
    )
    copies = [pltpu.make_async_copy(source, held, arrived.at[k]) for k, (source, held) in enumerate(pairs)]
    for copy in copies:
        copy.start()
    for copy in copies:
        copy.wait()
    slots, dests = innovation.shape
    live = lax.broadcasted_iota(jnp.int32, (slots, dests), 0) < counts[...]
    tile[0:slots, 0:dests] = jnp.where(live, innovation[...] * precision[...], 0.0)
    tile[slots : 2 * slots, 0:dests] = offsets[0]
    tile[2 * slots : 3 * slots, 0:dests] = offsets[1]
    tile[3 * slots : 4 * slots, 0:dests] = cells[...].astype(jnp.float32)
    rows[...] = tile[...].T
    for d in range(dests):
        for k in range(3):
            out[d, :, k * LANES : (k + 1) * LANES] = rows[pl.ds((d + k - 1) % dests, 1), :]


def fixed_body(std, sea, diffusivity, spread, coef, first, last, stage):
    channels, rows, cols = std.shape
    mask = sea[...].astype(jnp.float32)
    product = std[...].astype(jnp.float32) * mask[None]
    for part in range(cols // LANES):
        stage[part] = product[:, :, part * LANES : (part + 1) * LANES].reshape(channels * rows, LANES)
    coef[...] = diffusivity[...] * mask
    lane = lax.broadcasted_iota(jnp.int32, (channels, LANES), 1)
    ends = [jnp.zeros((channels, LANES), jnp.float32)] * 2
    for i in range(rows):
        here = [stage[part, pl.ds(i, channels, stride=rows), :] for part in range(cols // LANES)]
        for part, values in enumerate(here):
            spread[i, :, part * LANES : (part + 1) * LANES] = values
        inside = (lane >= RIM * i) & (lane < RIM * (i + 1))
        ends[0] = jnp.where(inside, pltpu.roll(here[0], (RIM * i) % LANES, 1), ends[0])
        ends[1] = jnp.where(inside, pltpu.roll(here[-1], (RIM * i + RIM) % LANES, 1), ends[1])
    lane_row = lax.broadcasted_iota(jnp.int32, (1, LANES), 1)
    for which, rim in enumerate((first, last)):
        edge = coef[:, 0:LANES] if which == 0 else coef[:, cols - LANES : cols]
        packed = jnp.zeros((1, LANES), jnp.float32)
        for i in range(rows):
            inside = (lane_row >= RIM * i) & (lane_row < RIM * (i + 1))
            turned = pltpu.roll(edge[i : i + 1], (RIM * i + RIM * which) % LANES, 1)
            packed = jnp.where(inside, turned, packed)
        rim[0:channels] = ends[which]
        rim[channels : channels + 8] = jnp.broadcast_to(packed, (8, LANES))


def record_fields(block, slots):
    quarter = block.shape[0] // 4
    lane = lax.broadcasted_iota(jnp.int32, (quarter, LANES), 1)
    fields = []
    for f in range(4):
        joined = None
        for b in range(4):
            part = block[b * quarter : (b + 1) * quarter]
            turn = (slots * (b - f)) % LANES
            if turn:
                part = pltpu.roll(part, turn, 1)
            joined = part if b == 0 else jnp.where(lane >= slots * b, part, joined)
        fields.append(joined)
    return fields


def build_body(arrived, spread, state, sides, whole, real, total, *held):
    rows, channels, cols = spread.shape
    slots = LANES // 4
    blocks = whole.shape[2]
    chunks = len(held) // 7
    a_high, a_low, b_high, b_low, c_both, d_high, d_low = [held[q * chunks : (q + 1) * chunks] for q in range(7)]

    for k in range(3):
        weight, east, north, cell = record_fields(arrived[:, 0, k * LANES : (k + 1) * LANES], slots)
        cell = cell.astype(jnp.int32)
        for f, values in enumerate((cell >> 12, (cell >> 8) & 15, cell & 255)):
            whole[k, f] = values
        if k == 1:
            parts = (weight * (1.0 - north), weight * north, 1.0 - east, east)
        else:
            parts = (1.0 - north, north, 1.0 - east, east, weight)
        for f, values in enumerate(parts):
            high = values.astype(jnp.bfloat16).astype(jnp.float32)
            if k == 1 or f == 4:
                real[k, 2 * f] = high
                real[k, 2 * f + 1] = values - high
            else:
                real[k, 2 * f] = values

    def pick(away, at, after):
        return jnp.where(away == 0, at, jnp.where(away == 1, after, 0.0))

    def block(n, c, here):
        row_of = lambda k, f: real[k, f, n : n + 1, :]
        index = lambda k, f, size: lax.broadcasted_iota(jnp.int32, (size, LANES), 0) - whole[k, f, n : n + 1, :]

        hot = jnp.where(index(1, 0, channels) == 0, 1.0, 0.0).astype(jnp.bfloat16)
        away = index(1, 1, rows)
        high, low = pick(away, row_of(1, 0), row_of(1, 2)), pick(away, row_of(1, 1), row_of(1, 3))
        wide = lambda x: jnp.broadcast_to(x, (channels, LANES)).astype(jnp.bfloat16)
        for row in range(rows):
            at = slice(row * channels, (row + 1) * channels)
            a_high[c][at, here] = hot * wide(high[row : row + 1])
            a_low[c][at, here] = hot * wide(low[row : row + 1])
        away = index(1, 2, cols)
        b_high[c][:, here] = pick(away, row_of(1, 4), row_of(1, 6)).astype(jnp.bfloat16)
        b_low[c][:, here] = pick(away, row_of(1, 5), row_of(1, 7)).astype(jnp.bfloat16)

        for side, (k, base) in enumerate(((0, cols - RIM), (2, 0))):
            hot = index(k, 0, channels) == 0
            for part in range(2):
                at = slice(part * channels, (part + 1) * channels)
                c_both[c][side, at, here] = jnp.where(hot, row_of(k, 8 + part), 0.0).astype(jnp.bfloat16)
            by_row = pick(index(k, 1, rows), row_of(k, 0), row_of(k, 2))
            by_col = pick(index(k, 2, RIM) + base, row_of(k, 4), row_of(k, 6))
            both = (by_row[:, None, :] * by_col[None, :, :]).reshape(rows * RIM, LANES)
            high = both.astype(jnp.bfloat16)
            d_high[c][side, :, here] = high
            d_low[c][side, :, here] = (both - high.astype(jnp.float32)).astype(jnp.bfloat16)

    dot = lambda x, y: lax.dot_general(x, y, NT, preferred_element_type=jnp.float32)
    per = blocks // chunks
    rim = [0.0, 0.0]
    for c in range(chunks):
        for n in range(per):
            block(c * per + n, c, slice(n * LANES, (n + 1) * LANES))
        first, second = b_high[c][...], b_low[c][...]
        part = dot(a_high[c][...], first) + (dot(a_high[c][...], second) + dot(a_low[c][...], first))
        total[...] = part if c == 0 else total[...] + part
        for side in range(2):
            first = dot(c_both[c][side], d_high[c][side])
            second = dot(c_both[c][side, 0:channels], d_low[c][side])
            rim[side] = rim[side] + (first[0:channels] + (first[channels:] + second))
    for side in range(2):
        sides[side] = rim[side]
    for i in range(rows):
        state[i] = total[i * channels : (i + 1) * channels, :] * spread[i]


def rim_body(state, sides, coef, rim_left, rim_right, tails, coef_out, to_up, to_down):
    rows, channels, cols = state.shape
    lane = lax.broadcasted_iota(jnp.int32, (channels, LANES), 1)
    lane_row = lax.broadcasted_iota(jnp.int32, (1, LANES), 1)

    def outer(left, right, i, lanes):
        left = pltpu.roll(left, (LANES - RIM - RIM * i) % LANES, 1)
        right = pltpu.roll(right, (LANES - RIM * i) % LANES, 1)
        return jnp.where(lanes < RIM, right, jnp.where(lanes >= LANES - RIM, left, 0.0))

    left = sides[0] * rim_left[0:channels]
    right = sides[1] * rim_right[0:channels]
    coef_out[:, 0:cols] = coef[...]
    for i in range(rows):
        tails[i] = outer(left, right, i, lane)
        coef_out[i : i + 1, cols : cols + LANES] = outer(
            rim_left[channels : channels + 1], rim_right[channels : channels + 1], i, lane_row
        )

    for out, start in ((to_down, 0), (to_up, rows - SWEEPS)):
        packed = jnp.zeros((channels, LANES), jnp.float32)
        for q in range(SWEEPS):
            i = start + q
            out[q * channels : (q + 1) * channels, :] = state[i]
            inside = (lane >= 2 * RIM * q) & (lane < 2 * RIM * (q + 1))
            packed = jnp.where(inside, pltpu.roll(tails[i], (2 * RIM * q + RIM) % LANES, 1), packed)
        base = SWEEPS * channels
        half = channels // 2
        out[base : base + half, 0:LANES] = packed[0:half]
        out[base : base + half, LANES : 2 * LANES] = packed[half:channels]
        base = base + half
        out[base : base + 8, :] = jnp.zeros((8, cols), jnp.float32)
        out[base : base + SWEEPS, :] = coef_out[start : start + SWEEPS, 0:cols]
        out[base + 8 : base + 16, :] = jnp.zeros((8, cols), jnp.float32)
        out[base + 8 : base + 8 + SWEEPS, 0:LANES] = coef_out[start : start + SWEEPS, cols : cols + LANES]


def set_faces(faces, field):
    rows, width = field.shape
    east = jnp.sqrt(field * pltpu.roll(field, width - 1, 1))
    north = jnp.sqrt(field * pltpu.roll(field, rows - 1, 0))
    west = pltpu.roll(east, 1, 1)
    south = pltpu.roll(north, 1, 0)
    faces[0, 0:rows] = 1.0 - ((east + west) + (north + south))
    for k, values in enumerate((east, west, north, south)):
        faces[1 + k, 0:rows] = values


def turns(load, count, width):
    return [[(pltpu.roll(load(r, g), width - 1, 1), pltpu.roll(load(r, g), 1, 1)) for r in range(count)] for g in range(4)]


def swept(load, turned, faces, first, store):
    width = faces.shape[2]
    for r in range(len(turned[0])):
        c, e, w, n, s = [jnp.broadcast_to(faces[k, pl.ds(first + r, 1), :], (8, width)) for k in range(5)]
        for g in range(len(turned)):
            east, west = turned[g][r]
            store(r, g, (c * load(r, g) + (e * east + w * west)) + (n * load(r + 1, g) + s * load(r - 1, g)))


def inner_body(state, tails, coef, edge_low, edge_high, middle, work, faces):
    rows, channels, cols = state.shape
    width = cols + LANES
    step = 4
    part = lambda g: slice(8 * g, 8 * (g + 1))

    set_faces(faces, coef[...])

    def fill(i, carry):
        work[0, i, :, 0:cols] = state[i]
        work[0, i, :, cols:width] = tails[i]
        return carry

    lax.fori_loop(0, rows, fill, 0)

    def sweep(t, carry):
        now, then = lax.rem(t, 2), lax.rem(t + 1, 2)
        for k in range(2):
            edge_low[t, k] = work[now, t + k]
            edge_high[t, k] = work[now, rows - 2 - t + k]

        def chunk(k, inside):
            row = t + 1 + step * k

            def store(r, g, values):
                work[then, row + r, part(g), :] = values

            load = lambda r, g: work[now, row + r, part(g), :]
            swept(load, turns(load, step, width), faces, row, store)
            return inside

        lax.fori_loop(0, lax.div(rows - 2 * (t + 1) + step - 1, step), chunk, 0)
        return carry

    lax.fori_loop(0, SWEEPS, sweep, 0)
    for k in range(rows - 2 * SWEEPS):
        middle[k] = work[SWEEPS % 2, SWEEPS + k]


def outer_body(edge_low, edge_high, middle, coef, spread, from_down, from_up, out, work_low, work_high, faces, stage):
    rows, channels, cols = spread.shape
    width = cols + LANES
    half = channels // 2
    lane = lax.broadcasted_iota(jnp.int32, (channels, LANES), 1)
    part = lambda g: slice(8 * g, 8 * (g + 1))

    stage[...] = jnp.zeros_like(stage)
    stage[SWEEPS : SWEEPS + rows, :] = coef[...]
    for block, work, start in ((from_down, work_low, 0), (from_up, work_high, SWEEPS + rows)):
        base = SWEEPS * channels
        packed = jnp.concatenate([block[base : base + half, 0:LANES], block[base : base + half, LANES : 2 * LANES]], axis=0)
        for q in range(SWEEPS):
            work[0, q, :, 0:cols] = block[q * channels : (q + 1) * channels, :]
            tail = pltpu.roll(packed, (LANES - 2 * RIM * q - RIM) % LANES, 1)
            work[0, q, :, cols:width] = jnp.where((lane < RIM) | (lane >= LANES - RIM), tail, 0.0)
        base = base + half
        stage[start : start + SWEEPS, 0:cols] = block[base : base + SWEEPS, :]
        stage[start : start + SWEEPS, cols:width] = block[base + 8 : base + 8 + SWEEPS, 0:LANES]
    set_faces(faces, stage[...])

    def sweep(t, carry):
        now, then = lax.rem(t, 2), lax.rem(t + 1, 2)

        def load_low(r, g):
            j = r + 1
            return work_low[now, j, part(g), :] if j < SWEEPS else edge_low[t, j - SWEEPS, part(g), :]

        def load_high(r, g):
            j = r + 1
            return work_high[now, j - 2, part(g), :] if j >= 2 else edge_high[t, j, part(g), :]

        def store_low(r, g, values):
            work_low[then, r, part(g), :] = values

        def store_high(r, g, values):
            work_high[then, r, part(g), :] = values

        low, high = turns(load_low, SWEEPS, width), turns(load_high, SWEEPS, width)
        swept(load_low, low, faces, t + 1, store_low)
        swept(load_high, high, faces, SWEEPS + rows - 1 - t, store_high)
        return carry

    lax.fori_loop(0, SWEEPS, sweep, 0)

    last = SWEEPS % 2
    for i in range(rows):
        if i < SWEEPS:
            done = work_low[last, i, :, 0:cols]
        elif i < rows - SWEEPS:
            done = middle[i - SWEEPS, :, 0:cols]
        else:
            done = work_high[last, i - (rows - SWEEPS), :, 0:cols]
        result = done * spread[i]
        for block in range(cols // LANES):
            first = (i // 8) * 8 * (cols // LANES) + block * 8 + i % 8
            out[pl.ds(first, channels, stride=rows * cols // LANES), :] = result[:, block * LANES : (block + 1) * LANES]


def per_device(
    obs_innovation,
    obs_precision,
    obs_offsets,
    obs_cell,
    obs_counts,
    land_sea,
    diffusivity,
    background_std,
):
    dests, slots = obs_innovation.shape[2:]
    channels, rows, cols = background_std.shape
    width = cols + LANES
    count_rows, count_cols = lax.axis_size("row"), lax.axis_size("col")
    records = dests * slots

    by_slot = lambda x: x.reshape(dests, slots).T
    offsets = obs_offsets.reshape(dests, 2, slots).transpose(1, 2, 0)
    vmem = lambda *shape: pltpu.VMEM(shape, jnp.float32)
    bf16 = lambda *shape: pltpu.VMEM(shape, jnp.bfloat16)
    packed = kernel_call(
        pack_body,
        "pack_records",
        f32(dests, 1, 3 * LANES),
        (by_slot(obs_innovation), by_slot(obs_precision), offsets, by_slot(obs_cell), obs_counts.reshape(1, dests)),
        [
            vmem(slots, dests),
            vmem(slots, dests),
            vmem(2, slots, dests),
            pltpu.VMEM((slots, dests), jnp.int32),
            pltpu.VMEM((1, dests), jnp.int32),
            vmem(LANES, LANES),
            vmem(LANES, LANES),
            pltpu.SemaphoreType.DMA((5,)),
        ],
        moved=200_000,
        place=pltpu.HBM,
        grant=ALL_VMEM_BYTES,
    )
    arrived = lax.all_to_all(packed, "col", split_axis=0, concat_axis=0, tiled=True)

    spread, coef, first, last = kernel_call(
        fixed_body,
        "fixed_fields",
        (f32(rows, channels, cols), f32(rows, cols), f32(channels + 8, LANES), f32(channels + 8, LANES)),
        (background_std, land_sea, diffusivity),
        [vmem(cols // LANES, channels * rows, LANES)],
        moved=2_000_000,
    )
    to_east = [(i, (i + 1) % count_cols) for i in range(count_cols)]
    to_west = [(j, i) for i, j in to_east]
    rim_left = lax.ppermute(last, "col", to_east)
    rim_right = lax.ppermute(first, "col", to_west)

    blocks = records // LANES
    chunks = min(CHUNKS, blocks)
    piece = records // chunks
    state, sides = kernel_call(
        build_body,
        "build_state",
        (f32(rows, channels, cols), f32(2, channels, LANES)),
        (arrived, spread),
        [pltpu.VMEM((3, 3, blocks, LANES), jnp.int32), vmem(3, 10, blocks, LANES), vmem(rows * channels, cols)]
        + [bf16(rows * channels, piece)] * (2 * chunks)
        + [bf16(cols, piece)] * (2 * chunks)
        + [bf16(2, 2 * channels, piece)] * chunks
        + [bf16(2, rows * RIM, piece)] * (2 * chunks),
        moved=10_000_000,
    )
    slab = SWEEPS * channels + channels // 2 + 16
    tails, coef_wide, to_up, to_down = kernel_call(
        rim_body,
        "build_rims",
        (f32(rows, channels, LANES), f32(rows, width), f32(slab, cols), f32(slab, cols)),
        (state, sides, coef, rim_left, rim_right),
        moved=2_000_000,
    )
    up = [(i, i + 1) for i in range(count_rows - 1)]
    down = [(j, i) for i, j in up]
    from_down = lax.ppermute(to_up, "row", up)
    from_up = lax.ppermute(to_down, "row", down)

    edge_low, edge_high, middle = kernel_call(
        inner_body,
        "inner_sweeps",
        (
            f32(SWEEPS, 2, channels, width),
            f32(SWEEPS, 2, channels, width),
            f32(rows - 2 * SWEEPS, channels, width),
        ),
        (state, tails, coef_wide),
        [vmem(2, rows + 4, channels, width), vmem(5, rows + 4, width)],
        moved=6_000_000,
    )
    depth = (rows + 2 * SWEEPS + 7) // 8 * 8
    out = kernel_call(
        outer_body,
        "outer_sweeps",
        f32(channels * rows * cols // LANES, LANES),
        (edge_low, edge_high, middle, coef_wide, spread, from_down, from_up),
        [vmem(2, SWEEPS, channels, width)] * 2 + [vmem(5, depth, width), vmem(depth, width)],
        moved=10_000_000,
    )
    out = out.reshape(channels, rows // 8, cols // LANES, 8, LANES)
    return out.transpose(0, 1, 3, 2, 4).reshape(channels, rows, cols)


def solution(mesh):
    placed = (
        P("row", "col", None, None),
        P("row", "col", None, None),
        P("row", "col", None, None, None),
        P("row", "col", None, None),
        P("row", "col", None),
        P("row", "col"),
        P("row", "col"),
        P(None, "row", "col"),
    )
    return jax.shard_map(
        per_device, mesh=mesh, in_specs=placed, out_specs=P(None, "row", "col"), check_vma=False
    )
```

time: 69.4 us -> 46.7 us (0.67)
  the two profiles are of different devices: /device:TPU:223 before, /device:TPU:192 now
where the time goes in v2:
time: 46.7 us; the launch traced here: 46.4 us
  starting transfers between devices  26.9 us (58%)
  Pallas kernels  13 us (28%)
  waiting for transfers between devices  6.35 us (14%)
    pallas_call x6, Pallas kernels, kernel_call(): pl.pallas_call(body, name=name, out_shape=outs, in_specs=[pl.BlockSpec(me...  13 us
    all_to_all x1, starting transfers between devices, per_device(): lax.all_to_all(packed, 'col', split_axis=0, concat_axis=0, tiled=True)  10.6 us
    ppermute x1, starting transfers between devices, per_device(): rim_right = lax.ppermute(first, 'col', to_west)  6.92 us
    ppermute x1, starting transfers between devices, per_device(): from_down = lax.ppermute(to_up, 'row', up)  5.5 us
    ppermute x1, waiting for transfers between devices, per_device(): from_up = lax.ppermute(to_down, 'row', down)  5.08 us
    ppermute x1, starting transfers between devices, per_device(): rim_left = lax.ppermute(last, 'col', to_east)  1.96 us
    ppermute x1, starting transfers between devices, per_device(): from_up = lax.ppermute(to_down, 'row', down)  1.92 us
    all_to_all x1, waiting for transfers between devices, per_device(): lax.all_to_all(packed, 'col', split_axis=0, concat_axis=0, tiled=True)  1.26 us
  transfers between devices with their start and end apart: 5, of which 2 were waited for; matrix products, arithmetic and copies ran while one was open for 0% of the time, Pallas kernels for 15%

profile of v2, /device:TPU:192, one launch (start us, length us, event | category | flops | bytes accessed | tf_op | source)
XLA Modules:
  0.0 46.4 jit_solution(5232880696746653014)
XLA Ops:
  0.0 0.0 copy-start
  0.0 1.7 %pack_records.1 = f32[64,1,384]{2,1,0:T(1,128)} custom-call(f32[32,64]{1,0:T(8,128)} %bitcast.19, f32[32,64]{1,0:T(8,128)} %bitcast.20, f32[2,32,64]{2,1,0:T(8,128)} %bitcast.18, s32[32,64]{1,0:T(8,128)} %bitcast.21, s32[1,64]{1,0:T(1,128)} %bitcast.22), custom_call_target="tpu_custom_call" | custom-call | bytes 200000 | tf_op jit(solution)/shard_map/pack_records/pallas_call | solution.py:20
  1.7 0.0 copy-start.1
  1.7 0.0 copy-start.2
  1.7 10.6 %all-to-all-start = ((f32[64,1,384]{2,1,0:T(1,128)}), f32[64,1,384]{2,1,0:T(1,128)S(1)}, u32[]{:S(2)}, u32[]{:S(2)}) async-start(f32[64,1,384]{2,1,0:T(1,128)} %pack_records.1), calls=%async_computation | async-start | bytes 196608 | tf_op jit(solution)/shard_map/all_to_all | solution.py:377
  12.3 0.0 copy-done
  12.3 0.0 copy-done.1
  12.3 0.0 copy-done.2
  12.3 0.3 fixed_fields.1
  12.6 2.0 %collective-permute-start = (f32[40,128]{1,0:T(8,128)S(1)}, f32[40,128]{1,0:T(8,128)S(1)}, u32[]{:S(2)}, u32[]{:S(2)}) collective-permute-start(f32[40,128]{1,0:T(8,128)S(1)} %get-tuple-element.22), channel_id=1, source_target_pairs={{0,1},{1,2},{2,3},{3,4},{4,5},{5,6},{6,7},{7,8},{8,9},{9,10},{10,1... | collective-permute-start | bytes 61448 | tf_op jit(solution)/shard_map/ppermute | solution.py:389
  14.6 6.9 %collective-permute-start.1 = (f32[40,128]{1,0:T(8,128)S(1)}, f32[40,128]{1,0:T(8,128)S(1)}, u32[]{:S(2)}, u32[]{:S(2)}) collective-permute-start(f32[40,128]{1,0:T(8,128)S(1)} %get-tuple-element.23), channel_id=1, source_target_pairs={{1,0},{2,1},{3,2},{4,3},{5,4},{6,5},{7,6},{8,7},{9,8},{10,9},{11,1... | collective-permute-start | bytes 61448 | tf_op jit(solution)/shard_map/ppermute | solution.py:390
  21.5 1.3 %all-to-all-done.arrived = f32[64,1,384]{2,1,0:T(1,128)S(1)} async-done(((f32[64,1,384]{2,1,0:T(1,128)}), f32[64,1,384]{2,1,0:T(1,128)S(1)}, u32[]{:S(2)}, u32[]{:S(2)}) %all-to-all-start) | async-done | bytes 98336 | tf_op jit(solution)/shard_map/all_to_all | solution.py:377
  22.8 3.2 %build_state.1 = (f32[16,32,256]{2,1,0:T(8,128)S(1)}, f32[2,32,128]{2,1,0:T(8,128)S(1)}) custom-call(f32[64,1,384]{2,1,0:T(1,128)S(1)} %all-to-all-done.arrived, f32[16,32,256]{2,1,0:T(8,128)S(1)} %get-tuple-element.18.spread), custom_call_target="tpu_custom_call" | custom-call | bytes 10000000 | tf_op jit(solution)/shard_map/build_state/pallas_call | solution.py:20
  26.0 0.0 collective-permute-done.rim_left
  26.0 0.0 collective-permute-done.1.rim_right
  26.1 0.3 build_rims.1
  26.4 5.5 %collective-permute-start.2 = (f32[224,256]{1,0:T(8,128)S(1)}, f32[224,256]{1,0:T(8,128)S(1)}, u32[]{:S(2)}, u32[]{:S(2)}) collective-permute-start(f32[224,256]{1,0:T(8,128)S(1)} %get-tuple-element.29), channel_id=1, source_target_pairs={{0,64},{64,128},{128,192},{192,256},{256,320},{320,384},{384,448},... | collective-permute-start | bytes 688136 | tf_op jit(solution)/shard_map/ppermute | solution.py:417
  31.9 1.9 %collective-permute-start.3 = (f32[224,256]{1,0:T(8,128)S(1)}, f32[224,256]{1,0:T(8,128)S(1)}, u32[]{:S(2)}, u32[]{:S(2)}) collective-permute-start(f32[224,256]{1,0:T(8,128)S(1)} %get-tuple-element.30), channel_id=1, source_target_pairs={{64,0},{128,64},{192,128},{256,192},{320,256},{384,320},{448,384},... | collective-permute-start | bytes 688136 | tf_op jit(solution)/shard_map/ppermute | solution.py:418
  33.8 3.4 %inner_sweeps.1 = (f32[6,2,32,384]{3,2,1,0:T(8,128)S(1)}, f32[6,2,32,384]{3,2,1,0:T(8,128)S(1)}, f32[4,32,384]{2,1,0:T(8,128)S(1)}) custom-call(f32[16,32,256]{2,1,0:T(8,128)S(1)} %get-tuple-element.19.state, f32[16,32,128]{2,1,0:T(8,128)S(1)} %get-tuple-element.24.tails, f32[16,384]{1,0:T(8,128)S(1)} %get-tuple-element.25.coef), custom_call_target="tpu_custom_call" | custom-call | bytes 6000000 | tf_op jit(solution)/shard_map/inner_sweeps/pallas_call | solution.py:20
  37.2 0.0 collective-permute-done.2.from_down
  37.2 5.1 %collective-permute-done.3.from_up = f32[224,256]{1,0:T(8,128)S(1)} collective-permute-done((f32[224,256]{1,0:T(8,128)S(1)}, f32[224,256]{1,0:T(8,128)S(1)}, u32[]{:S(2)}, u32[]{:S(2)}) %collective-permute-start.3) | collective-permute-done | bytes 229408 | tf_op jit(solution)/shard_map/ppermute | solution.py:418
  42.3 4.1 %outer_sweeps.1 = f32[1024,128]{1,0:T(8,128)} custom-call(f32[6,2,32,384]{3,2,1,0:T(8,128)S(1)} %get-tuple-element.26.edge_low, f32[6,2,32,384]{3,2,1,0:T(8,128)S(1)} %get-tuple-element.27.edge_high, f32[4,32,384]{2,1,0:T(8,128)S(1)} %get-tuple-element.28.middle, f32[16,384]{1,0:T(8,128)S(1)} %get-tuple-element.25.coef, ...), custom_call_target="tpu_custom_call" | custom-call | bytes 10000000 | tf_op jit(solution)/shard_map/outer_sweeps/pallas_call | solution.py:20
Async XLA Ops:
  0.0 12.3 %copy-start = (bf16[32,16,256]{2,1,0:T(8,128)(2,1)S(1)}, bf16[32,16,256]{2,1,0:T(8,128)(2,1)}, u32[]{:S(2)}) copy-start(bf16[32,16,256]{2,1,0:T(8,128)(2,1)} %std.1) | copy-start | bytes 786436
  1.7 10.6 %copy-start.1 = (s32[16,256]{1,0:T(8,128)S(1)}, s32[16,256]{1,0:T(8,128)}, u32[]{:S(2)}) copy-start(s32[16,256]{1,0:T(8,128)} %sea.1) | copy-start | bytes 49156
  1.7 10.6 %copy-start.2 = (f32[16,256]{1,0:T(8,128)S(1)}, f32[16,256]{1,0:T(8,128)}, u32[]{:S(2)}) copy-start(f32[16,256]{1,0:T(8,128)} %diffusivity.1) | copy-start | bytes 49156
  1.7 21.1 %all-to-all-start = ((f32[64,1,384]{2,1,0:T(1,128)}), f32[64,1,384]{2,1,0:T(1,128)S(1)}, u32[]{:S(2)}, u32[]{:S(2)}) async-start(f32[64,1,384]{2,1,0:T(1,128)} %pack_records.1), calls=%async_computation | async-start | bytes 196608 | tf_op jit(solution)/shard_map/all_to_all | solution.py:377
  12.6 13.4 %collective-permute-start = (f32[40,128]{1,0:T(8,128)S(1)}, f32[40,128]{1,0:T(8,128)S(1)}, u32[]{:S(2)}, u32[]{:S(2)}) collective-permute-start(f32[40,128]{1,0:T(8,128)S(1)} %get-tuple-element.22), channel_id=1, source_target_pairs={{0,1},{1,2},{2,3},{3,4},{4,5},{5,6},{6,7},{7,8},{8,9},{9,10},{10,1... | collective-permute-start | bytes 61448 | tf_op jit(solution)/shard_map/ppermute | solution.py:389
  14.6 11.4 %collective-permute-start.1 = (f32[40,128]{1,0:T(8,128)S(1)}, f32[40,128]{1,0:T(8,128)S(1)}, u32[]{:S(2)}, u32[]{:S(2)}) collective-permute-start(f32[40,128]{1,0:T(8,128)S(1)} %get-tuple-element.23), channel_id=1, source_target_pairs={{1,0},{2,1},{3,2},{4,3},{5,4},{6,5},{7,6},{8,7},{9,8},{10,9},{11,1... | collective-permute-start | bytes 61448 | tf_op jit(solution)/shard_map/ppermute | solution.py:390
  26.4 10.9 %collective-permute-start.2 = (f32[224,256]{1,0:T(8,128)S(1)}, f32[224,256]{1,0:T(8,128)S(1)}, u32[]{:S(2)}, u32[]{:S(2)}) collective-permute-start(f32[224,256]{1,0:T(8,128)S(1)} %get-tuple-element.29), channel_id=1, source_target_pairs={{0,64},{64,128},{128,192},{192,256},{256,320},{320,384},{384,448},... | collective-permute-start | bytes 688136 | tf_op jit(solution)/shard_map/ppermute | solution.py:417
  31.9 10.4 %collective-permute-start.3 = (f32[224,256]{1,0:T(8,128)S(1)}, f32[224,256]{1,0:T(8,128)S(1)}, u32[]{:S(2)}, u32[]{:S(2)}) collective-permute-start(f32[224,256]{1,0:T(8,128)S(1)} %get-tuple-element.30), channel_id=1, source_target_pairs={{64,0},{128,64},{192,128},{256,192},{320,256},{384,320},{448,384},... | collective-permute-start | bytes 688136 | tf_op jit(solution)/shard_map/ppermute | solution.py:418

commit v3 on v2

--- a/solution.py
+++ b/solution.py
@@ -1,3 +1,5 @@
+import functools
+
 import jax
 import jax.numpy as jnp
 from jax import lax
@@ -12,18 +14,19 @@
 VMEM_BYTES = 24 * 1024 * 1024
 ALL_VMEM_BYTES = 58 * 1024 * 1024
 
-WHOLE = pl.BlockSpec(memory_space=pltpu.VMEM)
 NT = (((1,), (1,)), ((), ()))
 
 
-def kernel_call(body, name, outs, inputs, scratch=(), moved=0, place=pltpu.VMEM, grant=VMEM_BYTES):
+def kernel_call(body, name, outs, inputs, scratch=(), moved=0, place=pltpu.VMEM, grant=VMEM_BYTES, held=(), out_place=pltpu.VMEM):
+    specs = [pl.BlockSpec(memory_space=out_place if k in held else place) for k in range(len(inputs))]
     return pl.pallas_call(
         body,
         name=name,
         out_shape=outs,
-        in_specs=[pl.BlockSpec(memory_space=place)] * len(inputs),
-        out_specs=jax.tree.map(lambda _: WHOLE, outs),
+        in_specs=specs,
+        out_specs=jax.tree.map(lambda _: pl.BlockSpec(memory_space=out_place), outs),
         scratch_shapes=list(scratch),
+        input_output_aliases={k: 0 for k in held},
         compiler_params=pltpu.CompilerParams(vmem_limit_bytes=grant),
         cost_estimate=pl.CostEstimate(flops=0, bytes_accessed=moved, transcendentals=0),
     )(*inputs)
@@ -237,102 +240,104 @@
             store(r, g, (c * load(r, g) + (e * east + w * west)) + (n * load(r + 1, g) + s * load(r - 1, g)))
 
 
+def side_by_side(state, tails, i, g):
+    here = slice(8 * g, 8 * (g + 1))
+    return jnp.concatenate([state[i, here, :], tails[i, here, :]], axis=1)
+
+
 def inner_body(state, tails, coef, edge_low, edge_high, middle, work, faces):
     rows, channels, cols = state.shape
     width = cols + LANES
-    step = 4
     part = lambda g: slice(8 * g, 8 * (g + 1))
 
     set_faces(faces, coef[...])
-
-    def fill(i, carry):
-        work[0, i, :, 0:cols] = state[i]
-        work[0, i, :, cols:width] = tails[i]
-        return carry
-
-    lax.fori_loop(0, rows, fill, 0)
-
-    def sweep(t, carry):
-        now, then = lax.rem(t, 2), lax.rem(t + 1, 2)
+    for g in range(channels // 8):
         for k in range(2):
-            edge_low[t, k] = work[now, t + k]
-            edge_high[t, k] = work[now, rows - 2 - t + k]
-
-        def chunk(k, inside):
-            row = t + 1 + step * k
-
-            def store(r, g, values):
-                work[then, row + r, part(g), :] = values
-
-            load = lambda r, g: work[now, row + r, part(g), :]
-            swept(load, turns(load, step, width), faces, row, store)
-            return inside
-
-        lax.fori_loop(0, lax.div(rows - 2 * (t + 1) + step - 1, step), chunk, 0)
-        return carry
-
-    lax.fori_loop(0, SWEEPS, sweep, 0)
-    for k in range(rows - 2 * SWEEPS):
-        middle[k] = work[SWEEPS % 2, SWEEPS + k]
-
-
-def outer_body(edge_low, edge_high, middle, coef, spread, from_down, from_up, out, work_low, work_high, faces, stage):
+            edge_low[0, k, part(g), :] = side_by_side(state, tails, k, g)
+            edge_high[0, k, part(g), :] = side_by_side(state, tails, rows - 2 + k, g)
+
+    def loader(t):
+        if t == 0:
+            return lambda r, g: side_by_side(state, tails, 1 + r, g)
+        return lambda r, g: work[t % 2, t + 1 + r, part(g), :]
+
+    def storer(t):
+        def store(r, g, values):
+            done, row = t + 1, t + 1 + r
+            if done == SWEEPS:
+                middle[r, part(g), :] = values
+                return
+            work[done % 2, row, part(g), :] = values
+            if row < done + 2:
+                edge_low[done, row - done, part(g), :] = values
+            if row >= rows - 2 - done:
+                edge_high[done, row - (rows - 2 - done), part(g), :] = values
+
+        return store
+
+    for t in range(SWEEPS):
+        load, count = loader(t), rows - 2 * (t + 1)
+        swept(load, turns(load, count, width), faces, t + 1, storer(t))
+
+
+def side_body(low, edge, middle, coef, spread, block, *rest):
+    out, work, faces, stage, result, sent = rest[-6:]
     rows, channels, cols = spread.shape
     width = cols + LANES
     half = channels // 2
+    keep = rows - SWEEPS
     lane = lax.broadcasted_iota(jnp.int32, (channels, LANES), 1)
     part = lambda g: slice(8 * g, 8 * (g + 1))
 
-    stage[...] = jnp.zeros_like(stage)
-    stage[SWEEPS : SWEEPS + rows, :] = coef[...]
-    for block, work, start in ((from_down, work_low, 0), (from_up, work_high, SWEEPS + rows)):
-        base = SWEEPS * channels
-        packed = jnp.concatenate([block[base : base + half, 0:LANES], block[base : base + half, LANES : 2 * LANES]], axis=0)
-        for q in range(SWEEPS):
-            work[0, q, :, 0:cols] = block[q * channels : (q + 1) * channels, :]
-            tail = pltpu.roll(packed, (LANES - 2 * RIM * q - RIM) % LANES, 1)
-            work[0, q, :, cols:width] = jnp.where((lane < RIM) | (lane >= LANES - RIM), tail, 0.0)
-        base = base + half
-        stage[start : start + SWEEPS, 0:cols] = block[base : base + SWEEPS, :]
-        stage[start : start + SWEEPS, cols:width] = block[base + 8 : base + 8 + SWEEPS, 0:LANES]
+    base = SWEEPS * channels
+    packed = jnp.concatenate([block[base : base + half, 0:LANES], block[base : base + half, LANES : 2 * LANES]], axis=0)
+    for q in range(SWEEPS):
+        work[0, q, :, 0:cols] = block[q * channels : (q + 1) * channels, :]
+        tail = pltpu.roll(packed, (LANES - 2 * RIM * q - RIM) % LANES, 1)
+        work[0, q, :, cols:width] = jnp.where((lane < RIM) | (lane >= LANES - RIM), tail, 0.0)
+    base = base + half
+    start = 0 if low else keep
+    stage[start : start + SWEEPS, 0:cols] = block[base : base + SWEEPS, :]
+    stage[start : start + SWEEPS, cols:width] = block[base + 8 : base + 8 + SWEEPS, 0:LANES]
+    if low:
+        stage[SWEEPS:rows, :] = coef[0:keep, :]
+    else:
+        stage[0:keep, :] = coef[SWEEPS:rows, :]
     set_faces(faces, stage[...])
 
-    def sweep(t, carry):
-        now, then = lax.rem(t, 2), lax.rem(t + 1, 2)
-
-        def load_low(r, g):
-            j = r + 1
-            return work_low[now, j, part(g), :] if j < SWEEPS else edge_low[t, j - SWEEPS, part(g), :]
-
-        def load_high(r, g):
-            j = r + 1
-            return work_high[now, j - 2, part(g), :] if j >= 2 else edge_high[t, j, part(g), :]
-
-        def store_low(r, g, values):
-            work_low[then, r, part(g), :] = values
-
-        def store_high(r, g, values):
-            work_high[then, r, part(g), :] = values
-
-        low, high = turns(load_low, SWEEPS, width), turns(load_high, SWEEPS, width)
-        swept(load_low, low, faces, t + 1, store_low)
-        swept(load_high, high, faces, SWEEPS + rows - 1 - t, store_high)
-        return carry
-
-    lax.fori_loop(0, SWEEPS, sweep, 0)
-
-    last = SWEEPS % 2
-    for i in range(rows):
-        if i < SWEEPS:
-            done = work_low[last, i, :, 0:cols]
-        elif i < rows - SWEEPS:
+    def loader(t):
+        def load(r, g):
+            j = r + 1 if low else r - 1
+            if 0 <= j < SWEEPS:
+                return work[t % 2, j, part(g), :]
+            return edge[t, j - SWEEPS if low else r + 1, part(g), :]
+
+        return load
+
+    def storer(t):
+        def store(r, g, values):
+            work[(t + 1) % 2, r, part(g), :] = values
+
+        return store
+
+    for t in range(SWEEPS):
+        load = loader(t)
+        swept(load, turns(load, SWEEPS, width), faces, t + 1 if low else keep - 1 - t, storer(t))
+
+    for i in range(0 if low else rows // 2, rows // 2 if low else rows):
+        if SWEEPS <= i < keep:
             done = middle[i - SWEEPS, :, 0:cols]
         else:
-            done = work_high[last, i - (rows - SWEEPS), :, 0:cols]
-        result = done * spread[i]
-        for block in range(cols // LANES):
-            first = (i // 8) * 8 * (cols // LANES) + block * 8 + i % 8
-            out[pl.ds(first, channels, stride=rows * cols // LANES), :] = result[:, block * LANES : (block + 1) * LANES]
+            done = work[SWEEPS % 2, i if low else i - keep, :, 0:cols]
+        done = done * spread[i]
+        for k in range(cols // LANES):
+            first = k * 8 + i % 8
+            result[pl.ds(first, channels, stride=rows // 2 * cols // LANES), :] = done[:, k * LANES : (k + 1) * LANES]
+    size = rows // 2 * cols // LANES
+    target = out.at[:, 0:size, :] if low else out.at[:, size : 2 * size, :]
+    copy = pltpu.make_async_copy(result.reshape(channels, size, LANES), target, sent)
+    copy.start()
+    copy.wait()
 
 
 def per_device(
@@ -426,18 +431,28 @@
             f32(rows - 2 * SWEEPS, channels, width),
         ),
         (state, tails, coef_wide),
-        [vmem(2, rows + 4, channels, width), vmem(5, rows + 4, width)],
+        [vmem(2, rows, channels, width), vmem(5, rows, width)],
         moved=6_000_000,
     )
-    depth = (rows + 2 * SWEEPS + 7) // 8 * 8
-    out = kernel_call(
-        outer_body,
-        "outer_sweeps",
-        f32(channels * rows * cols // LANES, LANES),
-        (edge_low, edge_high, middle, coef_wide, spread, from_down, from_up),
-        [vmem(2, SWEEPS, channels, width)] * 2 + [vmem(5, depth, width), vmem(depth, width)],
-        moved=10_000_000,
-    )
+    size = rows * cols // LANES
+    out = None
+    for low, edge, block in ((True, edge_low, from_down), (False, edge_high, from_up)):
+        out = kernel_call(
+            functools.partial(side_body, low),
+            "low_sweeps" if low else "high_sweeps",
+            f32(channels, size, LANES),
+            (edge, middle, coef_wide, spread, block) + (() if low else (out,)),
+            [
+                vmem(2, SWEEPS, channels, width),
+                vmem(5, rows, width),
+                vmem(rows, width),
+                vmem(channels * size // 2, LANES),
+                pltpu.SemaphoreType.DMA,
+            ],
+            moved=5_000_000,
+            held=() if low else (5,),
+            out_place=pltpu.HBM,
+        )
     out = out.reshape(channels, rows // 8, cols // LANES, 8, LANES)
     return out.transpose(0, 1, 3, 2, 4).reshape(channels, rows, cols)
 

time: 46.7 us -> 44.5 us (0.953)
  Pallas kernels: 13 us -> 10.9 us
    pallas_call x6 -> x7, Pallas kernels: 13 us -> 10.9 us  [kernel_call(): pl.pallas_call(body, name=name, out_shape=outs, in_specs=specs, out_specs...]
    ppermute x1, waiting for transfers between devices: 5.08 us -> 3.44 us  [per_device(): from_up = lax.ppermute(to_down, 'row', down)]
    ppermute x1, waiting for transfers between devices: 0.01 us -> 1.56 us  [per_device(): from_down = lax.ppermute(to_up, 'row', up)]
  transfers between devices with their start and end apart: 5 -> 5, of which waited for: 2 -> 3; matrix products, arithmetic and copies ran while one was open for 0% -> 0% of each run, Pallas kernels for 15% -> 16%
where the time goes in v3:
time: 44.5 us; the launch traced here: 44.2 us
  starting transfers between devices  26.9 us (60%)
  Pallas kernels  10.9 us (24%)
  waiting for transfers between devices  6.27 us (14%)
    pallas_call x7, Pallas kernels, kernel_call(): pl.pallas_call(body, name=name, out_shape=outs, in_specs=specs, out_specs...  10.9 us
    all_to_all x1, starting transfers between devices, per_device(): lax.all_to_all(packed, 'col', split_axis=0, concat_axis=0, tiled=True)  10.6 us
    ppermute x1, starting transfers between devices, per_device(): rim_right = lax.ppermute(first, 'col', to_west)  6.92 us
    ppermute x1, starting transfers between devices, per_device(): from_down = lax.ppermute(to_up, 'row', up)  5.5 us
    ppermute x1, waiting for transfers between devices, per_device(): from_up = lax.ppermute(to_down, 'row', down)  3.44 us
    ppermute x1, starting transfers between devices, per_device(): rim_left = lax.ppermute(last, 'col', to_east)  1.96 us
    ppermute x1, starting transfers between devices, per_device(): from_up = lax.ppermute(to_down, 'row', down)  1.92 us
    ppermute x1, waiting for transfers between devices, per_device(): from_down = lax.ppermute(to_up, 'row', up)  1.56 us
  transfers between devices with their start and end apart: 5, of which 3 were waited for; matrix products, arithmetic and copies ran while one was open for 0% of the time, Pallas kernels for 16%

profile of v3, /device:TPU:192, one launch (start us, length us, event | category | flops | bytes accessed | tf_op | source)
XLA Modules:
  0.0 44.2 jit_solution(6065502075780869900)
XLA Ops:
  0.0 0.0 copy-start
  0.0 1.7 %pack_records.1 = f32[64,1,384]{2,1,0:T(1,128)} custom-call(f32[32,64]{1,0:T(8,128)} %bitcast.19, f32[32,64]{1,0:T(8,128)} %bitcast.20, f32[2,32,64]{2,1,0:T(8,128)} %bitcast.18, s32[32,64]{1,0:T(8,128)} %bitcast.21, s32[1,64]{1,0:T(1,128)} %bitcast.22), custom_call_target="tpu_custom_call" | custom-call | bytes 200000 | tf_op jit(solution)/shard_map/pack_records/pallas_call | solution.py:22
  1.7 0.0 copy-start.1
  1.7 0.0 copy-start.2
  1.7 10.6 %all-to-all-start = ((f32[64,1,384]{2,1,0:T(1,128)}), f32[64,1,384]{2,1,0:T(1,128)S(1)}, u32[]{:S(2)}, u32[]{:S(2)}) async-start(f32[64,1,384]{2,1,0:T(1,128)} %pack_records.1), calls=%async_computation | async-start | bytes 196608 | tf_op jit(solution)/shard_map/all_to_all | solution.py:382
  12.3 0.0 copy-done
  12.3 0.0 copy-done.1
  12.3 0.0 copy-done.2
  12.3 0.3 fixed_fields.1
  12.6 2.0 %collective-permute-start = (f32[40,128]{1,0:T(8,128)S(1)}, f32[40,128]{1,0:T(8,128)S(1)}, u32[]{:S(2)}, u32[]{:S(2)}) collective-permute-start(f32[40,128]{1,0:T(8,128)S(1)} %get-tuple-element.22), channel_id=1, source_target_pairs={{0,1},{1,2},{2,3},{3,4},{4,5},{5,6},{6,7},{7,8},{8,9},{9,10},{10,1... | collective-permute-start | bytes 61448 | tf_op jit(solution)/shard_map/ppermute | solution.py:394
  14.6 6.9 %collective-permute-start.1 = (f32[40,128]{1,0:T(8,128)S(1)}, f32[40,128]{1,0:T(8,128)S(1)}, u32[]{:S(2)}, u32[]{:S(2)}) collective-permute-start(f32[40,128]{1,0:T(8,128)S(1)} %get-tuple-element.23), channel_id=1, source_target_pairs={{1,0},{2,1},{3,2},{4,3},{5,4},{6,5},{7,6},{8,7},{9,8},{10,9},{11,1... | collective-permute-start | bytes 61448 | tf_op jit(solution)/shard_map/ppermute | solution.py:395
  21.5 1.3 %all-to-all-done.arrived = f32[64,1,384]{2,1,0:T(1,128)S(1)} async-done(((f32[64,1,384]{2,1,0:T(1,128)}), f32[64,1,384]{2,1,0:T(1,128)S(1)}, u32[]{:S(2)}, u32[]{:S(2)}) %all-to-all-start) | async-done | bytes 98336 | tf_op jit(solution)/shard_map/all_to_all | solution.py:382
  22.8 3.2 %build_state.1 = (f32[16,32,256]{2,1,0:T(8,128)S(1)}, f32[2,32,128]{2,1,0:T(8,128)S(1)}) custom-call(f32[64,1,384]{2,1,0:T(1,128)S(1)} %all-to-all-done.arrived, f32[16,32,256]{2,1,0:T(8,128)S(1)} %get-tuple-element.18.spread), custom_call_target="tpu_custom_call" | custom-call | bytes 10000000 | tf_op jit(solution)/shard_map/build_state/pallas_call | solution.py:22
  26.0 0.0 collective-permute-done.rim_left
  26.0 0.0 collective-permute-done.1.rim_right
  26.1 0.3 build_rims.1
  26.4 5.5 %collective-permute-start.3 = (f32[224,256]{1,0:T(8,128)S(1)}, f32[224,256]{1,0:T(8,128)S(1)}, u32[]{:S(2)}, u32[]{:S(2)}) collective-permute-start(f32[224,256]{1,0:T(8,128)S(1)} %get-tuple-element.30), channel_id=1, source_target_pairs={{0,64},{64,128},{128,192},{192,256},{256,320},{320,384},{384,448},... | collective-permute-start | bytes 688136 | tf_op jit(solution)/shard_map/ppermute | solution.py:422
  31.9 1.9 %collective-permute-start.2 = (f32[224,256]{1,0:T(8,128)S(1)}, f32[224,256]{1,0:T(8,128)S(1)}, u32[]{:S(2)}, u32[]{:S(2)}) collective-permute-start(f32[224,256]{1,0:T(8,128)S(1)} %get-tuple-element.28), channel_id=1, source_target_pairs={{64,0},{128,64},{192,128},{256,192},{320,256},{384,320},{448,384},... | collective-permute-start | bytes 688136 | tf_op jit(solution)/shard_map/ppermute | solution.py:423
  33.8 1.6 %inner_sweeps.1 = (f32[6,2,32,384]{3,2,1,0:T(8,128)S(1)}, f32[6,2,32,384]{3,2,1,0:T(8,128)S(1)}, f32[4,32,384]{2,1,0:T(8,128)S(1)}) custom-call(f32[16,32,256]{2,1,0:T(8,128)S(1)} %get-tuple-element.19.state, f32[16,32,128]{2,1,0:T(8,128)S(1)} %get-tuple-element.24.tails, f32[16,384]{1,0:T(8,128)S(1)} %get-tuple-element.25.coef), custom_call_target="tpu_custom_call" | custom-call | bytes 6000000 | tf_op jit(solution)/shard_map/inner_sweeps/pallas_call | solution.py:22
  35.4 1.6 %collective-permute-done.3.block = f32[224,256]{1,0:T(8,128)S(1)} collective-permute-done((f32[224,256]{1,0:T(8,128)S(1)}, f32[224,256]{1,0:T(8,128)S(1)}, u32[]{:S(2)}, u32[]{:S(2)}) %collective-permute-start.3) | collective-permute-done | bytes 229408 | tf_op jit(solution)/shard_map/ppermute | solution.py:422
  37.0 1.9 %low_sweeps.1.rest_0_ = f32[32,32,128]{2,1,0:T(8,128)} custom-call(f32[6,2,32,384]{3,2,1,0:T(8,128)S(1)} %get-tuple-element.29.edge, f32[4,32,384]{2,1,0:T(8,128)S(1)} %get-tuple-element.27.middle, f32[16,384]{1,0:T(8,128)S(1)} %get-tuple-element.25.coef, f32[16,32,256]{2,1,0:T(8,128)S(1)} %get-tuple-element.18.spread, ...), custom_call_target="tpu_custom_call" | custom-call | bytes 5000000 | tf_op jit(solution)/shard_map/low_sweeps/pallas_call | solution.py:22
  38.9 3.4 %collective-permute-done.2.block = f32[224,256]{1,0:T(8,128)S(1)} collective-permute-done((f32[224,256]{1,0:T(8,128)S(1)}, f32[224,256]{1,0:T(8,128)S(1)}, u32[]{:S(2)}, u32[]{:S(2)}) %collective-permute-start.2) | collective-permute-done | bytes 229408 | tf_op jit(solution)/shard_map/ppermute | solution.py:423
  42.3 1.9 %high_sweeps.1 = f32[32,32,128]{2,1,0:T(8,128)} custom-call(f32[6,2,32,384]{3,2,1,0:T(8,128)S(1)} %get-tuple-element.26.edge, f32[4,32,384]{2,1,0:T(8,128)S(1)} %get-tuple-element.27.middle, f32[16,384]{1,0:T(8,128)S(1)} %get-tuple-element.25.coef, f32[16,32,256]{2,1,0:T(8,128)S(1)} %get-tuple-element.18.spread, ...), custom_call_target="tpu_custom_call", output_to_operand_aliasing={{}: (5, {})} | custom-call | bytes 5000000 | tf_op jit(solution)/shard_map/high_sweeps/pallas_call | solution.py:22
Async XLA Ops:
  0.0 12.3 %copy-start = (bf16[32,16,256]{2,1,0:T(8,128)(2,1)S(1)}, bf16[32,16,256]{2,1,0:T(8,128)(2,1)}, u32[]{:S(2)}) copy-start(bf16[32,16,256]{2,1,0:T(8,128)(2,1)} %std.1) | copy-start | bytes 786436
  1.7 10.6 %copy-start.1 = (s32[16,256]{1,0:T(8,128)S(1)}, s32[16,256]{1,0:T(8,128)}, u32[]{:S(2)}) copy-start(s32[16,256]{1,0:T(8,128)} %sea.1) | copy-start | bytes 49156
  1.7 10.6 %copy-start.2 = (f32[16,256]{1,0:T(8,128)S(1)}, f32[16,256]{1,0:T(8,128)}, u32[]{:S(2)}) copy-start(f32[16,256]{1,0:T(8,128)} %diffusivity.1) | copy-start | bytes 49156
  1.7 21.1 %all-to-all-start = ((f32[64,1,384]{2,1,0:T(1,128)}), f32[64,1,384]{2,1,0:T(1,128)S(1)}, u32[]{:S(2)}, u32[]{:S(2)}) async-start(f32[64,1,384]{2,1,0:T(1,128)} %pack_records.1), calls=%async_computation | async-start | bytes 196608 | tf_op jit(solution)/shard_map/all_to_all | solution.py:382
  12.6 13.4 %collective-permute-start = (f32[40,128]{1,0:T(8,128)S(1)}, f32[40,128]{1,0:T(8,128)S(1)}, u32[]{:S(2)}, u32[]{:S(2)}) collective-permute-start(f32[40,128]{1,0:T(8,128)S(1)} %get-tuple-element.22), channel_id=1, source_target_pairs={{0,1},{1,2},{2,3},{3,4},{4,5},{5,6},{6,7},{7,8},{8,9},{9,10},{10,1... | collective-permute-start | bytes 61448 | tf_op jit(solution)/shard_map/ppermute | solution.py:394
  14.6 11.4 %collective-permute-start.1 = (f32[40,128]{1,0:T(8,128)S(1)}, f32[40,128]{1,0:T(8,128)S(1)}, u32[]{:S(2)}, u32[]{:S(2)}) collective-permute-start(f32[40,128]{1,0:T(8,128)S(1)} %get-tuple-element.23), channel_id=1, source_target_pairs={{1,0},{2,1},{3,2},{4,3},{5,4},{6,5},{7,6},{8,7},{9,8},{10,9},{11,1... | collective-permute-start | bytes 61448 | tf_op jit(solution)/shard_map/ppermute | solution.py:395
  26.4 10.6 %collective-permute-start.3 = (f32[224,256]{1,0:T(8,128)S(1)}, f32[224,256]{1,0:T(8,128)S(1)}, u32[]{:S(2)}, u32[]{:S(2)}) collective-permute-start(f32[224,256]{1,0:T(8,128)S(1)} %get-tuple-element.30), channel_id=1, source_target_pairs={{0,64},{64,128},{128,192},{192,256},{256,320},{320,384},{384,448},... | collective-permute-start | bytes 688136 | tf_op jit(solution)/shard_map/ppermute | solution.py:422
  31.9 10.4 %collective-permute-start.2 = (f32[224,256]{1,0:T(8,128)S(1)}, f32[224,256]{1,0:T(8,128)S(1)}, u32[]{:S(2)}, u32[]{:S(2)}) collective-permute-start(f32[224,256]{1,0:T(8,128)S(1)} %get-tuple-element.28), channel_id=1, source_target_pairs={{64,0},{128,64},{192,128},{256,192},{320,256},{384,320},{448,384},... | collective-permute-start | bytes 688136 | tf_op jit(solution)/shard_map/ppermute | solution.py:423

commit v4 on v3

--- a/solution.py
+++ b/solution.py
@@ -58,10 +58,14 @@
     rows[...] = tile[...].T
     for d in range(dests):
         for k in range(3):
-            out[d, :, k * LANES : (k + 1) * LANES] = rows[pl.ds((d + k - 1) % dests, 1), :]
-
-
-def fixed_body(std, sea, diffusivity, spread, coef, first, last, stage):
+            out[dests - 1 - d, :, k * LANES : (k + 1) * LANES] = rows[pl.ds((d + k - 1) % dests, 1), :]
+
+
+def odd_column():
+    return lax.rem(lax.axis_index("col"), 2) == 1
+
+
+def fixed_body(std, sea, diffusivity, spread, coef, near, far, stage):
     channels, rows, cols = std.shape
     mask = sea[...].astype(jnp.float32)
     product = std[...].astype(jnp.float32) * mask[None]
@@ -78,15 +82,17 @@
         ends[0] = jnp.where(inside, pltpu.roll(here[0], (RIM * i) % LANES, 1), ends[0])
         ends[1] = jnp.where(inside, pltpu.roll(here[-1], (RIM * i + RIM) % LANES, 1), ends[1])
     lane_row = lax.broadcasted_iota(jnp.int32, (1, LANES), 1)
-    for which, rim in enumerate((first, last)):
+    for which in range(2):
         edge = coef[:, 0:LANES] if which == 0 else coef[:, cols - LANES : cols]
         packed = jnp.zeros((1, LANES), jnp.float32)
         for i in range(rows):
             inside = (lane_row >= RIM * i) & (lane_row < RIM * (i + 1))
             turned = pltpu.roll(edge[i : i + 1], (RIM * i + RIM * which) % LANES, 1)
             packed = jnp.where(inside, turned, packed)
-        rim[0:channels] = ends[which]
-        rim[channels : channels + 8] = jnp.broadcast_to(packed, (8, LANES))
+        ends[which] = jnp.concatenate([ends[which], jnp.broadcast_to(packed, (8, LANES))], axis=0)
+    odd = odd_column()
+    near[...] = jnp.where(odd, ends[0], ends[1])
+    far[...] = jnp.where(odd, ends[1], ends[0])
 
 
 def record_fields(block, slots):
@@ -179,7 +185,7 @@
         state[i] = total[i * channels : (i + 1) * channels, :] * spread[i]
 
 
-def rim_body(state, sides, coef, rim_left, rim_right, tails, coef_out, to_up, to_down):
+def rim_body(state, sides, coef, near, far, tails, coef_out, to_up, to_down):
     rows, channels, cols = state.shape
     lane = lax.broadcasted_iota(jnp.int32, (channels, LANES), 1)
     lane_row = lax.broadcasted_iota(jnp.int32, (1, LANES), 1)
@@ -189,6 +195,9 @@
         right = pltpu.roll(right, (LANES - RIM * i) % LANES, 1)
         return jnp.where(lanes < RIM, right, jnp.where(lanes >= LANES - RIM, left, 0.0))
 
+    odd = odd_column()
+    rim_left = jnp.where(odd, near[...], far[...])
+    rim_right = jnp.where(odd, far[...], near[...])
     left = sides[0] * rim_left[0:channels]
     right = sides[1] * rim_right[0:channels]
     coef_out[:, 0:cols] = coef[...]
@@ -379,9 +388,9 @@
         place=pltpu.HBM,
         grant=ALL_VMEM_BYTES,
     )
-    arrived = lax.all_to_all(packed, "col", split_axis=0, concat_axis=0, tiled=True)
-
-    spread, coef, first, last = kernel_call(
+    arrived = lax.all_to_all(packed, "col", split_axis=0, concat_axis=0, tiled=True, axis_index_groups=[list(range(dests))[::-1]])
+
+    spread, coef, near, far = kernel_call(
         fixed_body,
         "fixed_fields",
         (f32(rows, channels, cols), f32(rows, cols), f32(channels + 8, LANES), f32(channels + 8, LANES)),
@@ -389,10 +398,8 @@
         [vmem(cols // LANES, channels * rows, LANES)],
         moved=2_000_000,
     )
-    to_east = [(i, (i + 1) % count_cols) for i in range(count_cols)]
-    to_west = [(j, i) for i, j in to_east]
-    rim_left = lax.ppermute(last, "col", to_east)
-    rim_right = lax.ppermute(first, "col", to_west)
+    near = lax.ppermute(near, "col", [(i, i ^ 1) for i in range(count_cols)])
+    far = lax.ppermute(far, "col", [(i, (((i + 1) ^ 1) - 1) % count_cols) for i in range(count_cols)])
 
     blocks = records // LANES
     chunks = min(CHUNKS, blocks)
@@ -414,7 +421,7 @@
         rim_body,
         "build_rims",
         (f32(rows, channels, LANES), f32(rows, width), f32(slab, cols), f32(slab, cols)),
-        (state, sides, coef, rim_left, rim_right),
+        (state, sides, coef, near, far),
         moved=2_000_000,
     )
     up = [(i, i + 1) for i in range(count_rows - 1)]

time: 44.5 us -> 41 us (0.921)
  starting transfers between devices: 26.9 us -> 22.7 us
  waiting for transfers between devices: 6.27 us -> 6.86 us
    ppermute x2, starting transfers between devices: 8.88 us -> 3.99 us  [the longest x1 2 us: per_device(): lax.ppermute(far, 'col', [(i, ((i + 1 ^ 1) - 1) % count_cols) for i in ra...]
    ppermute x1, waiting for transfers between devices: 1.56 us -> 0.21 us  [per_device(): from_down = lax.ppermute(to_up, 'row', up)]
    ppermute x2, waiting for transfers between devices: 0.01 us -> 1 us  [the longest x1 1 us: per_device(): lax.ppermute(far, 'col', [(i, ((i + 1 ^ 1) - 1) % count_cols) for i in ra...]
    all_to_all x1, waiting for transfers between devices: 1.26 us -> 2.17 us  [per_device(): lax.all_to_all(packed, 'col', split_axis=0, concat_axis=0, tiled=True, ax...]
    all_to_all x1, starting transfers between devices: 10.6 us -> 11.3 us  [per_device(): lax.all_to_all(packed, 'col', split_axis=0, concat_axis=0, tiled=True, ax...]
  transfers between devices with their start and end apart: 5 -> 5, of which waited for: 3 -> 4; matrix products, arithmetic and copies ran while one was open for 0% -> 0% of each run, Pallas kernels for 16% -> 17%
where the time goes in v4:
time: 41 us; the launch traced here: 40.6 us
  starting transfers between devices  22.7 us (55%)
  Pallas kernels  10.9 us (27%)
  waiting for transfers between devices  6.86 us (17%)
    all_to_all x1, starting transfers between devices, per_device(): lax.all_to_all(packed, 'col', split_axis=0, concat_axis=0, tiled=True, ax...  11.3 us
    pallas_call x7, Pallas kernels, kernel_call(): pl.pallas_call(body, name=name, out_shape=outs, in_specs=specs, out_specs...  10.9 us
    ppermute x1, starting transfers between devices, per_device(): from_down = lax.ppermute(to_up, 'row', up)  5.49 us
    ppermute x1, waiting for transfers between devices, per_device(): from_up = lax.ppermute(to_down, 'row', down)  3.48 us
    all_to_all x1, waiting for transfers between devices, per_device(): lax.all_to_all(packed, 'col', split_axis=0, concat_axis=0, tiled=True, ax...  2.17 us
    ppermute x1, starting transfers between devices, per_device(): lax.ppermute(far, 'col', [(i, ((i + 1 ^ 1) - 1) % count_cols) for i in ra...  2 us
    ppermute x1, starting transfers between devices, per_device(): near = lax.ppermute(near, 'col', [(i, i ^ 1) for i in range(count_cols)])  1.99 us
    ppermute x1, starting transfers between devices, per_device(): from_up = lax.ppermute(to_down, 'row', down)  1.92 us
  transfers between devices with their start and end apart: 5, of which 4 were waited for; matrix products, arithmetic and copies ran while one was open for 0% of the time, Pallas kernels for 17%

profile of v4, /device:TPU:192, one launch (start us, length us, event | category | flops | bytes accessed | tf_op | source)
XLA Modules:
  0.0 40.6 jit_solution(2834720655727363809)
XLA Ops:
  0.0 0.0 copy-start
  0.0 1.7 %pack_records.1 = f32[64,1,384]{2,1,0:T(1,128)} custom-call(f32[32,64]{1,0:T(8,128)} %bitcast.19, f32[32,64]{1,0:T(8,128)} %bitcast.20, f32[2,32,64]{2,1,0:T(8,128)} %bitcast.18, s32[32,64]{1,0:T(8,128)} %bitcast.21, s32[1,64]{1,0:T(1,128)} %bitcast.22), custom_call_target="tpu_custom_call" | custom-call | bytes 200000 | tf_op jit(solution)/shard_map/pack_records/pallas_call | solution.py:22
  1.7 0.0 copy-start.1
  1.7 0.0 copy-start.2
  1.7 11.3 %all-to-all-start = ((f32[64,1,384]{2,1,0:T(1,128)}), f32[64,1,384]{2,1,0:T(1,128)S(1)}, u32[]{:S(2)}, u32[]{:S(2)}) async-start(f32[64,1,384]{2,1,0:T(1,128)} %pack_records.1), calls=%async_computation | async-start | bytes 196608 | tf_op jit(solution)/shard_map/all_to_all | solution.py:391
  13.0 0.0 copy-done
  13.1 0.0 copy-done.1
  13.1 0.0 copy-done.2
  13.1 0.3 fixed_fields.1
  13.4 2.0 %collective-permute-start = (f32[40,128]{1,0:T(8,128)S(1)}, f32[40,128]{1,0:T(8,128)S(1)}, u32[]{:S(2)}, u32[]{:S(2)}) collective-permute-start(f32[40,128]{1,0:T(8,128)S(1)} %get-tuple-element.22), channel_id=1, source_target_pairs={{0,1},{1,0},{2,3},{3,2},{4,5},{5,4},{6,7},{7,6},{8,9},{9,8},{10,11... | collective-permute-start | bytes 61448 | tf_op jit(solution)/shard_map/ppermute | solution.py:401
  15.4 2.0 %collective-permute-start.1 = (f32[40,128]{1,0:T(8,128)S(1)}, f32[40,128]{1,0:T(8,128)S(1)}, u32[]{:S(2)}, u32[]{:S(2)}) collective-permute-start(f32[40,128]{1,0:T(8,128)S(1)} %get-tuple-element.23), channel_id=1, source_target_pairs={{0,63},{1,2},{2,1},{3,4},{4,3},{5,6},{6,5},{7,8},{8,7},{9,10},{10,... | collective-permute-start | bytes 61448 | tf_op jit(solution)/shard_map/ppermute | solution.py:402
  17.4 2.2 %all-to-all-done.arrived = f32[64,1,384]{2,1,0:T(1,128)S(1)} async-done(((f32[64,1,384]{2,1,0:T(1,128)}), f32[64,1,384]{2,1,0:T(1,128)S(1)}, u32[]{:S(2)}, u32[]{:S(2)}) %all-to-all-start) | async-done | bytes 98336 | tf_op jit(solution)/shard_map/all_to_all | solution.py:391
  19.6 3.2 %build_state.1 = (f32[16,32,256]{2,1,0:T(8,128)S(1)}, f32[2,32,128]{2,1,0:T(8,128)S(1)}) custom-call(f32[64,1,384]{2,1,0:T(1,128)S(1)} %all-to-all-done.arrived, f32[16,32,256]{2,1,0:T(8,128)S(1)} %get-tuple-element.18.spread), custom_call_target="tpu_custom_call" | custom-call | bytes 10000000 | tf_op jit(solution)/shard_map/build_state/pallas_call | solution.py:22
  22.8 0.0 collective-permute-done.near
  22.8 1.0 %collective-permute-done.1.far = f32[40,128]{1,0:T(8,128)S(1)} collective-permute-done((f32[40,128]{1,0:T(8,128)S(1)}, f32[40,128]{1,0:T(8,128)S(1)}, u32[]{:S(2)}, u32[]{:S(2)}) %collective-permute-start.1) | collective-permute-done | bytes 20512 | tf_op jit(solution)/shard_map/ppermute | solution.py:402
  23.8 0.3 build_rims.1
  24.1 5.5 %collective-permute-start.3 = (f32[224,256]{1,0:T(8,128)S(1)}, f32[224,256]{1,0:T(8,128)S(1)}, u32[]{:S(2)}, u32[]{:S(2)}) collective-permute-start(f32[224,256]{1,0:T(8,128)S(1)} %get-tuple-element.30), channel_id=1, source_target_pairs={{0,64},{64,128},{128,192},{192,256},{256,320},{320,384},{384,448},... | collective-permute-start | bytes 688136 | tf_op jit(solution)/shard_map/ppermute | solution.py:429
  29.6 1.9 %collective-permute-start.2 = (f32[224,256]{1,0:T(8,128)S(1)}, f32[224,256]{1,0:T(8,128)S(1)}, u32[]{:S(2)}, u32[]{:S(2)}) collective-permute-start(f32[224,256]{1,0:T(8,128)S(1)} %get-tuple-element.28), channel_id=1, source_target_pairs={{64,0},{128,64},{192,128},{256,192},{320,256},{384,320},{448,384},... | collective-permute-start | bytes 688136 | tf_op jit(solution)/shard_map/ppermute | solution.py:430
  31.5 1.6 %inner_sweeps.1 = (f32[6,2,32,384]{3,2,1,0:T(8,128)S(1)}, f32[6,2,32,384]{3,2,1,0:T(8,128)S(1)}, f32[4,32,384]{2,1,0:T(8,128)S(1)}) custom-call(f32[16,32,256]{2,1,0:T(8,128)S(1)} %get-tuple-element.19.state, f32[16,32,128]{2,1,0:T(8,128)S(1)} %get-tuple-element.24.tails, f32[16,384]{1,0:T(8,128)S(1)} %get-tuple-element.25.coef), custom_call_target="tpu_custom_call" | custom-call | bytes 6000000 | tf_op jit(solution)/shard_map/inner_sweeps/pallas_call | solution.py:22
  33.2 0.2 collective-permute-done.3.block
  33.4 1.9 %low_sweeps.1.rest_0_ = f32[32,32,128]{2,1,0:T(8,128)} custom-call(f32[6,2,32,384]{3,2,1,0:T(8,128)S(1)} %get-tuple-element.29.edge, f32[4,32,384]{2,1,0:T(8,128)S(1)} %get-tuple-element.27.middle, f32[16,384]{1,0:T(8,128)S(1)} %get-tuple-element.25.coef, f32[16,32,256]{2,1,0:T(8,128)S(1)} %get-tuple-element.18.spread, ...), custom_call_target="tpu_custom_call" | custom-call | bytes 5000000 | tf_op jit(solution)/shard_map/low_sweeps/pallas_call | solution.py:22
  35.3 3.5 %collective-permute-done.2.block = f32[224,256]{1,0:T(8,128)S(1)} collective-permute-done((f32[224,256]{1,0:T(8,128)S(1)}, f32[224,256]{1,0:T(8,128)S(1)}, u32[]{:S(2)}, u32[]{:S(2)}) %collective-permute-start.2) | collective-permute-done | bytes 229408 | tf_op jit(solution)/shard_map/ppermute | solution.py:430
  38.7 1.9 %high_sweeps.1 = f32[32,32,128]{2,1,0:T(8,128)} custom-call(f32[6,2,32,384]{3,2,1,0:T(8,128)S(1)} %get-tuple-element.26.edge, f32[4,32,384]{2,1,0:T(8,128)S(1)} %get-tuple-element.27.middle, f32[16,384]{1,0:T(8,128)S(1)} %get-tuple-element.25.coef, f32[16,32,256]{2,1,0:T(8,128)S(1)} %get-tuple-element.18.spread, ...), custom_call_target="tpu_custom_call", output_to_operand_aliasing={{}: (5, {})} | custom-call | bytes 5000000 | tf_op jit(solution)/shard_map/high_sweeps/pallas_call | solution.py:22
Async XLA Ops:
  0.0 13.0 %copy-start = (bf16[32,16,256]{2,1,0:T(8,128)(2,1)S(1)}, bf16[32,16,256]{2,1,0:T(8,128)(2,1)}, u32[]{:S(2)}) copy-start(bf16[32,16,256]{2,1,0:T(8,128)(2,1)} %std.1) | copy-start | bytes 786436
  1.7 11.4 %copy-start.1 = (s32[16,256]{1,0:T(8,128)S(1)}, s32[16,256]{1,0:T(8,128)}, u32[]{:S(2)}) copy-start(s32[16,256]{1,0:T(8,128)} %sea.1) | copy-start | bytes 49156
  1.7 11.4 %copy-start.2 = (f32[16,256]{1,0:T(8,128)S(1)}, f32[16,256]{1,0:T(8,128)}, u32[]{:S(2)}) copy-start(f32[16,256]{1,0:T(8,128)} %diffusivity.1) | copy-start | bytes 49156
  1.7 17.9 %all-to-all-start = ((f32[64,1,384]{2,1,0:T(1,128)}), f32[64,1,384]{2,1,0:T(1,128)S(1)}, u32[]{:S(2)}, u32[]{:S(2)}) async-start(f32[64,1,384]{2,1,0:T(1,128)} %pack_records.1), calls=%async_computation | async-start | bytes 196608 | tf_op jit(solution)/shard_map/all_to_all | solution.py:391
  13.4 9.4 %collective-permute-start = (f32[40,128]{1,0:T(8,128)S(1)}, f32[40,128]{1,0:T(8,128)S(1)}, u32[]{:S(2)}, u32[]{:S(2)}) collective-permute-start(f32[40,128]{1,0:T(8,128)S(1)} %get-tuple-element.22), channel_id=1, source_target_pairs={{0,1},{1,0},{2,3},{3,2},{4,5},{5,4},{6,7},{7,6},{8,9},{9,8},{10,11... | collective-permute-start | bytes 61448 | tf_op jit(solution)/shard_map/ppermute | solution.py:401
  15.4 8.4 %collective-permute-start.1 = (f32[40,128]{1,0:T(8,128)S(1)}, f32[40,128]{1,0:T(8,128)S(1)}, u32[]{:S(2)}, u32[]{:S(2)}) collective-permute-start(f32[40,128]{1,0:T(8,128)S(1)} %get-tuple-element.23), channel_id=1, source_target_pairs={{0,63},{1,2},{2,1},{3,4},{4,3},{5,6},{6,5},{7,8},{8,7},{9,10},{10,... | collective-permute-start | bytes 61448 | tf_op jit(solution)/shard_map/ppermute | solution.py:402
  24.1 9.3 %collective-permute-start.3 = (f32[224,256]{1,0:T(8,128)S(1)}, f32[224,256]{1,0:T(8,128)S(1)}, u32[]{:S(2)}, u32[]{:S(2)}) collective-permute-start(f32[224,256]{1,0:T(8,128)S(1)} %get-tuple-element.30), channel_id=1, source_target_pairs={{0,64},{64,128},{128,192},{192,256},{256,320},{320,384},{384,448},... | collective-permute-start | bytes 688136 | tf_op jit(solution)/shard_map/ppermute | solution.py:429
  29.6 9.1 %collective-permute-start.2 = (f32[224,256]{1,0:T(8,128)S(1)}, f32[224,256]{1,0:T(8,128)S(1)}, u32[]{:S(2)}, u32[]{:S(2)}) collective-permute-start(f32[224,256]{1,0:T(8,128)S(1)} %get-tuple-element.28), channel_id=1, source_target_pairs={{64,0},{128,64},{192,128},{256,192},{320,256},{384,320},{448,384},... | collective-permute-start | bytes 688136 | tf_op jit(solution)/shard_map/ppermute | solution.py:430

commit v5 on v4

--- a/solution.py
+++ b/solution.py
@@ -65,7 +65,7 @@
     return lax.rem(lax.axis_index("col"), 2) == 1
 
 
-def fixed_body(std, sea, diffusivity, spread, coef, near, far, stage):
+def fixed_body(std, sea, diffusivity, spread, coef, far, near, stage):
     channels, rows, cols = std.shape
     mask = sea[...].astype(jnp.float32)
     product = std[...].astype(jnp.float32) * mask[None]
@@ -150,9 +150,17 @@
             at = slice(row * channels, (row + 1) * channels)
             a_high[c][at, here] = hot * wide(high[row : row + 1])
             a_low[c][at, here] = hot * wide(low[row : row + 1])
-        away = index(1, 2, cols)
-        b_high[c][:, here] = pick(away, row_of(1, 4), row_of(1, 6)).astype(jnp.bfloat16)
-        b_low[c][:, here] = pick(away, row_of(1, 5), row_of(1, 7)).astype(jnp.bfloat16)
+        tile = lambda x: jnp.broadcast_to(x, (16, LANES)).astype(jnp.bfloat16)
+        column = whole[1, 2, n : n + 1, :].astype(jnp.float32)
+        at, after = tile(column), tile(column + 1.0)
+        factors = [tile(row_of(1, f)) for f in (4, 5, 6, 7)]
+        none = jnp.zeros((16, LANES), jnp.bfloat16)
+        for q in range(cols // 16):
+            some = slice(16 * q, 16 * (q + 1))
+            line = (lax.broadcasted_iota(jnp.int32, (16, LANES), 0) + 16 * q).astype(jnp.float32).astype(jnp.bfloat16)
+            first, second = line == at, line == after
+            b_high[c][some, here] = jnp.where(first, factors[0], jnp.where(second, factors[2], none))
+            b_low[c][some, here] = jnp.where(first, factors[1], jnp.where(second, factors[3], none))
 
         for side, (k, base) in enumerate(((0, cols - RIM), (2, 0))):
             hot = index(k, 0, channels) == 0
@@ -185,7 +193,7 @@
         state[i] = total[i * channels : (i + 1) * channels, :] * spread[i]
 
 
-def rim_body(state, sides, coef, near, far, tails, coef_out, to_up, to_down):
+def rim_body(state, sides, coef, far, near, tails, coef_out, to_up, to_down):
     rows, channels, cols = state.shape
     lane = lax.broadcasted_iota(jnp.int32, (channels, LANES), 1)
     lane_row = lax.broadcasted_iota(jnp.int32, (1, LANES), 1)
@@ -333,20 +341,24 @@
         load = loader(t)
         swept(load, turns(load, SWEEPS, width), faces, t + 1 if low else keep - 1 - t, storer(t))
 
-    for i in range(0 if low else rows // 2, rows // 2 if low else rows):
-        if SWEEPS <= i < keep:
-            done = middle[i - SWEEPS, :, 0:cols]
-        else:
-            done = work[SWEEPS % 2, i if low else i - keep, :, 0:cols]
-        done = done * spread[i]
-        for k in range(cols // LANES):
-            first = k * 8 + i % 8
-            result[pl.ds(first, channels, stride=rows // 2 * cols // LANES), :] = done[:, k * LANES : (k + 1) * LANES]
     size = rows // 2 * cols // LANES
     target = out.at[:, 0:size, :] if low else out.at[:, size : 2 * size, :]
-    copy = pltpu.make_async_copy(result.reshape(channels, size, LANES), target, sent)
-    copy.start()
-    copy.wait()
+    source = result.reshape(channels, size, LANES)
+    copies = []
+    for g in range(channels // 8):
+        for i in range(0 if low else rows // 2, rows // 2 if low else rows):
+            if SWEEPS <= i < keep:
+                done = middle[i - SWEEPS, part(g), 0:cols]
+            else:
+                done = work[SWEEPS % 2, i if low else i - keep, part(g), 0:cols]
+            done = done * spread[i, part(g), :]
+            for k in range(cols // LANES):
+                first = 8 * g * size + k * 8 + i % 8
+                result[pl.ds(first, 8, stride=size), :] = done[:, k * LANES : (k + 1) * LANES]
+        copies.append(pltpu.make_async_copy(source.at[part(g)], target.at[part(g)], sent.at[g]))
+        copies[-1].start()
+    for copy in copies:
+        copy.wait()
 
 
 def per_device(
@@ -390,7 +402,7 @@
     )
     arrived = lax.all_to_all(packed, "col", split_axis=0, concat_axis=0, tiled=True, axis_index_groups=[list(range(dests))[::-1]])
 
-    spread, coef, near, far = kernel_call(
+    spread, coef, far, near = kernel_call(
         fixed_body,
         "fixed_fields",
         (f32(rows, channels, cols), f32(rows, cols), f32(channels + 8, LANES), f32(channels + 8, LANES)),
@@ -398,8 +410,8 @@
         [vmem(cols // LANES, channels * rows, LANES)],
         moved=2_000_000,
     )
+    far = lax.ppermute(far, "col", [(i, (((i + 1) ^ 1) - 1) % count_cols) for i in range(count_cols)])
     near = lax.ppermute(near, "col", [(i, i ^ 1) for i in range(count_cols)])
-    far = lax.ppermute(far, "col", [(i, (((i + 1) ^ 1) - 1) % count_cols) for i in range(count_cols)])
 
     blocks = records // LANES
     chunks = min(CHUNKS, blocks)
@@ -421,7 +433,7 @@
         rim_body,
         "build_rims",
         (f32(rows, channels, LANES), f32(rows, width), f32(slab, cols), f32(slab, cols)),
-        (state, sides, coef, near, far),
+        (state, sides, coef, far, near),
         moved=2_000_000,
     )
     up = [(i, i + 1) for i in range(count_rows - 1)]
@@ -454,7 +466,7 @@
                 vmem(5, rows, width),
                 vmem(rows, width),
                 vmem(channels * size // 2, LANES),
-                pltpu.SemaphoreType.DMA,
+                pltpu.SemaphoreType.DMA((channels // 8,)),
             ],
             moved=5_000_000,
             held=() if low else (5,),

time: 41 us -> 40.6 us (level)
  starting transfers between devices: 22.7 us -> 23.5 us
  waiting for transfers between devices: 6.86 us -> 6.08 us
    ppermute x1, waiting for transfers between devices: 1 us -> 0.01 us  [per_device(): lax.ppermute(far, 'col', [(i, ((i + 1 ^ 1) - 1) % count_cols) for i in ra...]
    ppermute x1, waiting for transfers between devices: 0.21 us -> 1.19 us  [per_device(): from_down = lax.ppermute(to_up, 'row', up)]
    all_to_all x1, waiting for transfers between devices: 2.17 us -> 1.39 us  [per_device(): lax.all_to_all(packed, 'col', split_axis=0, concat_axis=0, tiled=True, ax...]
    ppermute x1, starting transfers between devices: 1.99 us -> 2.75 us  [per_device(): near = lax.ppermute(near, 'col', [(i, i ^ 1) for i in range(count_cols)])]
    pallas_call x7, Pallas kernels: 10.9 us -> 10.5 us  [kernel_call(): pl.pallas_call(body, name=name, out_shape=outs, in_specs=specs, out_specs...]
  transfers between devices with their start and end apart: 5 -> 5, of which waited for: 4 -> 3; matrix products, arithmetic and copies ran while one was open for 0% -> 0% of each run, Pallas kernels for 17% -> 17%
where the time goes in v5:
time: 40.6 us; the launch traced here: 40.2 us
  starting transfers between devices  23.5 us (58%)
  Pallas kernels  10.5 us (26%)
  waiting for transfers between devices  6.08 us (15%)
    all_to_all x1, starting transfers between devices, per_device(): lax.all_to_all(packed, 'col', split_axis=0, concat_axis=0, tiled=True, ax...  11.3 us
    pallas_call x7, Pallas kernels, kernel_call(): pl.pallas_call(body, name=name, out_shape=outs, in_specs=specs, out_specs...  10.5 us
    ppermute x1, starting transfers between devices, per_device(): from_down = lax.ppermute(to_up, 'row', up)  5.5 us
    ppermute x1, waiting for transfers between devices, per_device(): from_up = lax.ppermute(to_down, 'row', down)  3.5 us
    ppermute x1, starting transfers between devices, per_device(): near = lax.ppermute(near, 'col', [(i, i ^ 1) for i in range(count_cols)])  2.75 us
    ppermute x1, starting transfers between devices, per_device(): lax.ppermute(far, 'col', [(i, ((i + 1 ^ 1) - 1) % count_cols) for i in ra...  2.02 us
    ppermute x1, starting transfers between devices, per_device(): from_up = lax.ppermute(to_down, 'row', down)  1.92 us
    all_to_all x1, waiting for transfers between devices, per_device(): lax.all_to_all(packed, 'col', split_axis=0, concat_axis=0, tiled=True, ax...  1.39 us
  transfers between devices with their start and end apart: 5, of which 3 were waited for; matrix products, arithmetic and copies ran while one was open for 0% of the time, Pallas kernels for 17%

profile of v5, /device:TPU:192, one launch (start us, length us, event | category | flops | bytes accessed | tf_op | source)
XLA Modules:
  0.0 40.2 jit_solution(2961909057149325302)
XLA Ops:
  0.0 0.0 copy-start
  0.0 1.7 %pack_records.1 = f32[64,1,384]{2,1,0:T(1,128)} custom-call(f32[32,64]{1,0:T(8,128)} %bitcast.19, f32[32,64]{1,0:T(8,128)} %bitcast.20, f32[2,32,64]{2,1,0:T(8,128)} %bitcast.18, s32[32,64]{1,0:T(8,128)} %bitcast.21, s32[1,64]{1,0:T(1,128)} %bitcast.22), custom_call_target="tpu_custom_call" | custom-call | bytes 200000 | tf_op jit(solution)/shard_map/pack_records/pallas_call | solution.py:22
  1.7 0.0 copy-start.1
  1.7 0.0 copy-start.2
  1.7 11.3 %all-to-all-start = ((f32[64,1,384]{2,1,0:T(1,128)}), f32[64,1,384]{2,1,0:T(1,128)S(1)}, u32[]{:S(2)}, u32[]{:S(2)}) async-start(f32[64,1,384]{2,1,0:T(1,128)} %pack_records.1), calls=%async_computation | async-start | bytes 196608 | tf_op jit(solution)/shard_map/all_to_all | solution.py:403
  13.0 0.0 copy-done
  13.1 0.0 copy-done.1
  13.1 0.0 copy-done.2
  13.1 0.3 fixed_fields.1
  13.4 2.0 %collective-permute-start = (f32[40,128]{1,0:T(8,128)S(1)}, f32[40,128]{1,0:T(8,128)S(1)}, u32[]{:S(2)}, u32[]{:S(2)}) collective-permute-start(f32[40,128]{1,0:T(8,128)S(1)} %get-tuple-element.22), channel_id=1, source_target_pairs={{0,63},{1,2},{2,1},{3,4},{4,3},{5,6},{6,5},{7,8},{8,7},{9,10},{10,... | collective-permute-start | bytes 61448 | tf_op jit(solution)/shard_map/ppermute | solution.py:413
  15.4 2.8 %collective-permute-start.1 = (f32[40,128]{1,0:T(8,128)S(1)}, f32[40,128]{1,0:T(8,128)S(1)}, u32[]{:S(2)}, u32[]{:S(2)}) collective-permute-start(f32[40,128]{1,0:T(8,128)S(1)} %get-tuple-element.23), channel_id=1, source_target_pairs={{0,1},{1,0},{2,3},{3,2},{4,5},{5,4},{6,7},{7,6},{8,9},{9,8},{10,11... | collective-permute-start | bytes 61448 | tf_op jit(solution)/shard_map/ppermute | solution.py:414
  18.2 1.4 %all-to-all-done.arrived = f32[64,1,384]{2,1,0:T(1,128)S(1)} async-done(((f32[64,1,384]{2,1,0:T(1,128)}), f32[64,1,384]{2,1,0:T(1,128)S(1)}, u32[]{:S(2)}, u32[]{:S(2)}) %all-to-all-start) | async-done | bytes 98336 | tf_op jit(solution)/shard_map/all_to_all | solution.py:403
  19.6 2.9 %build_state.1 = (f32[16,32,256]{2,1,0:T(8,128)S(1)}, f32[2,32,128]{2,1,0:T(8,128)S(1)}) custom-call(f32[64,1,384]{2,1,0:T(1,128)S(1)} %all-to-all-done.arrived, f32[16,32,256]{2,1,0:T(8,128)S(1)} %get-tuple-element.18.spread), custom_call_target="tpu_custom_call" | custom-call | bytes 10000000 | tf_op jit(solution)/shard_map/build_state/pallas_call | solution.py:22
  22.5 0.0 collective-permute-done.far
  22.5 0.0 collective-permute-done.1.near
  22.5 0.3 build_rims.1
  22.8 5.5 %collective-permute-start.3 = (f32[224,256]{1,0:T(8,128)S(1)}, f32[224,256]{1,0:T(8,128)S(1)}, u32[]{:S(2)}, u32[]{:S(2)}) collective-permute-start(f32[224,256]{1,0:T(8,128)S(1)} %get-tuple-element.30), channel_id=1, source_target_pairs={{0,64},{64,128},{128,192},{192,256},{256,320},{320,384},{384,448},... | collective-permute-start | bytes 688136 | tf_op jit(solution)/shard_map/ppermute | solution.py:441
  28.3 1.9 %collective-permute-start.2 = (f32[224,256]{1,0:T(8,128)S(1)}, f32[224,256]{1,0:T(8,128)S(1)}, u32[]{:S(2)}, u32[]{:S(2)}) collective-permute-start(f32[224,256]{1,0:T(8,128)S(1)} %get-tuple-element.28), channel_id=1, source_target_pairs={{64,0},{128,64},{192,128},{256,192},{320,256},{384,320},{448,384},... | collective-permute-start | bytes 688136 | tf_op jit(solution)/shard_map/ppermute | solution.py:442
  30.2 1.6 %inner_sweeps.1 = (f32[6,2,32,384]{3,2,1,0:T(8,128)S(1)}, f32[6,2,32,384]{3,2,1,0:T(8,128)S(1)}, f32[4,32,384]{2,1,0:T(8,128)S(1)}) custom-call(f32[16,32,256]{2,1,0:T(8,128)S(1)} %get-tuple-element.19.state, f32[16,32,128]{2,1,0:T(8,128)S(1)} %get-tuple-element.24.tails, f32[16,384]{1,0:T(8,128)S(1)} %get-tuple-element.25.coef), custom_call_target="tpu_custom_call" | custom-call | bytes 6000000 | tf_op jit(solution)/shard_map/inner_sweeps/pallas_call | solution.py:22
  31.9 1.2 %collective-permute-done.3.block = f32[224,256]{1,0:T(8,128)S(1)} collective-permute-done((f32[224,256]{1,0:T(8,128)S(1)}, f32[224,256]{1,0:T(8,128)S(1)}, u32[]{:S(2)}, u32[]{:S(2)}) %collective-permute-start.3) | collective-permute-done | bytes 229408 | tf_op jit(solution)/shard_map/ppermute | solution.py:441
  33.1 1.8 %low_sweeps.1.rest_0_ = f32[32,32,128]{2,1,0:T(8,128)} custom-call(f32[6,2,32,384]{3,2,1,0:T(8,128)S(1)} %get-tuple-element.29.edge, f32[4,32,384]{2,1,0:T(8,128)S(1)} %get-tuple-element.27.middle, f32[16,384]{1,0:T(8,128)S(1)} %get-tuple-element.25.coef, f32[16,32,256]{2,1,0:T(8,128)S(1)} %get-tuple-element.18.spread, ...), custom_call_target="tpu_custom_call" | custom-call | bytes 5000000 | tf_op jit(solution)/shard_map/low_sweeps/pallas_call | solution.py:22
  34.9 3.5 %collective-permute-done.2.block = f32[224,256]{1,0:T(8,128)S(1)} collective-permute-done((f32[224,256]{1,0:T(8,128)S(1)}, f32[224,256]{1,0:T(8,128)S(1)}, u32[]{:S(2)}, u32[]{:S(2)}) %collective-permute-start.2) | collective-permute-done | bytes 229408 | tf_op jit(solution)/shard_map/ppermute | solution.py:442
  38.4 1.8 %high_sweeps.1 = f32[32,32,128]{2,1,0:T(8,128)} custom-call(f32[6,2,32,384]{3,2,1,0:T(8,128)S(1)} %get-tuple-element.26.edge, f32[4,32,384]{2,1,0:T(8,128)S(1)} %get-tuple-element.27.middle, f32[16,384]{1,0:T(8,128)S(1)} %get-tuple-element.25.coef, f32[16,32,256]{2,1,0:T(8,128)S(1)} %get-tuple-element.18.spread, ...), custom_call_target="tpu_custom_call", output_to_operand_aliasing={{}: (5, {})} | custom-call | bytes 5000000 | tf_op jit(solution)/shard_map/high_sweeps/pallas_call | solution.py:22
Async XLA Ops:
  0.0 13.0 %copy-start = (bf16[32,16,256]{2,1,0:T(8,128)(2,1)S(1)}, bf16[32,16,256]{2,1,0:T(8,128)(2,1)}, u32[]{:S(2)}) copy-start(bf16[32,16,256]{2,1,0:T(8,128)(2,1)} %std.1) | copy-start | bytes 786436
  1.7 11.4 %copy-start.1 = (s32[16,256]{1,0:T(8,128)S(1)}, s32[16,256]{1,0:T(8,128)}, u32[]{:S(2)}) copy-start(s32[16,256]{1,0:T(8,128)} %sea.1) | copy-start | bytes 49156
  1.7 11.4 %copy-start.2 = (f32[16,256]{1,0:T(8,128)S(1)}, f32[16,256]{1,0:T(8,128)}, u32[]{:S(2)}) copy-start(f32[16,256]{1,0:T(8,128)} %diffusivity.1) | copy-start | bytes 49156
  1.7 17.9 %all-to-all-start = ((f32[64,1,384]{2,1,0:T(1,128)}), f32[64,1,384]{2,1,0:T(1,128)S(1)}, u32[]{:S(2)}, u32[]{:S(2)}) async-start(f32[64,1,384]{2,1,0:T(1,128)} %pack_records.1), calls=%async_computation | async-start | bytes 196608 | tf_op jit(solution)/shard_map/all_to_all | solution.py:403
  13.4 9.1 %collective-permute-start = (f32[40,128]{1,0:T(8,128)S(1)}, f32[40,128]{1,0:T(8,128)S(1)}, u32[]{:S(2)}, u32[]{:S(2)}) collective-permute-start(f32[40,128]{1,0:T(8,128)S(1)} %get-tuple-element.22), channel_id=1, source_target_pairs={{0,63},{1,2},{2,1},{3,4},{4,3},{5,6},{6,5},{7,8},{8,7},{9,10},{10,... | collective-permute-start | bytes 61448 | tf_op jit(solution)/shard_map/ppermute | solution.py:413
  15.4 7.1 %collective-permute-start.1 = (f32[40,128]{1,0:T(8,128)S(1)}, f32[40,128]{1,0:T(8,128)S(1)}, u32[]{:S(2)}, u32[]{:S(2)}) collective-permute-start(f32[40,128]{1,0:T(8,128)S(1)} %get-tuple-element.23), channel_id=1, source_target_pairs={{0,1},{1,0},{2,3},{3,2},{4,5},{5,4},{6,7},{7,6},{8,9},{9,8},{10,11... | collective-permute-start | bytes 61448 | tf_op jit(solution)/shard_map/ppermute | solution.py:414
  22.8 10.3 %collective-permute-start.3 = (f32[224,256]{1,0:T(8,128)S(1)}, f32[224,256]{1,0:T(8,128)S(1)}, u32[]{:S(2)}, u32[]{:S(2)}) collective-permute-start(f32[224,256]{1,0:T(8,128)S(1)} %get-tuple-element.30), channel_id=1, source_target_pairs={{0,64},{64,128},{128,192},{192,256},{256,320},{320,384},{384,448},... | collective-permute-start | bytes 688136 | tf_op jit(solution)/shard_map/ppermute | solution.py:441
  28.3 10.1 %collective-permute-start.2 = (f32[224,256]{1,0:T(8,128)S(1)}, f32[224,256]{1,0:T(8,128)S(1)}, u32[]{:S(2)}, u32[]{:S(2)}) collective-permute-start(f32[224,256]{1,0:T(8,128)S(1)} %get-tuple-element.28), channel_id=1, source_target_pairs={{64,0},{128,64},{192,128},{256,192},{320,256},{384,320},{448,384},... | collective-permute-start | bytes 688136 | tf_op jit(solution)/shard_map/ppermute | solution.py:442

commit v6 on v5

--- a/solution.py
+++ b/solution.py
@@ -229,8 +229,12 @@
         base = base + half
         out[base : base + 8, :] = jnp.zeros((8, cols), jnp.float32)
         out[base : base + SWEEPS, :] = coef_out[start : start + SWEEPS, 0:cols]
-        out[base + 8 : base + 16, :] = jnp.zeros((8, cols), jnp.float32)
-        out[base + 8 : base + 8 + SWEEPS, 0:LANES] = coef_out[start : start + SWEEPS, cols : cols + LANES]
+        packed = jnp.zeros((1, LANES), jnp.float32)
+        for q in range(SWEEPS):
+            inside = (lane_row >= 2 * RIM * q) & (lane_row < 2 * RIM * (q + 1))
+            tail = coef_out[start + q : start + q + 1, cols : cols + LANES]
+            packed = jnp.where(inside, pltpu.roll(tail, (2 * RIM * q + RIM) % LANES, 1), packed)
+        out[base + SWEEPS : base + SWEEPS + 1, 0:LANES] = packed
 
 
 def set_faces(faces, field):
@@ -315,7 +319,10 @@
     base = base + half
     start = 0 if low else keep
     stage[start : start + SWEEPS, 0:cols] = block[base : base + SWEEPS, :]
-    stage[start : start + SWEEPS, cols:width] = block[base + 8 : base + 8 + SWEEPS, 0:LANES]
+    packed = block[base + SWEEPS : base + SWEEPS + 1, 0:LANES]
+    for q in range(SWEEPS):
+        tail = pltpu.roll(packed, (LANES - 2 * RIM * q - RIM) % LANES, 1)
+        stage[start + q : start + q + 1, cols:width] = jnp.where((lane[0:1] < RIM) | (lane[0:1] >= LANES - RIM), tail, 0.0)
     if low:
         stage[SWEEPS:rows, :] = coef[0:keep, :]
     else:
@@ -428,7 +435,7 @@
         + [bf16(2, rows * RIM, piece)] * (2 * chunks),
         moved=10_000_000,
     )
-    slab = SWEEPS * channels + channels // 2 + 16
+    slab = SWEEPS * channels + channels // 2 + 8
     tails, coef_wide, to_up, to_down = kernel_call(
         rim_body,
         "build_rims",

time: 40.6 us -> 40.5 us (level)
  no operation moved by 1% of the time
where the time goes in v6:
time: 40.5 us; the launch traced here: 40.1 us
  starting transfers between devices  23.5 us (58%)
  Pallas kernels  10.6 us (26%)
  waiting for transfers between devices  5.84 us (14%)
    all_to_all x1, starting transfers between devices, per_device(): lax.all_to_all(packed, 'col', split_axis=0, concat_axis=0, tiled=True, ax...  11.3 us
    pallas_call x7, Pallas kernels, kernel_call(): pl.pallas_call(body, name=name, out_shape=outs, in_specs=specs, out_specs...  10.6 us
    ppermute x1, starting transfers between devices, per_device(): from_down = lax.ppermute(to_up, 'row', up)  5.5 us
    ppermute x1, waiting for transfers between devices, per_device(): from_up = lax.ppermute(to_down, 'row', down)  3.43 us
    ppermute x1, starting transfers between devices, per_device(): near = lax.ppermute(near, 'col', [(i, i ^ 1) for i in range(count_cols)])  2.75 us
    ppermute x1, starting transfers between devices, per_device(): lax.ppermute(far, 'col', [(i, ((i + 1 ^ 1) - 1) % count_cols) for i in ra...  2.02 us
    ppermute x1, starting transfers between devices, per_device(): from_up = lax.ppermute(to_down, 'row', down)  1.92 us
    all_to_all x1, waiting for transfers between devices, per_device(): lax.all_to_all(packed, 'col', split_axis=0, concat_axis=0, tiled=True, ax...  1.39 us
  transfers between devices with their start and end apart: 5, of which 3 were waited for; matrix products, arithmetic and copies ran while one was open for 0% of the time, Pallas kernels for 17%

profile of v6, /device:TPU:192, one launch (start us, length us, event | category | flops | bytes accessed | tf_op | source)
XLA Modules:
  0.0 40.1 jit_solution(13748766570165593681)
XLA Ops:
  0.0 0.0 copy-start
  0.0 1.7 %pack_records.1 = f32[64,1,384]{2,1,0:T(1,128)} custom-call(f32[32,64]{1,0:T(8,128)} %bitcast.19, f32[32,64]{1,0:T(8,128)} %bitcast.20, f32[2,32,64]{2,1,0:T(8,128)} %bitcast.18, s32[32,64]{1,0:T(8,128)} %bitcast.21, s32[1,64]{1,0:T(1,128)} %bitcast.22), custom_call_target="tpu_custom_call" | custom-call | bytes 200000 | tf_op jit(solution)/shard_map/pack_records/pallas_call | solution.py:22
  1.7 0.0 copy-start.1
  1.7 0.0 copy-start.2
  1.7 11.3 %all-to-all-start = ((f32[64,1,384]{2,1,0:T(1,128)}), f32[64,1,384]{2,1,0:T(1,128)S(1)}, u32[]{:S(2)}, u32[]{:S(2)}) async-start(f32[64,1,384]{2,1,0:T(1,128)} %pack_records.1), calls=%async_computation | async-start | bytes 196608 | tf_op jit(solution)/shard_map/all_to_all | solution.py:410
  13.0 0.0 copy-done
  13.1 0.0 copy-done.1
  13.1 0.0 copy-done.2
  13.1 0.3 fixed_fields.1
  13.4 2.0 %collective-permute-start = (f32[40,128]{1,0:T(8,128)S(1)}, f32[40,128]{1,0:T(8,128)S(1)}, u32[]{:S(2)}, u32[]{:S(2)}) collective-permute-start(f32[40,128]{1,0:T(8,128)S(1)} %get-tuple-element.22), channel_id=1, source_target_pairs={{0,63},{1,2},{2,1},{3,4},{4,3},{5,6},{6,5},{7,8},{8,7},{9,10},{10,... | collective-permute-start | bytes 61448 | tf_op jit(solution)/shard_map/ppermute | solution.py:420
  15.4 2.8 %collective-permute-start.1 = (f32[40,128]{1,0:T(8,128)S(1)}, f32[40,128]{1,0:T(8,128)S(1)}, u32[]{:S(2)}, u32[]{:S(2)}) collective-permute-start(f32[40,128]{1,0:T(8,128)S(1)} %get-tuple-element.23), channel_id=1, source_target_pairs={{0,1},{1,0},{2,3},{3,2},{4,5},{5,4},{6,7},{7,6},{8,9},{9,8},{10,11... | collective-permute-start | bytes 61448 | tf_op jit(solution)/shard_map/ppermute | solution.py:421
  18.2 1.4 %all-to-all-done.arrived = f32[64,1,384]{2,1,0:T(1,128)S(1)} async-done(((f32[64,1,384]{2,1,0:T(1,128)}), f32[64,1,384]{2,1,0:T(1,128)S(1)}, u32[]{:S(2)}, u32[]{:S(2)}) %all-to-all-start) | async-done | bytes 98336 | tf_op jit(solution)/shard_map/all_to_all | solution.py:410
  19.6 2.9 %build_state.1 = (f32[16,32,256]{2,1,0:T(8,128)S(1)}, f32[2,32,128]{2,1,0:T(8,128)S(1)}) custom-call(f32[64,1,384]{2,1,0:T(1,128)S(1)} %all-to-all-done.arrived, f32[16,32,256]{2,1,0:T(8,128)S(1)} %get-tuple-element.18.spread), custom_call_target="tpu_custom_call" | custom-call | bytes 10000000 | tf_op jit(solution)/shard_map/build_state/pallas_call | solution.py:22
  22.5 0.0 collective-permute-done.far
  22.5 0.0 collective-permute-done.1.near
  22.5 0.3 build_rims.1
  22.8 5.5 %collective-permute-start.3 = (f32[216,256]{1,0:T(8,128)S(1)}, f32[216,256]{1,0:T(8,128)S(1)}, u32[]{:S(2)}, u32[]{:S(2)}) collective-permute-start(f32[216,256]{1,0:T(8,128)S(1)} %get-tuple-element.30), channel_id=1, source_target_pairs={{0,64},{64,128},{128,192},{192,256},{256,320},{320,384},{384,448},... | collective-permute-start | bytes 663560 | tf_op jit(solution)/shard_map/ppermute | solution.py:448
  28.3 1.9 %collective-permute-start.2 = (f32[216,256]{1,0:T(8,128)S(1)}, f32[216,256]{1,0:T(8,128)S(1)}, u32[]{:S(2)}, u32[]{:S(2)}) collective-permute-start(f32[216,256]{1,0:T(8,128)S(1)} %get-tuple-element.28), channel_id=1, source_target_pairs={{64,0},{128,64},{192,128},{256,192},{320,256},{384,320},{448,384},... | collective-permute-start | bytes 663560 | tf_op jit(solution)/shard_map/ppermute | solution.py:449
  30.3 1.6 %inner_sweeps.1 = (f32[6,2,32,384]{3,2,1,0:T(8,128)S(1)}, f32[6,2,32,384]{3,2,1,0:T(8,128)S(1)}, f32[4,32,384]{2,1,0:T(8,128)S(1)}) custom-call(f32[16,32,256]{2,1,0:T(8,128)S(1)} %get-tuple-element.19.state, f32[16,32,128]{2,1,0:T(8,128)S(1)} %get-tuple-element.24.tails, f32[16,384]{1,0:T(8,128)S(1)} %get-tuple-element.25.coef), custom_call_target="tpu_custom_call" | custom-call | bytes 6000000 | tf_op jit(solution)/shard_map/inner_sweeps/pallas_call | solution.py:22
  31.9 1.0 %collective-permute-done.3.block = f32[216,256]{1,0:T(8,128)S(1)} collective-permute-done((f32[216,256]{1,0:T(8,128)S(1)}, f32[216,256]{1,0:T(8,128)S(1)}, u32[]{:S(2)}, u32[]{:S(2)}) %collective-permute-start.3) | collective-permute-done | bytes 221216 | tf_op jit(solution)/shard_map/ppermute | solution.py:448
  32.9 1.9 %low_sweeps.1.rest_0_ = f32[32,32,128]{2,1,0:T(8,128)} custom-call(f32[6,2,32,384]{3,2,1,0:T(8,128)S(1)} %get-tuple-element.29.edge, f32[4,32,384]{2,1,0:T(8,128)S(1)} %get-tuple-element.27.middle, f32[16,384]{1,0:T(8,128)S(1)} %get-tuple-element.25.coef, f32[16,32,256]{2,1,0:T(8,128)S(1)} %get-tuple-element.18.spread, ...), custom_call_target="tpu_custom_call" | custom-call | bytes 5000000 | tf_op jit(solution)/shard_map/low_sweeps/pallas_call | solution.py:22
  34.8 3.4 %collective-permute-done.2.block = f32[216,256]{1,0:T(8,128)S(1)} collective-permute-done((f32[216,256]{1,0:T(8,128)S(1)}, f32[216,256]{1,0:T(8,128)S(1)}, u32[]{:S(2)}, u32[]{:S(2)}) %collective-permute-start.2) | collective-permute-done | bytes 221216 | tf_op jit(solution)/shard_map/ppermute | solution.py:449
  38.2 1.9 %high_sweeps.1 = f32[32,32,128]{2,1,0:T(8,128)} custom-call(f32[6,2,32,384]{3,2,1,0:T(8,128)S(1)} %get-tuple-element.26.edge, f32[4,32,384]{2,1,0:T(8,128)S(1)} %get-tuple-element.27.middle, f32[16,384]{1,0:T(8,128)S(1)} %get-tuple-element.25.coef, f32[16,32,256]{2,1,0:T(8,128)S(1)} %get-tuple-element.18.spread, ...), custom_call_target="tpu_custom_call", output_to_operand_aliasing={{}: (5, {})} | custom-call | bytes 5000000 | tf_op jit(solution)/shard_map/high_sweeps/pallas_call | solution.py:22
Async XLA Ops:
  0.0 13.0 %copy-start = (bf16[32,16,256]{2,1,0:T(8,128)(2,1)S(1)}, bf16[32,16,256]{2,1,0:T(8,128)(2,1)}, u32[]{:S(2)}) copy-start(bf16[32,16,256]{2,1,0:T(8,128)(2,1)} %std.1) | copy-start | bytes 786436
  1.7 11.4 %copy-start.1 = (s32[16,256]{1,0:T(8,128)S(1)}, s32[16,256]{1,0:T(8,128)}, u32[]{:S(2)}) copy-start(s32[16,256]{1,0:T(8,128)} %sea.1) | copy-start | bytes 49156
  1.7 11.4 %copy-start.2 = (f32[16,256]{1,0:T(8,128)S(1)}, f32[16,256]{1,0:T(8,128)}, u32[]{:S(2)}) copy-start(f32[16,256]{1,0:T(8,128)} %diffusivity.1) | copy-start | bytes 49156
  1.7 17.9 %all-to-all-start = ((f32[64,1,384]{2,1,0:T(1,128)}), f32[64,1,384]{2,1,0:T(1,128)S(1)}, u32[]{:S(2)}, u32[]{:S(2)}) async-start(f32[64,1,384]{2,1,0:T(1,128)} %pack_records.1), calls=%async_computation | async-start | bytes 196608 | tf_op jit(solution)/shard_map/all_to_all | solution.py:410
  13.4 9.1 %collective-permute-start = (f32[40,128]{1,0:T(8,128)S(1)}, f32[40,128]{1,0:T(8,128)S(1)}, u32[]{:S(2)}, u32[]{:S(2)}) collective-permute-start(f32[40,128]{1,0:T(8,128)S(1)} %get-tuple-element.22), channel_id=1, source_target_pairs={{0,63},{1,2},{2,1},{3,4},{4,3},{5,6},{6,5},{7,8},{8,7},{9,10},{10,... | collective-permute-start | bytes 61448 | tf_op jit(solution)/shard_map/ppermute | solution.py:420
  15.4 7.1 %collective-permute-start.1 = (f32[40,128]{1,0:T(8,128)S(1)}, f32[40,128]{1,0:T(8,128)S(1)}, u32[]{:S(2)}, u32[]{:S(2)}) collective-permute-start(f32[40,128]{1,0:T(8,128)S(1)} %get-tuple-element.23), channel_id=1, source_target_pairs={{0,1},{1,0},{2,3},{3,2},{4,5},{5,4},{6,7},{7,6},{8,9},{9,8},{10,11... | collective-permute-start | bytes 61448 | tf_op jit(solution)/shard_map/ppermute | solution.py:421
  22.8 10.1 %collective-permute-start.3 = (f32[216,256]{1,0:T(8,128)S(1)}, f32[216,256]{1,0:T(8,128)S(1)}, u32[]{:S(2)}, u32[]{:S(2)}) collective-permute-start(f32[216,256]{1,0:T(8,128)S(1)} %get-tuple-element.30), channel_id=1, source_target_pairs={{0,64},{64,128},{128,192},{192,256},{256,320},{320,384},{384,448},... | collective-permute-start | bytes 663560 | tf_op jit(solution)/shard_map/ppermute | solution.py:448
  28.3 9.9 %collective-permute-start.2 = (f32[216,256]{1,0:T(8,128)S(1)}, f32[216,256]{1,0:T(8,128)S(1)}, u32[]{:S(2)}, u32[]{:S(2)}) collective-permute-start(f32[216,256]{1,0:T(8,128)S(1)} %get-tuple-element.28), channel_id=1, source_target_pairs={{64,0},{128,64},{192,128},{256,192},{320,256},{384,320},{448,384},... | collective-permute-start | bytes 663560 | tf_op jit(solution)/shard_map/ppermute | solution.py:449

commit v7 on v6

--- a/solution.py
+++ b/solution.py
@@ -36,7 +36,7 @@
     return jax.ShapeDtypeStruct(shape, jnp.float32)
 
 
-def pack_body(innovation_in, precision_in, offsets_in, cells_in, counts_in, out, innovation, precision, offsets, cells, counts, tile, rows, arrived):
+def pack_body(innovation_in, precision_in, offsets_in, cells_in, counts_in, out, innovation, precision, offsets, cells, counts, tile, rows, arrived, staged, sent):
     pairs = (
         (counts_in, counts),
         (innovation_in, innovation),
@@ -56,9 +56,17 @@
     tile[2 * slots : 3 * slots, 0:dests] = offsets[1]
     tile[3 * slots : 4 * slots, 0:dests] = cells[...].astype(jnp.float32)
     rows[...] = tile[...].T
-    for d in range(dests):
-        for k in range(3):
-            out[dests - 1 - d, :, k * LANES : (k + 1) * LANES] = rows[pl.ds((d + k - 1) % dests, 1), :]
+    half = dests // 2
+    leaving = []
+    for part in range(2):
+        here = slice(part * half, (part + 1) * half)
+        for q in range(part * half, (part + 1) * half):
+            for k in range(3):
+                staged[q, :, k * LANES : (k + 1) * LANES] = rows[pl.ds((dests - 2 - q + k) % dests, 1), :]
+        leaving.append(pltpu.make_async_copy(staged.at[here], out.at[here], sent.at[part]))
+        leaving[-1].start()
+    for copy in leaving:
+        copy.wait()
 
 
 def odd_column():
@@ -402,10 +410,13 @@
             vmem(LANES, LANES),
             vmem(LANES, LANES),
             pltpu.SemaphoreType.DMA((5,)),
+            vmem(dests, 1, 3 * LANES),
+            pltpu.SemaphoreType.DMA((2,)),
         ],
         moved=200_000,
         place=pltpu.HBM,
         grant=ALL_VMEM_BYTES,
+        out_place=pltpu.HBM,
     )
     arrived = lax.all_to_all(packed, "col", split_axis=0, concat_axis=0, tiled=True, axis_index_groups=[list(range(dests))[::-1]])
 

time: 40.5 us -> 40.5 us (level)
  no operation moved by 1% of the time
where the time goes in v7:
time: 40.5 us; the launch traced here: 40.1 us
  starting transfers between devices  23.5 us (58%)
  Pallas kernels  10.6 us (26%)
  waiting for transfers between devices  5.84 us (14%)
    all_to_all x1, starting transfers between devices, per_device(): lax.all_to_all(packed, 'col', split_axis=0, concat_axis=0, tiled=True, ax...  11.3 us
    pallas_call x7, Pallas kernels, kernel_call(): pl.pallas_call(body, name=name, out_shape=outs, in_specs=specs, out_specs...  10.6 us
    ppermute x1, starting transfers between devices, per_device(): from_down = lax.ppermute(to_up, 'row', up)  5.5 us
    ppermute x1, waiting for transfers between devices, per_device(): from_up = lax.ppermute(to_down, 'row', down)  3.43 us
    ppermute x1, starting transfers between devices, per_device(): near = lax.ppermute(near, 'col', [(i, i ^ 1) for i in range(count_cols)])  2.75 us
    ppermute x1, starting transfers between devices, per_device(): lax.ppermute(far, 'col', [(i, ((i + 1 ^ 1) - 1) % count_cols) for i in ra...  2.02 us
    ppermute x1, starting transfers between devices, per_device(): from_up = lax.ppermute(to_down, 'row', down)  1.92 us
    all_to_all x1, waiting for transfers between devices, per_device(): lax.all_to_all(packed, 'col', split_axis=0, concat_axis=0, tiled=True, ax...  1.39 us
  transfers between devices with their start and end apart: 5, of which 3 were waited for; matrix products, arithmetic and copies ran while one was open for 0% of the time, Pallas kernels for 17%

profile of v7, /device:TPU:192, one launch (start us, length us, event | category | flops | bytes accessed | tf_op | source)
XLA Modules:
  0.0 40.1 jit_solution(16860873084527843820)
XLA Ops:
  0.0 0.0 copy-start
  0.0 1.7 %pack_records.1 = f32[64,1,384]{2,1,0:T(1,128)} custom-call(f32[32,64]{1,0:T(8,128)} %bitcast.19, f32[32,64]{1,0:T(8,128)} %bitcast.20, f32[2,32,64]{2,1,0:T(8,128)} %bitcast.18, s32[32,64]{1,0:T(8,128)} %bitcast.21, s32[1,64]{1,0:T(1,128)} %bitcast.22), custom_call_target="tpu_custom_call" | custom-call | bytes 200000 | tf_op jit(solution)/shard_map/pack_records/pallas_call | solution.py:22
  1.7 0.0 copy-start.1
  1.7 0.0 copy-start.2
  1.7 11.3 %all-to-all-start = ((f32[64,1,384]{2,1,0:T(1,128)}), f32[64,1,384]{2,1,0:T(1,128)S(1)}, u32[]{:S(2)}, u32[]{:S(2)}) async-start(f32[64,1,384]{2,1,0:T(1,128)} %pack_records.1), calls=%async_computation | async-start | bytes 196608 | tf_op jit(solution)/shard_map/all_to_all | solution.py:421
  13.0 0.0 copy-done
  13.1 0.0 copy-done.1
  13.1 0.0 copy-done.2
  13.1 0.3 fixed_fields.1
  13.4 2.0 %collective-permute-start = (f32[40,128]{1,0:T(8,128)S(1)}, f32[40,128]{1,0:T(8,128)S(1)}, u32[]{:S(2)}, u32[]{:S(2)}) collective-permute-start(f32[40,128]{1,0:T(8,128)S(1)} %get-tuple-element.22), channel_id=1, source_target_pairs={{0,63},{1,2},{2,1},{3,4},{4,3},{5,6},{6,5},{7,8},{8,7},{9,10},{10,... | collective-permute-start | bytes 61448 | tf_op jit(solution)/shard_map/ppermute | solution.py:431
  15.4 2.8 %collective-permute-start.1 = (f32[40,128]{1,0:T(8,128)S(1)}, f32[40,128]{1,0:T(8,128)S(1)}, u32[]{:S(2)}, u32[]{:S(2)}) collective-permute-start(f32[40,128]{1,0:T(8,128)S(1)} %get-tuple-element.23), channel_id=1, source_target_pairs={{0,1},{1,0},{2,3},{3,2},{4,5},{5,4},{6,7},{7,6},{8,9},{9,8},{10,11... | collective-permute-start | bytes 61448 | tf_op jit(solution)/shard_map/ppermute | solution.py:432
  18.2 1.4 %all-to-all-done.arrived = f32[64,1,384]{2,1,0:T(1,128)S(1)} async-done(((f32[64,1,384]{2,1,0:T(1,128)}), f32[64,1,384]{2,1,0:T(1,128)S(1)}, u32[]{:S(2)}, u32[]{:S(2)}) %all-to-all-start) | async-done | bytes 98336 | tf_op jit(solution)/shard_map/all_to_all | solution.py:421
  19.6 2.9 %build_state.1 = (f32[16,32,256]{2,1,0:T(8,128)S(1)}, f32[2,32,128]{2,1,0:T(8,128)S(1)}) custom-call(f32[64,1,384]{2,1,0:T(1,128)S(1)} %all-to-all-done.arrived, f32[16,32,256]{2,1,0:T(8,128)S(1)} %get-tuple-element.18.spread), custom_call_target="tpu_custom_call" | custom-call | bytes 10000000 | tf_op jit(solution)/shard_map/build_state/pallas_call | solution.py:22
  22.5 0.0 collective-permute-done.far
  22.5 0.0 collective-permute-done.1.near
  22.5 0.3 build_rims.1
  22.8 5.5 %collective-permute-start.3 = (f32[216,256]{1,0:T(8,128)S(1)}, f32[216,256]{1,0:T(8,128)S(1)}, u32[]{:S(2)}, u32[]{:S(2)}) collective-permute-start(f32[216,256]{1,0:T(8,128)S(1)} %get-tuple-element.30), channel_id=1, source_target_pairs={{0,64},{64,128},{128,192},{192,256},{256,320},{320,384},{384,448},... | collective-permute-start | bytes 663560 | tf_op jit(solution)/shard_map/ppermute | solution.py:459
  28.3 1.9 %collective-permute-start.2 = (f32[216,256]{1,0:T(8,128)S(1)}, f32[216,256]{1,0:T(8,128)S(1)}, u32[]{:S(2)}, u32[]{:S(2)}) collective-permute-start(f32[216,256]{1,0:T(8,128)S(1)} %get-tuple-element.28), channel_id=1, source_target_pairs={{64,0},{128,64},{192,128},{256,192},{320,256},{384,320},{448,384},... | collective-permute-start | bytes 663560 | tf_op jit(solution)/shard_map/ppermute | solution.py:460
  30.3 1.6 %inner_sweeps.1 = (f32[6,2,32,384]{3,2,1,0:T(8,128)S(1)}, f32[6,2,32,384]{3,2,1,0:T(8,128)S(1)}, f32[4,32,384]{2,1,0:T(8,128)S(1)}) custom-call(f32[16,32,256]{2,1,0:T(8,128)S(1)} %get-tuple-element.19.state, f32[16,32,128]{2,1,0:T(8,128)S(1)} %get-tuple-element.24.tails, f32[16,384]{1,0:T(8,128)S(1)} %get-tuple-element.25.coef), custom_call_target="tpu_custom_call" | custom-call | bytes 6000000 | tf_op jit(solution)/shard_map/inner_sweeps/pallas_call | solution.py:22
  31.9 1.0 %collective-permute-done.3.block = f32[216,256]{1,0:T(8,128)S(1)} collective-permute-done((f32[216,256]{1,0:T(8,128)S(1)}, f32[216,256]{1,0:T(8,128)S(1)}, u32[]{:S(2)}, u32[]{:S(2)}) %collective-permute-start.3) | collective-permute-done | bytes 221216 | tf_op jit(solution)/shard_map/ppermute | solution.py:459
  32.9 1.9 %low_sweeps.1.rest_0_ = f32[32,32,128]{2,1,0:T(8,128)} custom-call(f32[6,2,32,384]{3,2,1,0:T(8,128)S(1)} %get-tuple-element.29.edge, f32[4,32,384]{2,1,0:T(8,128)S(1)} %get-tuple-element.27.middle, f32[16,384]{1,0:T(8,128)S(1)} %get-tuple-element.25.coef, f32[16,32,256]{2,1,0:T(8,128)S(1)} %get-tuple-element.18.spread, ...), custom_call_target="tpu_custom_call" | custom-call | bytes 5000000 | tf_op jit(solution)/shard_map/low_sweeps/pallas_call | solution.py:22
  34.8 3.4 %collective-permute-done.2.block = f32[216,256]{1,0:T(8,128)S(1)} collective-permute-done((f32[216,256]{1,0:T(8,128)S(1)}, f32[216,256]{1,0:T(8,128)S(1)}, u32[]{:S(2)}, u32[]{:S(2)}) %collective-permute-start.2) | collective-permute-done | bytes 221216 | tf_op jit(solution)/shard_map/ppermute | solution.py:460
  38.2 1.9 %high_sweeps.1 = f32[32,32,128]{2,1,0:T(8,128)} custom-call(f32[6,2,32,384]{3,2,1,0:T(8,128)S(1)} %get-tuple-element.26.edge, f32[4,32,384]{2,1,0:T(8,128)S(1)} %get-tuple-element.27.middle, f32[16,384]{1,0:T(8,128)S(1)} %get-tuple-element.25.coef, f32[16,32,256]{2,1,0:T(8,128)S(1)} %get-tuple-element.18.spread, ...), custom_call_target="tpu_custom_call", output_to_operand_aliasing={{}: (5, {})} | custom-call | bytes 5000000 | tf_op jit(solution)/shard_map/high_sweeps/pallas_call | solution.py:22
Async XLA Ops:
  0.0 13.0 %copy-start = (bf16[32,16,256]{2,1,0:T(8,128)(2,1)S(1)}, bf16[32,16,256]{2,1,0:T(8,128)(2,1)}, u32[]{:S(2)}) copy-start(bf16[32,16,256]{2,1,0:T(8,128)(2,1)} %std.1) | copy-start | bytes 786436
  1.7 11.4 %copy-start.1 = (s32[16,256]{1,0:T(8,128)S(1)}, s32[16,256]{1,0:T(8,128)}, u32[]{:S(2)}) copy-start(s32[16,256]{1,0:T(8,128)} %sea.1) | copy-start | bytes 49156
  1.7 11.4 %copy-start.2 = (f32[16,256]{1,0:T(8,128)S(1)}, f32[16,256]{1,0:T(8,128)}, u32[]{:S(2)}) copy-start(f32[16,256]{1,0:T(8,128)} %diffusivity.1) | copy-start | bytes 49156
  1.7 17.9 %all-to-all-start = ((f32[64,1,384]{2,1,0:T(1,128)}), f32[64,1,384]{2,1,0:T(1,128)S(1)}, u32[]{:S(2)}, u32[]{:S(2)}) async-start(f32[64,1,384]{2,1,0:T(1,128)} %pack_records.1), calls=%async_computation | async-start | bytes 196608 | tf_op jit(solution)/shard_map/all_to_all | solution.py:421
  13.4 9.1 %collective-permute-start = (f32[40,128]{1,0:T(8,128)S(1)}, f32[40,128]{1,0:T(8,128)S(1)}, u32[]{:S(2)}, u32[]{:S(2)}) collective-permute-start(f32[40,128]{1,0:T(8,128)S(1)} %get-tuple-element.22), channel_id=1, source_target_pairs={{0,63},{1,2},{2,1},{3,4},{4,3},{5,6},{6,5},{7,8},{8,7},{9,10},{10,... | collective-permute-start | bytes 61448 | tf_op jit(solution)/shard_map/ppermute | solution.py:431
  15.4 7.1 %collective-permute-start.1 = (f32[40,128]{1,0:T(8,128)S(1)}, f32[40,128]{1,0:T(8,128)S(1)}, u32[]{:S(2)}, u32[]{:S(2)}) collective-permute-start(f32[40,128]{1,0:T(8,128)S(1)} %get-tuple-element.23), channel_id=1, source_target_pairs={{0,1},{1,0},{2,3},{3,2},{4,5},{5,4},{6,7},{7,6},{8,9},{9,8},{10,11... | collective-permute-start | bytes 61448 | tf_op jit(solution)/shard_map/ppermute | solution.py:432
  22.8 10.1 %collective-permute-start.3 = (f32[216,256]{1,0:T(8,128)S(1)}, f32[216,256]{1,0:T(8,128)S(1)}, u32[]{:S(2)}, u32[]{:S(2)}) collective-permute-start(f32[216,256]{1,0:T(8,128)S(1)} %get-tuple-element.30), channel_id=1, source_target_pairs={{0,64},{64,128},{128,192},{192,256},{256,320},{320,384},{384,448},... | collective-permute-start | bytes 663560 | tf_op jit(solution)/shard_map/ppermute | solution.py:459
  28.3 9.9 %collective-permute-start.2 = (f32[216,256]{1,0:T(8,128)S(1)}, f32[216,256]{1,0:T(8,128)S(1)}, u32[]{:S(2)}, u32[]{:S(2)}) collective-permute-start(f32[216,256]{1,0:T(8,128)S(1)} %get-tuple-element.28), channel_id=1, source_target_pairs={{64,0},{128,64},{192,128},{256,192},{320,256},{384,320},{448,384},... | collective-permute-start | bytes 663560 | tf_op jit(solution)/shard_map/ppermute | solution.py:460
